TPU v7x, 256 devices: a whole 4x4x8 slice. The times are simulated.
256 devices in a mesh: rep: 8 (over x, y_hi), fsdp: 32 (over z, y_lo, core).
Axes of the slice: x: 4, y: 4 (y_hi: 2, y_lo: 2; y = y_hi * 2 + y_lo), z: 8, core: 2. Of those that a mesh axis runs over, the one named last changes fastest.
Arguments:
- activations: bfloat16 [8, 24576, 6144], P('rep', 'fsdp'), may hold values from -6 to 6
- out_grads: bfloat16 [8, 24576, 512], P('rep', 'fsdp'), may hold values from -0.0390625 to 0.0390625
- momentum: float32 [8, 6144, 512], P('rep', 'fsdp'), may hold values from -6 to 6
- indices: int32 [8, 96, 8, 128], P('rep', 'fsdp'), may hold values from 0 to 4095, as said below
- counts: int32 [8], P('rep'), may hold values from 64 to 128, as said below
Outputs:
- new_momentum: float32 [8, 6144, 512], P('rep', 'fsdp')
- step_dir: float32 [6144, 512], P('fsdp')
Inputs may be any that keep to these rules, and one draw needn't show every extreme that they name: `indices`: in each replica's list for one tile the 128 entries are distinct; only the first counts[r] slots of replica r are in use, the others hold further distinct positions that are not chosen. `counts`: the same count holds for every tile of one replica; some replica uses all 128 slots.
All inputs are finite; a program needn't handle non-finite values.
Results may differ from a plain program's by a relative error of at most 0.0003.
Values may be sent and summed in bfloat16 or wider, within the bound.
No kernel may reach another device: no remote copies, remote signals or barrier semaphores. Data moves between devices by JAX's collectives and lax.ppermute only.
A program may use at most 192 MiB of HBM per device.

v0:
```python
import math

import jax
import jax.numpy as jnp
from jax import lax
from jax.sharding import PartitionSpec as P

CH = 64


def cosine_table(side):
    freq = lax.broadcasted_iota(jnp.int32, (side, side), 0).astype(jnp.float32)
    place = lax.broadcasted_iota(jnp.int32, (side, side), 1).astype(jnp.float32)
    table = jnp.cos(math.pi * (2.0 * place + 1.0) * freq / (2.0 * side)) * math.sqrt(2.0 / side)
    return jnp.where(freq < 0.5, table * math.sqrt(0.5), table)


def forward_tiles(field, table):
    height, breadth = field.shape
    side = table.shape[0]
    blocks = field.reshape(height // side, side, breadth // side, side)
    result = jnp.einsum("ka,iajb,lb->ijkl", table, blocks, table, precision=lax.Precision.HIGHEST)
    return result.reshape(height // side, breadth // side, side * side)


def inverse_tiles(values, table):
    tile_rows, tile_cols, flat_size = values.shape
    side = table.shape[0]
    grid = values.reshape(tile_rows, tile_cols, side, side)
    blocks = jnp.einsum("ka,ijkl,lb->iajb", table, grid, table, precision=lax.Precision.HIGHEST)
    return blocks.reshape(tile_rows * side, tile_cols * side)


def scatter_slots(values, places, flat_size):
    tile_rows, tile_cols, width_slots = values.shape
    tile_count = tile_rows * tile_cols
    tile_ids = jnp.broadcast_to(
        jnp.arange(tile_count, dtype=jnp.int32)[:, None], (tile_count, width_slots)
    )
    dense = jnp.zeros((tile_count, flat_size), jnp.float32)
    dense = dense.at[tile_ids, places.reshape(tile_count, width_slots)].add(
        values.reshape(tile_count, width_slots)
    )
    return dense.reshape(tile_rows, tile_cols, flat_size)


def token_contract(left, right):
    return lax.dot_general(
        left, right, (((0,), (0,)), ((), ())), preferred_element_type=jnp.float32
    )


def body(activations, out_grads, momentum, indices, counts):
    table = cosine_table(CH)
    inputs = activations[0]
    grads = out_grads[0]
    gradient = lax.psum_scatter(
        token_contract(inputs, grads), "fsdp", scatter_dimension=0, tiled=True
    )
    moment = 0.9 * momentum[0] + gradient
    coefficients = forward_tiles(moment, table)
    places = indices[0]
    picked = jnp.take_along_axis(coefficients, places, axis=2)
    live = lax.broadcasted_iota(jnp.int32, places.shape, 2) < counts[0]
    picked = jnp.where(live, picked, jnp.zeros_like(picked))
    flat_size = CH * CH
    sparse = scatter_slots(picked, places, flat_size)
    new_moment = moment - inverse_tiles(sparse, table)
    total = lax.psum(sparse, "rep")
    decoded = inverse_tiles(total, table)
    step_dir = decoded * lax.rsqrt(decoded * decoded + 0.04)
    return (new_moment[None], step_dir)


def solution(mesh):
    placed = (
        P("rep", "fsdp", None),
        P("rep", "fsdp", None),
        P("rep", "fsdp", None),
        P("rep", "fsdp", None, None),
        P("rep"),
    )
    return jax.shard_map(
        body,
        mesh=mesh,
        in_specs=placed,
        out_specs=(P("rep", "fsdp", None), P("fsdp", None)),
        check_vma=False,
    )
```

profile of v0, /device:TPU:1, one launch (start us, length us, event | category | flops | bytes accessed | tf_op | source)
XLA Modules:
  0.0 320.2 jit_solution(5387826179682432554)
XLA Ops:
  7.2 0.0 copy-start
  7.2 0.0 reduce-scatter.2.cloned.1.call-start
  7.2 1.1 copy-done
  8.3 11.9 %fusion = f32[6144,512]{1,0:T(8,128)} fusion(bf16[1,768,6144]{2,1,0:T(8,128)(2,1)} %param.5, bf16[1,768,512]{2,1,0:T(8,128)(2,1)S(1)} %copy-done), kind=kOutput, calls=%fused_computation.2 | convolution fusion | flops 4831838208 | bytes 22806528 | tf_op jit(solution)/shard_map/dot_general | solution.py:48
  20.2 0.0 reduce-scatter.2.cloned.1.call-update
  21.0 0.0 copy-done.3
  21.0 0.0 copy-done.4
  21.0 0.1 multiply_reduce_fusion
  21.1 0.0 copy-done.5
  21.1 0.1 and_reduce_fusion
  21.2 151.5 %reduce-scatter.2.cloned.1.call-done = f32[192,512]{1,0:T(8,128)} async-done(((f32[6144,512]{1,0:T(8,128)}), f32[192,512]{1,0:T(8,128)}) %reduce-scatter.2.cloned.1.call-update) | async-done | bytes 393232 | tf_op jit(solution)/shard_map/reduce_scatter | solution.py:57
  172.7 1.1 bitcast_add_fusion
  173.8 0.2 reshape.103
  173.9 1.1 fusion.3
  175.0 0.9 fusion.13
  176.0 0.3 reshape.104
  176.3 24.1 %gather_fusion = f32[3072]{0:T(1024)S(1)} fusion(f32[3,8,4096]{2,1,0:T(8,128)S(1)} %reshape.104, s32[3072]{0:T(1024)S(1)} %fusion.55), kind=kCustom, calls=%fused_computation | custom fusion | bytes 61440 | tf_op jit(solution)/shard_map/jit(take_along_axis)/gather | solution.py:63
  200.4 16.7 %scatter_custom_fusion = f32[98304]{0:T(1024)S(1)} fusion(s32[3072]{0:T(1024)S(1)} %select_bitcast_fusion, f32[3072]{0:T(1024)S(1)} %fusion.57, f32[]{:T(128)} %constant.15.clone.1), kind=kCustom, calls=%fused_computation.12 | custom fusion | flops 3072 | bytes 393220
  217.1 0.2 reshape_reshape.3
  217.3 1.0 fusion.11
  218.3 0.2 all-reduce.2.cloned.1.call-start
  218.5 0.5 all-reduce.2.cloned.1.call-update
  219.1 0.9 convolution_bitcast_fusion.1
  220.0 0.5 copy.8
  220.5 0.2 reshape.105
  220.7 0.8 subtract_bitcast_fusion
  221.5 87.2 %all-reduce.2.cloned.1.call-done = f32[3,8,64,64]{3,2,1,0:T(8,128)} async-done(((f32[3,8,64,64]{3,2,1,0:T(8,128)}), f32[3,8,64,64]{3,2,1,0:T(8,128)}) %all-reduce.2.cloned.1.call-update) | async-done | bytes 393232 | tf_op jit(solution)/shard_map/psum | solution.py:69
  308.7 2.1 fusion.8
  310.9 0.9 convolution_bitcast_fusion
  311.8 0.5 copy.9
  312.3 0.2 reshape.108
  312.5 0.8 rsqrt_multiply_fusion
  (15 shorter events, 0.1 us)
Async XLA Ops:
  7.2 1.1 copy-start
  7.2 165.5 %reduce-scatter.2.cloned.1.call-start = ((), (), s32[]{:S(2)}) async-start(), calls=%async_computation.1 | async-start | bytes 12976128 | tf_op jit(solution)/shard_map/reduce_scatter | solution.py:57
  20.2 0.8 copy-start.3
  20.2 0.8 copy-start.4
  20.2 0.9 copy-start.5
  20.2 152.5 %copy-start.2 = (f32[1,192,512]{2,1,0:T(8,128)S(1)}, f32[1,192,512]{2,1,0:T(8,128)}, u32[]{:S(2)}) copy-start(f32[1,192,512]{2,1,0:T(8,128)} %param.7) | copy-start | bytes 1179652
  217.3 1.3 copy-start.1
  218.3 90.4 %all-reduce.2.cloned.1.call-start = ((), (), s32[]{:S(2)}) async-start(), calls=%async_computation.2 | async-start | bytes 1572864 | tf_op jit(solution)/shard_map/psum | solution.py:69
Sparse Core Ops, SparseCore 0:
  20.4 152.2 reduce-scatter.1
  221.8 86.8 all-reduce.1
where the time goes:
time: 324 us; the launch traced here: 320 us
  waiting for transfers between devices  239 us (74%)
  local copies, waits for them, and re-layouts  27.2 us (8%)
  other arithmetic  19.5 us (6%)
  matrix products  18.9 us (6%)
  between operations  14.9 us (5%)
    reduce_scatter x1, waiting for transfers between devices, body(): lax.psum_scatter(token_contract(inputs, grads), 'fsdp', scatter_dimension...  152 us
    psum x1, waiting for transfers between devices, body(): total = lax.psum(sparse, 'rep')  87.2 us
    gather x1, local copies, waits for them, and re-layouts, body(): picked = jnp.take_along_axis(coefficients, places, axis=2)  24.1 us
    unnamed x4, other arithmetic  16.8 us
    dot_general x1, matrix products, token_contract(): lax.dot_general(left, right, (((0,), (0,)), ((), ())), preferred_element_...  11.9 us
  transfers between devices with their start and end apart: 2, of which 2 were waited for; matrix products, arithmetic and copies ran while one was open for 1% of the time, Pallas kernels for 0%

commit v1 on v0

v1 whole, which is shorter than its diff:
```python
import math

import jax
import jax.numpy as jnp
import numpy as np
from jax import lax
from jax.experimental import pallas as pl
from jax.experimental.pallas import tpu as pltpu
from jax.sharding import PartitionSpec as P

CH = 64
SLOTS = 128
BF = jnp.bfloat16
F32 = jnp.float32


def cosine_table(side):
    freq = np.arange(side, dtype=np.float64)[:, None]
    place = np.arange(side, dtype=np.float64)[None, :]
    table = np.cos(math.pi * (2.0 * place + 1.0) * freq / (2.0 * side)) * math.sqrt(2.0 / side)
    return np.where(freq < 0.5, table * math.sqrt(0.5), table)


def two_terms(matrix):
    high = matrix.astype(np.float32).astype(BF)
    low = (matrix - high.astype(np.float64)).astype(np.float32).astype(BF)
    return np.stack([high, low])


def split(x):
    high = x.astype(BF)
    return high, (x - high.astype(F32)).astype(BF)


def dot(a, b):
    return jnp.dot(a, b, preferred_element_type=F32)


def dot_nt(a, b):
    return lax.dot_general(a, b, (((1,), (1,)), ((), ())), preferred_element_type=F32)


def left_product(table, x):
    high, low = split(x)
    return dot(table[0], high) + (dot(table[0], low) + dot(table[1], high))


def right_product(x, table):
    width = table.shape[-1]
    pieces = []
    for start in range(0, x.shape[1], width):
        high, low = split(x[:, start:start + width])
        pieces.append(dot(high, table[0]) + (dot(low, table[0]) + dot(high, table[1])))
    return jnp.concatenate(pieces, axis=1)


def pick_kernel(grad, momentum, places, rows, rows_t, cols, cols_t, new_moment, payload, coef, sparse):
    moment = 0.9 * momentum[...] + grad[...]
    coef[...] = right_product(left_product(rows, moment), cols_t)
    tile_rows, tile_cols = grad.shape[0] // CH, grad.shape[1] // CH
    group = 4
    tiles = tile_rows * tile_cols
    for i in range(tile_rows):
        for h in range(tile_cols // group):
            first = i * tile_cols + h * group
            part = [places[first + n:first + n + 1, :] for n in range(group)]
            flat = jnp.concatenate(part, axis=1)
            row_code = flat >> 6
            col_code = jnp.concatenate([(p & 63) + CH * n for n, p in enumerate(part)], axis=1)
            width = group * SLOTS
            in_col = lax.broadcasted_iota(jnp.int32, (group * CH, width), 0) == col_code
            in_row = lax.broadcasted_iota(jnp.int32, (CH, width), 0) == row_code
            col_hot = jnp.where(in_col, 1.0, 0.0).astype(BF)
            row_hot = jnp.where(in_row, 1.0, 0.0).astype(BF)
            block = coef[i * CH:(i + 1) * CH, h * group * CH:(h + 1) * group * CH]
            high, low = split(block)
            spread = dot(high, col_hot) + dot(low, col_hot)
            value = jnp.sum(jnp.where(in_row, spread, 0.0), axis=0, keepdims=True)
            for n in range(group):
                one = value[:, n * SLOTS:(n + 1) * SLOTS]
                for r in range(payload.shape[0]):
                    payload[r, first + n:first + n + 1, :] = one
            sparse[i * CH:(i + 1) * CH, h * group * CH:(h + 1) * group * CH] = block * dot_nt(row_hot, col_hot)
    for r in range(payload.shape[0]):
        payload[r, tiles:, :] = places[...].astype(F32)
    new_moment[...] = moment - right_product(left_product(rows_t, sparse[...]), cols)


def decode_kernel(gathered, rows_t, cols, step_dir, total):
    reps = gathered.shape[0]
    tiles = gathered.shape[1] // 2
    tile_cols = total.shape[1] // CH
    for pair in range(tiles // 2):
        blocks = []
        for t in (2 * pair, 2 * pair + 1):
            highs, lows, hots = [], [], []
            for r in range(reps):
                value = gathered[r, t:t + 1, :]
                place = gathered[r, tiles + t:tiles + t + 1, :].astype(jnp.int32)
                in_row = lax.broadcasted_iota(jnp.int32, (CH, SLOTS), 0) == (place >> 6)
                in_col = lax.broadcasted_iota(jnp.int32, (CH, SLOTS), 0) == (place & 63)
                high, low = split(value)
                highs.append(jnp.where(in_row, high.astype(F32), 0.0).astype(BF))
                lows.append(jnp.where(in_row, low.astype(F32), 0.0).astype(BF))
                hots.append(jnp.where(in_col, 1.0, 0.0).astype(BF))
            both = jnp.concatenate([jnp.concatenate(highs, axis=1), jnp.concatenate(lows, axis=1)], axis=0)
            out = dot_nt(both, jnp.concatenate(hots, axis=1))
            blocks.append(out[:CH] + out[CH:])
        i, j = (2 * pair) // tile_cols, (2 * pair) % tile_cols
        total[i * CH:(i + 1) * CH, j * CH:(j + 2) * CH] = jnp.concatenate(blocks, axis=1)
    decoded = right_product(left_product(rows_t, total[...]), cols)
    step_dir[...] = decoded * lax.rsqrt(decoded * decoded + 0.04)


def body(activations, out_grads, momentum, indices, counts):
    reps = lax.axis_size("rep")
    table = cosine_table(CH)
    rows = np.kron(np.eye(3), table)
    cols = np.kron(np.eye(4), table)
    rows, rows_t, cols, cols_t = (jnp.asarray(two_terms(m)) for m in (rows, rows.T, cols, cols.T))
    height, breadth = momentum.shape[1:]
    tiles = (height // CH) * (breadth // CH)
    live = lax.broadcasted_iota(jnp.int32, indices.shape[1:], 2) < counts[0]
    places = jnp.where(live, indices[0], -1).reshape(tiles, SLOTS)
    gradient = lax.psum_scatter(
        lax.dot_general(activations[0], out_grads[0], (((0,), (0,)), ((), ())), preferred_element_type=F32),
        "fsdp", scatter_dimension=0, tiled=True,
    )
    new_moment, payload = pl.pallas_call(
        pick_kernel,
        out_shape=[
            jax.ShapeDtypeStruct((height, breadth), F32),
            jax.ShapeDtypeStruct((reps, 2 * tiles, SLOTS), F32),
        ],
        scratch_shapes=[pltpu.VMEM((height, breadth), F32), pltpu.VMEM((height, breadth), F32)],
        compiler_params=pltpu.CompilerParams(vmem_limit_bytes=32 << 20),
        name="pick",
    )(gradient, momentum[0], places, rows, rows_t, cols, cols_t)
    gathered = lax.all_to_all(payload, "rep", 0, 0)
    step_dir = pl.pallas_call(
        decode_kernel,
        out_shape=jax.ShapeDtypeStruct((height, breadth), F32),
        scratch_shapes=[pltpu.VMEM((height, breadth), F32)],
        compiler_params=pltpu.CompilerParams(vmem_limit_bytes=32 << 20),
        name="decode",
    )(gathered, rows_t, cols)
    return (new_moment[None], step_dir)


def solution(mesh):
    placed = (
        P("rep", "fsdp", None),
        P("rep", "fsdp", None),
        P("rep", "fsdp", None),
        P("rep", "fsdp", None, None),
        P("rep"),
    )
    return jax.shard_map(
        body,
        mesh=mesh,
        in_specs=placed,
        out_specs=(P("rep", "fsdp", None), P("fsdp", None)),
        check_vma=False,
    )
```

time: 324 us -> 202 us (0.62)
  waiting for transfers between devices: 239 us -> 154 us
  local copies, waits for them, and re-layouts: 27.2 us -> 2.1 us
  other arithmetic: 19.5 us -> 0.01 us
  blocking collectives: 0 us -> 12.3 us
  matrix products: 18.9 us -> 11.8 us
  Pallas kernels: 0 us -> 6.46 us
    psum x1 -> x0, waiting for transfers between devices: 87.2 us -> none  [body(): total = lax.psum(sparse, 'rep')]
    gather x1 -> x0, local copies, waits for them, and re-layouts: 24.1 us -> none  [body(): picked = jnp.take_along_axis(coefficients, places, axis=2)]
    unnamed x4 -> x0, other arithmetic: 16.8 us -> none
    all_to_all x0 -> x1, blocking collectives: none -> 12.3 us  [body(): gathered = lax.all_to_all(payload, 'rep', 0, 0)]
    dot_general x7 -> x1, matrix products: 18.9 us -> 11.8 us  [body(): lax.dot_general(activations[0], out_grads[0], (((0,), (0,)), ((), ())), p...]
    pallas_call x0 -> x2, Pallas kernels: none -> 6.46 us  [the longest x1 3.36 us: body(): pl.pallas_call(decode_kernel, out_shape=jax.ShapeDtypeStruct((height, bre...]
  transfers between devices with their start and end apart: 2 -> 1, of which waited for: 2 -> 1; matrix products, arithmetic and copies ran while one was open for 1% -> 0% of each run, Pallas kernels for 0% -> 0%
where the time goes in v1:
time: 202 us; the launch traced here: 201 us
  waiting for transfers between devices  154 us (76%)
  between operations  14.8 us (7%)
  blocking collectives  12.3 us (6%)
  matrix products  11.8 us (6%)
  Pallas kernels  6.46 us (3%)
  local copies, waits for them, and re-layouts  2.1 us (1%)
    reduce_scatter x1, waiting for transfers between devices, body(): lax.psum_scatter(lax.dot_general(activations[0], out_grads[0], (((0,), (0...  154 us
    all_to_all x1, blocking collectives, body(): gathered = lax.all_to_all(payload, 'rep', 0, 0)  12.3 us
    dot_general x1, matrix products, body(): lax.dot_general(activations[0], out_grads[0], (((0,), (0,)), ((), ())), p...  11.8 us
  transfers between devices with their start and end apart: 1, of which 1 were waited for; matrix products, arithmetic and copies ran while one was open for 0% of the time, Pallas kernels for 0%

profile of v1, /device:TPU:1, one launch (start us, length us, event | category | flops | bytes accessed | tf_op | source)
XLA Modules:
  0.0 201.3 jit_solution(6405078801697215921)
XLA Ops:
  7.2 0.0 copy-start
  7.2 0.0 reduce-scatter.2.cloned.1.call-start
  7.2 1.1 copy-done
  8.3 11.8 %fusion = f32[6144,512]{1,0:T(8,128)} fusion(bf16[1,768,6144]{2,1,0:T(8,128)(2,1)} %param.9, bf16[1,768,512]{2,1,0:T(8,128)(2,1)S(1)} %copy-done), kind=kOutput, calls=%fused_computation | convolution fusion | flops 4831838208 | bytes 22806528 | tf_op jit(solution)/shard_map/dot_general | solution.py:126
  20.1 0.0 copy-start.7
  20.1 0.0 copy-start.1
  20.1 0.0 copy-start.2
  20.1 0.0 copy-start.3
  20.1 0.0 copy-start.5
  20.2 0.0 copy-start.6
  20.2 0.0 reduce-scatter.2.cloned.1.call-update
  21.0 0.0 copy-done.7
  21.0 153.7 %reduce-scatter.2.cloned.1.call-done.grad = f32[192,512]{1,0:T(8,128)} async-done(((f32[6144,512]{1,0:T(8,128)}), f32[192,512]{1,0:T(8,128)}) %reduce-scatter.2.cloned.1.call-update) | async-done | bytes 393232 | tf_op jit(solution)/shard_map/reduce_scatter | solution.py:125
  174.7 0.0 copy-done.1
  174.7 0.0 copy-done.2
  174.7 0.0 copy-done.3
  174.7 0.0 copy-done.5
  174.7 0.0 copy-done.6
  174.7 0.0 copy-start.4
  174.7 1.0 copy-done.4
  175.7 3.1 %pick.1 = (f32[192,512]{1,0:T(8,128)}, f32[8,48,128]{2,1,0:T(8,128)S(1)}) custom-call(f32[192,512]{1,0:T(8,128)S(1)} %copy-done.4, f32[192,512]{1,0:T(8,128)S(1)} %bitcast.12, s32[24,128]{1,0:T(8,128)S(1)} %bitcast_select_fusion.places, bf16[2,192,192]{2,1,0:T(8,128)(2,1)S(1)} %copy-done.6, bf16[2,192,192]{2,1,0:T(8,128)(2,1)S(1)} %copy-done.2, ...), custom_call_target="tpu_custom_call" | custom-call | tf_op jit(solution)/shard_map/pick/pallas_call | solution.py:129
  178.8 12.3 %all_to_all.5.gathered = f32[8,48,128]{2,1,0:T(8,128)S(1)} all-to-all(f32[8,48,128]{2,1,0:T(8,128)S(1)} %get-tuple-element.5), channel_id=1, replica_groups=mesh['rep'=8,'fsdp'=32] {'rep'}, dimensions={0} | all-to-all | bytes 393216 | tf_op jit(solution)/shard_map/all_to_all | solution.py:139
  191.1 3.4 %decode.1 = f32[192,512]{1,0:T(8,128)} custom-call(f32[8,48,128]{2,1,0:T(8,128)S(1)} %all_to_all.5.gathered, bf16[2,192,192]{2,1,0:T(8,128)(2,1)S(1)} %copy-done.2, bf16[2,256,256]{2,1,0:T(8,128)(2,1)S(1)} %copy-done.1), custom_call_target="tpu_custom_call" | custom-call | tf_op jit(solution)/shard_map/decode/pallas_call | solution.py:140
  (2 shorter events, 0.0 us)
Async XLA Ops:
  7.2 1.1 copy-start
  7.2 167.5 %reduce-scatter.2.cloned.1.call-start = ((), (), s32[]{:S(2)}) async-start(), calls=%async_computation.2 | async-start | bytes 12976128 | tf_op jit(solution)/shard_map/reduce_scatter | solution.py:125
  20.1 0.8 copy-start.7
  20.1 154.5 %copy-start.1 = (bf16[2,256,256]{2,1,0:T(8,128)(2,1)S(1)}, bf16[2,256,256]{2,1,0:T(8,128)(2,1)}, u32[]{:S(2)}) copy-start(bf16[2,256,256]{2,1,0:T(8,128)(2,1)} %constant.12.clone.cols) | copy-start | bytes 786436
  20.1 154.5 %copy-start.2 = (bf16[2,192,192]{2,1,0:T(8,128)(2,1)S(1)}, bf16[2,192,192]{2,1,0:T(8,128)(2,1)}, u32[]{:S(2)}) copy-start(bf16[2,192,192]{2,1,0:T(8,128)(2,1)} %constant.11.clone.rows_t) | copy-start | bytes 442372
  20.1 154.5 %copy-start.3 = (f32[1,192,512]{2,1,0:T(8,128)S(1)}, f32[1,192,512]{2,1,0:T(8,128)}, u32[]{:S(2)}) copy-start(f32[1,192,512]{2,1,0:T(8,128)} %param.11) | copy-start | bytes 1179652
  20.1 154.5 %copy-start.5 = (bf16[2,256,256]{2,1,0:T(8,128)(2,1)S(1)}, bf16[2,256,256]{2,1,0:T(8,128)(2,1)}, u32[]{:S(2)}) copy-start(bf16[2,256,256]{2,1,0:T(8,128)(2,1)} %constant.13.clone.cols_t) | copy-start | bytes 786436
  20.2 154.5 %copy-start.6 = (bf16[2,192,192]{2,1,0:T(8,128)(2,1)S(1)}, bf16[2,192,192]{2,1,0:T(8,128)(2,1)}, u32[]{:S(2)}) copy-start(bf16[2,192,192]{2,1,0:T(8,128)(2,1)} %constant.10.clone.rows) | copy-start | bytes 442372
  174.7 1.0 copy-start.4
Sparse Core Ops, SparseCore 0:
  20.3 154.3 reduce-scatter.1

commit v2 on v1

--- a/solution.py
+++ b/solution.py
@@ -12,6 +12,10 @@
 SLOTS = 128
 BF = jnp.bfloat16
 F32 = jnp.float32
+I16 = jnp.int16
+HEAD = 16
+ORDER = (4, 3, -3, 2, -2, 1, -1, 0)
+VMEM = 40 << 20
 
 
 def cosine_table(side):
@@ -54,8 +58,114 @@
     return jnp.concatenate(pieces, axis=1)
 
 
-def pick_kernel(grad, momentum, places, rows, rows_t, cols, cols_t, new_moment, payload, coef, sparse):
-    moment = 0.9 * momentum[...] + grad[...]
+def encode(x, out):
+    top = jnp.max(jnp.abs(x), axis=0, keepdims=True)
+    code = jnp.ceil(128.0 * jnp.log2(jnp.maximum(top, 1e-30))) + 1.0
+    scale = 32767.0 * jnp.exp2(code * (-1.0 / 128.0))
+    height = x.shape[0]
+    out[:height, :] = jnp.round(x * scale).astype(jnp.int32).astype(I16)
+    out[height:, :] = jnp.broadcast_to(code, (HEAD, x.shape[1])).astype(jnp.int32).astype(I16)
+
+
+def decode(ref):
+    height = ref.shape[0] - HEAD
+    code = ref[height:, :].astype(jnp.int32).astype(F32)[:1, :]
+    scale = jnp.exp2(code * (1.0 / 128.0)) * (1.0 / 32767.0)
+    return ref[:height, :].astype(jnp.int32).astype(F32) * scale
+
+
+def product_kernel(spot, inputs, grads, away, kept, both):
+    both[...] = lax.dot_general(inputs[...], grads[...], (((0,), (0,)), ((), ())), preferred_element_type=F32)
+    height = kept.shape[0]
+    core = spot[spot.shape[0] - 1]
+    kept[...] = both[pl.ds(pl.multiple_of(core * height, height), height), :]
+    encode(both[pl.ds(pl.multiple_of((1 - core) * height, height), height), :], away)
+
+
+def products(inputs, grads, blocks, core, height):
+    tokens, breadth = grads.shape
+    steps = blocks.shape[0]
+    return pl.pallas_call(
+        product_kernel,
+        grid_spec=pltpu.PrefetchScalarGridSpec(
+            num_scalar_prefetch=1,
+            grid=(steps,),
+            in_specs=[
+                pl.BlockSpec((tokens, 2 * height), lambda i, spot: (0, spot[i])),
+                pl.BlockSpec((tokens, breadth), lambda i, spot: (0, 0)),
+            ],
+            out_specs=[
+                pl.BlockSpec((None, height + HEAD, breadth), lambda i, spot: (i, 0, 0)),
+                pl.BlockSpec((None, height, breadth), lambda i, spot: (i, 0, 0)),
+            ],
+            scratch_shapes=[pltpu.VMEM((2 * height, breadth), F32)],
+        ),
+        out_shape=[
+            jax.ShapeDtypeStruct((steps, height + HEAD, breadth), I16),
+            jax.ShapeDtypeStruct((steps, height, breadth), F32),
+        ],
+        compiler_params=pltpu.CompilerParams(vmem_limit_bytes=VMEM),
+        cost_estimate=pl.CostEstimate(
+            flops=steps * 4 * height * tokens * breadth,
+            bytes_accessed=steps * (4 * height * tokens + 6 * height * breadth),
+            transcendentals=0,
+        ),
+        name="products",
+    )(jnp.concatenate([blocks, core[None]]), inputs, grads)
+
+
+def hop_kernel(columns, *refs):
+    kept, other = refs[:2]
+    out = refs[-1]
+    total = kept[...] + decode(other)
+    for ref in refs[2:-1]:
+        part = decode(ref)
+        if part.shape[1] < total.shape[1]:
+            pad = jnp.zeros((part.shape[0], total.shape[1] - part.shape[1]), F32)
+            part = jnp.concatenate([pad, part] if columns else [part, pad], axis=1)
+        total = total + part
+    if out.shape[1] < total.shape[1]:
+        width = out.shape[1]
+        total = total[:, columns * width:(columns + 1) * width]
+    encode(total, out)
+
+
+def hop(kept, other, slot, arrived, columns, width):
+    steps, height, breadth = kept.shape
+    return pl.pallas_call(
+        lambda *refs: hop_kernel(columns, *refs),
+        grid=(1,),
+        in_specs=[
+            pl.BlockSpec((None, height, breadth), lambda i: (slot, 0, 0)),
+            pl.BlockSpec((None, height + HEAD, breadth), lambda i: (slot, 0, 0)),
+        ] + [pl.BlockSpec(a.shape, lambda i: (0, 0)) for a in arrived],
+        out_specs=pl.BlockSpec((height + HEAD, width), lambda i: (0, 0)),
+        out_shape=jax.ShapeDtypeStruct((height + HEAD, width), I16),
+        compiler_params=pltpu.CompilerParams(vmem_limit_bytes=VMEM),
+        cost_estimate=pl.CostEstimate(flops=10 * height * breadth, bytes_accessed=10 * height * breadth, transcendentals=0),
+        name="hop",
+    )(kept, other, *arrived)
+
+
+def ring_sum(kept, other, ahead, behind):
+    def at(slot):
+        for (start, array), (_, remote) in zip(reversed(kept), reversed(other)):
+            if slot >= start:
+                return array, remote, slot - start
+
+    breadth = kept[0][1].shape[2]
+    half = breadth // 2
+    forth = lax.ppermute(hop(*at(0), [], 0, half), "fsdp", ahead)
+    back = lax.ppermute(hop(*at(0), [], 1, half), "fsdp", behind)
+    for step in range(3):
+        forth = lax.ppermute(hop(*at(1 + 2 * step), [forth], 0, breadth), "fsdp", ahead)
+        back = lax.ppermute(hop(*at(2 + 2 * step), [back], 1, breadth), "fsdp", behind)
+    return (*at(7), [forth, back])
+
+
+def pick_kernel(kept, other, forth, back, across, momentum, places, rows, rows_t, cols, cols_t, new_moment, payload, coef, sparse):
+    grad = kept[...] + decode(other) + decode(forth) + decode(back) + decode(across)
+    moment = 0.9 * momentum[...] + grad
     coef[...] = right_product(left_product(rows, moment), cols_t)
     tile_rows, tile_cols = grad.shape[0] // CH, grad.shape[1] // CH
     group = 4
@@ -122,20 +232,62 @@
     tiles = (height // CH) * (breadth // CH)
     live = lax.broadcasted_iota(jnp.int32, indices.shape[1:], 2) < counts[0]
     places = jnp.where(live, indices[0], -1).reshape(tiles, SLOTS)
-    gradient = lax.psum_scatter(
-        lax.dot_general(activations[0], out_grads[0], (((0,), (0,)), ((), ())), preferred_element_type=F32),
-        "fsdp", scatter_dimension=0, tiled=True,
-    )
+    chips = lax.axis_size("fsdp") // 4
+    me = lax.axis_index("fsdp")
+    z, y, core = me // 4, (me // 2) % 2, me % 2
+
+    def route(move):
+        pairs = []
+        for place in range(4 * chips):
+            to_z, to_y, to_core = move(place // 4, (place // 2) % 2, place % 2)
+            pairs.append((place, ((to_z % chips) * 2 + to_y) * 2 + to_core))
+        return pairs
+
+    ahead = route(lambda z, y, c: (z + 1, y, c))
+    behind = route(lambda z, y, c: (z - 1, y, c))
+    beside = route(lambda z, y, c: (z, 1 - y, c))
+    within = route(lambda z, y, c: (z, y, 1 - c))
+    order = np.array(ORDER, np.int32)
+    inputs, grads = activations[0], out_grads[0]
+
+    def stream(target, cuts):
+        blocks = ((z + order) % chips) * 2 + target
+        kept, other = [], []
+        for start, stop in zip(cuts[:-1], cuts[1:]):
+            away, own = products(inputs, grads, blocks[start:stop], core, height)
+            kept.append((start, own))
+            other.append((start, lax.ppermute(away, "fsdp", within)))
+        return kept, other
+
+    first = stream(1 - y, (0, 3, 8))
+    second = stream(y, (0, 3, 8))
+    part, remote, slot, ends = ring_sum(*first, ahead, behind)
+    across = lax.ppermute(hop(part, remote, slot, ends, 0, breadth), "fsdp", beside)
+    part, remote, slot, ends = ring_sum(*second, ahead, behind)
+
+    def whole(array):
+        return pl.BlockSpec(array.shape, lambda i, n=array.ndim: (0,) * n)
+
+    rest = (*ends, across, momentum[0], places, rows, rows_t, cols, cols_t)
     new_moment, payload = pl.pallas_call(
         pick_kernel,
+        grid=(1,),
+        in_specs=[
+            pl.BlockSpec((None, height, breadth), lambda i: (slot, 0, 0)),
+            pl.BlockSpec((None, height + HEAD, breadth), lambda i: (slot, 0, 0)),
+        ] + [whole(a) for a in rest],
+        out_specs=[
+            pl.BlockSpec((height, breadth), lambda i: (0, 0)),
+            pl.BlockSpec((reps, 2 * tiles, SLOTS), lambda i: (0, 0, 0)),
+        ],
         out_shape=[
             jax.ShapeDtypeStruct((height, breadth), F32),
             jax.ShapeDtypeStruct((reps, 2 * tiles, SLOTS), F32),
         ],
         scratch_shapes=[pltpu.VMEM((height, breadth), F32), pltpu.VMEM((height, breadth), F32)],
-        compiler_params=pltpu.CompilerParams(vmem_limit_bytes=32 << 20),
+        compiler_params=pltpu.CompilerParams(vmem_limit_bytes=VMEM),
         name="pick",
-    )(gradient, momentum[0], places, rows, rows_t, cols, cols_t)
+    )(part, remote, *rest)
     gathered = lax.all_to_all(payload, "rep", 0, 0)
     step_dir = pl.pallas_call(
         decode_kernel,

time: 202 us -> 103 us (0.51)
  the two profiles are of different devices: /device:TPU:1 before, /device:TPU:8 now
where the time goes in v2:
time: 103 us; the launch traced here: 102 us
  Pallas kernels  33.1 us (32%)
  starting transfers between devices  24.2 us (23%)
  waiting for transfers between devices  21.3 us (21%)
  blocking collectives  14 us (14%)
  local copies, waits for them, and re-layouts  7.07 us (7%)
  between operations  1.61 us (2%)
    pallas_call x4, Pallas kernels, products(): pl.pallas_call(product_kernel, grid_spec=pltpu.PrefetchScalarGridSpec(num...  15.5 us
    all_to_all x1, blocking collectives, body(): gathered = lax.all_to_all(payload, 'rep', 0, 0)  14 us
    pallas_call x17, Pallas kernels, hop(): pl.pallas_call(lambda *refs: hop_kernel(columns, *refs), grid=(1,), in_sp...  11 us
    ppermute x2, starting transfers between devices, ring_sum(): back = lax.ppermute(hop(*at(0), [], 1, half), 'fsdp', behind)  9.22 us
    ppermute x2, waiting for transfers between devices, ring_sum(): forth = lax.ppermute(hop(*at(0), [], 0, half), 'fsdp', ahead)  8.81 us
    ppermute x6, starting transfers between devices, ring_sum(): lax.ppermute(hop(*at(2 + 2 * step), [back], 1, breadth), 'fsdp', behind)  7.96 us
    unnamed x30, local copies, waits for them, and re-layouts  6.93 us
    ppermute x6, starting transfers between devices, ring_sum(): lax.ppermute(hop(*at(1 + 2 * step), [forth], 0, breadth), 'fsdp', ahead)  5.19 us
  transfers between devices with their start and end apart: 21, of which 8 were waited for; matrix products, arithmetic and copies ran while one was open for 0% of the time, Pallas kernels for 23%

profile of v2, /device:TPU:8, one launch (start us, length us, event | category | flops | bytes accessed | tf_op | source)
XLA Modules:
  0.0 102.1 jit_solution(17215874402208281858)
XLA Ops:
  1.4 3.7 %copy-done = bf16[1,768,6144]{2,1,0:T(8,128)(2,1)S(1)} copy-done((bf16[1,768,6144]{2,1,0:T(8,128)(2,1)S(1)}, bf16[1,768,6144]{2,1,0:T(8,128)(2,1)}, u32[]{:S(2)}) %copy-start) | copy-done | bytes 9437208
  5.1 1.1 %copy-done.5 = bf16[1,768,512]{2,1,0:T(8,128)(2,1)S(1)} copy-done((bf16[1,768,512]{2,1,0:T(8,128)(2,1)S(1)}, bf16[1,768,512]{2,1,0:T(8,128)(2,1)}, u32[]{:S(2)}) %copy-start.5) | copy-done | bytes 786456
  6.2 3.3 %products.7 = (s16[3,208,512]{2,1,0:T(8,128)(2,1)}, f32[3,192,512]{2,1,0:T(8,128)S(1)}) custom-call(s32[4]{0:T(128)S(1)} %get-tuple-element.27.spot, bf16[768,6144]{1,0:T(8,128)(2,1)S(1)} %bitcast.11, bf16[768,512]{1,0:T(8,128)(2,1)S(1)} %bitcast.17), custom_call_target="tpu_custom_call" | custom-call | flops 905969664 | bytes 3538944 | tf_op jit(solution)/shard_map/products/pallas_call | solution.py:88
  9.6 1.0 %copy-done.1 = f32[3,192,512]{2,1,0:T(8,128)} copy-done((f32[3,192,512]{2,1,0:T(8,128)}, f32[3,192,512]{2,1,0:T(8,128)S(1)}, u32[]{:S(2)}) %copy-start.1) | copy-done | bytes 1179672
  10.8 4.8 %products.6 = (s16[5,208,512]{2,1,0:T(8,128)(2,1)}, f32[5,192,512]{2,1,0:T(8,128)S(1)}) custom-call(s32[6]{0:T(128)S(1)} %get-tuple-element.25.spot, bf16[768,6144]{1,0:T(8,128)(2,1)S(1)} %bitcast.12, bf16[768,512]{1,0:T(8,128)(2,1)S(1)} %bitcast.18), custom_call_target="tpu_custom_call" | custom-call | flops 1509949440 | bytes 5898240 | tf_op jit(solution)/shard_map/products/pallas_call | solution.py:88
  16.1 3.3 %products.5 = (s16[3,208,512]{2,1,0:T(8,128)(2,1)}, f32[3,192,512]{2,1,0:T(8,128)S(1)}) custom-call(s32[4]{0:T(128)S(1)} %get-tuple-element.26.spot, bf16[768,6144]{1,0:T(8,128)(2,1)S(1)} %bitcast.13, bf16[768,512]{1,0:T(8,128)(2,1)S(1)} %bitcast.19), custom_call_target="tpu_custom_call" | custom-call | flops 905969664 | bytes 3538944 | tf_op jit(solution)/shard_map/products/pallas_call | solution.py:88
  19.5 1.0 %copy-done.3 = f32[3,192,512]{2,1,0:T(8,128)} copy-done((f32[3,192,512]{2,1,0:T(8,128)}, f32[3,192,512]{2,1,0:T(8,128)S(1)}, u32[]{:S(2)}) %copy-start.3) | copy-done | bytes 1179672
  20.5 4.0 %products.4 = (s16[5,208,512]{2,1,0:T(8,128)(2,1)S(1)}, f32[5,192,512]{2,1,0:T(8,128)S(1)}) custom-call(s32[6]{0:T(128)S(1)} %get-tuple-element.24.spot, bf16[768,6144]{1,0:T(8,128)(2,1)S(1)} %bitcast.16, bf16[768,512]{1,0:T(8,128)(2,1)S(1)} %bitcast.20), custom_call_target="tpu_custom_call" | custom-call | flops 1509949440 | bytes 5898240 | tf_op jit(solution)/shard_map/products/pallas_call | solution.py:88
  26.2 5.9 %collective-permute-start.16 = (s16[208,256]{1,0:T(8,128)(2,1)S(1)}, s16[208,256]{1,0:T(8,128)(2,1)S(1)}, u32[]{:S(2)}, u32[]{:S(2)}) collective-permute-start(s16[208,256]{1,0:T(8,128)(2,1)S(1)} %hop.29), channel_id=1, source_target_pairs={{0,28},{1,29},{2,30},{3,31},{4,0},{5,1},{6,2},{7,3},{8,4},{9,5},{1... | collective-permute-start | bytes 319496 | tf_op jit(solution)/shard_map/ppermute | solution.py:159
  33.3 3.3 %collective-permute-start.6 = (s16[208,256]{1,0:T(8,128)(2,1)S(1)}, s16[208,256]{1,0:T(8,128)(2,1)S(1)}, u32[]{:S(2)}, u32[]{:S(2)}) collective-permute-start(s16[208,256]{1,0:T(8,128)(2,1)S(1)} %hop.21), channel_id=1, source_target_pairs={{0,28},{1,29},{2,30},{3,31},{4,0},{5,1},{6,2},{7,3},{8,4},{9,5},{1... | collective-permute-start | bytes 319496 | tf_op jit(solution)/shard_map/ppermute | solution.py:159
  36.6 1.1 %hop.30 = s16[208,512]{1,0:T(8,128)(2,1)S(1)} custom-call(f32[3,192,512]{2,1,0:T(8,128)S(1)} %copy-done.2, s16[3,208,512]{2,1,0:T(8,128)(2,1)} %collective-permute-done.11.refs_1_, s16[208,256]{1,0:T(8,128)(2,1)S(1)} %collective-permute-done.16.refs_2_), custom_call_target="tpu_custom_call" | custom-call | flops 983040 | bytes 983040 | tf_op jit(solution)/shard_map/hop/pallas_call | solution.py:135
  37.7 1.7 %collective-permute-start.17 = (s16[208,512]{1,0:T(8,128)(2,1)S(1)}, s16[208,512]{1,0:T(8,128)(2,1)S(1)}, u32[]{:S(2)}, u32[]{:S(2)}) collective-permute-start(s16[208,512]{1,0:T(8,128)(2,1)S(1)} %hop.30), channel_id=1, source_target_pairs={{0,28},{1,29},{2,30},{3,31},{4,0},{5,1},{6,2},{7,3},{8,4},{9,5},{1... | collective-permute-start | bytes 638984 | tf_op jit(solution)/shard_map/ppermute | solution.py:162
  39.4 1.1 %hop.26 = s16[208,512]{1,0:T(8,128)(2,1)S(1)} custom-call(f32[3,192,512]{2,1,0:T(8,128)S(1)} %copy-done.2, s16[3,208,512]{2,1,0:T(8,128)(2,1)} %collective-permute-done.11.refs_1_, s16[208,256]{1,0:T(8,128)(2,1)S(1)} %collective-permute-done.12.refs_2_), custom_call_target="tpu_custom_call" | custom-call | flops 983040 | bytes 983040 | tf_op jit(solution)/shard_map/hop/pallas_call | solution.py:135
  41.3 8.8 %collective-permute-done.2.refs_2_ = s16[208,256]{1,0:T(8,128)(2,1)S(1)} collective-permute-done((s16[208,256]{1,0:T(8,128)(2,1)S(1)}, s16[208,256]{1,0:T(8,128)(2,1)S(1)}, u32[]{:S(2)}, u32[]{:S(2)}) %collective-permute-start.2) | collective-permute-done | bytes 106528 | tf_op jit(solution)/shard_map/ppermute | solution.py:158
  50.3 2.1 %collective-permute-start.3 = (s16[208,512]{1,0:T(8,128)(2,1)S(1)}, s16[208,512]{1,0:T(8,128)(2,1)S(1)}, u32[]{:S(2)}, u32[]{:S(2)}) collective-permute-start(s16[208,512]{1,0:T(8,128)(2,1)S(1)} %hop.18), channel_id=1, source_target_pairs={{0,4},{1,5},{2,6},{3,7},{4,8},{5,9},{6,10},{7,11},{8,12},{9,13},{1... | collective-permute-start | bytes 638984 | tf_op jit(solution)/shard_map/ppermute | solution.py:161
  52.4 1.1 %hop.31 = s16[208,512]{1,0:T(8,128)(2,1)S(1)} custom-call(f32[5,192,512]{2,1,0:T(8,128)S(1)} %get-tuple-element.16.refs_0_, s16[5,208,512]{2,1,0:T(8,128)(2,1)} %collective-permute-done.10.refs_1_, s16[208,512]{1,0:T(8,128)(2,1)S(1)} %collective-permute-done.17.refs_2_), custom_call_target="tpu_custom_call" | custom-call | flops 983040 | bytes 983040 | tf_op jit(solution)/shard_map/hop/pallas_call | solution.py:135
  53.5 1.5 %collective-permute-start.18 = (s16[208,512]{1,0:T(8,128)(2,1)S(1)}, s16[208,512]{1,0:T(8,128)(2,1)S(1)}, u32[]{:S(2)}, u32[]{:S(2)}) collective-permute-start(s16[208,512]{1,0:T(8,128)(2,1)S(1)} %hop.31), channel_id=1, source_target_pairs={{0,28},{1,29},{2,30},{3,31},{4,0},{5,1},{6,2},{7,3},{8,4},{9,5},{1... | collective-permute-start | bytes 638984 | tf_op jit(solution)/shard_map/ppermute | solution.py:162
  55.0 1.1 %hop.27 = s16[208,512]{1,0:T(8,128)(2,1)S(1)} custom-call(f32[5,192,512]{2,1,0:T(8,128)S(1)} %get-tuple-element.16.refs_0_, s16[5,208,512]{2,1,0:T(8,128)(2,1)} %collective-permute-done.10.refs_1_, s16[208,512]{1,0:T(8,128)(2,1)S(1)} %collective-permute-done.13.refs_2_), custom_call_target="tpu_custom_call" | custom-call | flops 983040 | bytes 983040 | tf_op jit(solution)/shard_map/hop/pallas_call | solution.py:135
  57.0 1.1 %collective-permute-done.7.refs_2_ = s16[208,512]{1,0:T(8,128)(2,1)S(1)} collective-permute-done((s16[208,512]{1,0:T(8,128)(2,1)S(1)}, s16[208,512]{1,0:T(8,128)(2,1)S(1)}, u32[]{:S(2)}, u32[]{:S(2)}) %collective-permute-start.7) | collective-permute-done | bytes 213024 | tf_op jit(solution)/shard_map/ppermute | solution.py:162
  58.3 1.4 %collective-permute-start.8 = (s16[208,512]{1,0:T(8,128)(2,1)S(1)}, s16[208,512]{1,0:T(8,128)(2,1)S(1)}, u32[]{:S(2)}, u32[]{:S(2)}) collective-permute-start(s16[208,512]{1,0:T(8,128)(2,1)S(1)} %hop.23), channel_id=1, source_target_pairs={{0,28},{1,29},{2,30},{3,31},{4,0},{5,1},{6,2},{7,3},{8,4},{9,5},{1... | collective-permute-start | bytes 638984 | tf_op jit(solution)/shard_map/ppermute | solution.py:162
  60.7 2.0 %collective-permute-done.18.refs_2_ = s16[208,512]{1,0:T(8,128)(2,1)S(1)} collective-permute-done((s16[208,512]{1,0:T(8,128)(2,1)S(1)}, s16[208,512]{1,0:T(8,128)(2,1)S(1)}, u32[]{:S(2)}, u32[]{:S(2)}) %collective-permute-start.18) | collective-permute-done | bytes 213024 | tf_op jit(solution)/shard_map/ppermute | solution.py:162
  62.7 1.1 %hop.32 = s16[208,512]{1,0:T(8,128)(2,1)S(1)} custom-call(f32[5,192,512]{2,1,0:T(8,128)S(1)} %get-tuple-element.16.refs_0_, s16[5,208,512]{2,1,0:T(8,128)(2,1)} %collective-permute-done.10.refs_1_, s16[208,512]{1,0:T(8,128)(2,1)S(1)} %collective-permute-done.18.refs_2_), custom_call_target="tpu_custom_call" | custom-call | flops 983040 | bytes 983040 | tf_op jit(solution)/shard_map/hop/pallas_call | solution.py:135
  65.2 1.1 %hop.28 = s16[208,512]{1,0:T(8,128)(2,1)S(1)} custom-call(f32[5,192,512]{2,1,0:T(8,128)S(1)} %get-tuple-element.16.refs_0_, s16[5,208,512]{2,1,0:T(8,128)(2,1)} %collective-permute-done.10.refs_1_, s16[208,512]{1,0:T(8,128)(2,1)S(1)} %collective-permute-done.14.refs_2_), custom_call_target="tpu_custom_call" | custom-call | flops 983040 | bytes 983040 | tf_op jit(solution)/shard_map/hop/pallas_call | solution.py:135
  68.0 2.6 %collective-permute-start.9 = (s16[208,512]{1,0:T(8,128)(2,1)S(1)}, s16[208,512]{1,0:T(8,128)(2,1)S(1)}, u32[]{:S(2)}, u32[]{:S(2)}) collective-permute-start(s16[208,512]{1,0:T(8,128)(2,1)S(1)} %hop.24), channel_id=1, source_target_pairs={{0,28},{1,29},{2,30},{3,31},{4,0},{5,1},{6,2},{7,3},{8,4},{9,5},{1... | collective-permute-start | bytes 638984 | tf_op jit(solution)/shard_map/ppermute | solution.py:162
  70.9 1.0 collective-permute-done.19.refs_3_
  71.9 2.4 %collective-permute-done.15.refs_2_ = s16[208,512]{1,0:T(8,128)(2,1)S(1)} collective-permute-done((s16[208,512]{1,0:T(8,128)(2,1)S(1)}, s16[208,512]{1,0:T(8,128)(2,1)S(1)}, u32[]{:S(2)}, u32[]{:S(2)}) %collective-permute-start.15) | collective-permute-done | bytes 213024 | tf_op jit(solution)/shard_map/ppermute | solution.py:161
  74.3 1.2 %hop.33 = s16[208,512]{1,0:T(8,128)(2,1)S(1)} custom-call(f32[5,192,512]{2,1,0:T(8,128)S(1)} %get-tuple-element.16.refs_0_, s16[5,208,512]{2,1,0:T(8,128)(2,1)} %collective-permute-done.10.refs_1_, s16[208,512]{1,0:T(8,128)(2,1)S(1)} %collective-permute-done.15.refs_2_, s16[208,512]{1,0:T(8,128)(2,1)S(1)} %collective-permute-done.19.refs_3_), custom_call_target="tpu_custom_call" | custom-call | flops 983040 | bytes 983040 | tf_op jit(solution)/shard_map/hop/pallas_call | solution.py:135
  76.1 1.9 %collective-permute-done.5.forth = s16[208,512]{1,0:T(8,128)(2,1)S(1)} collective-permute-done((s16[208,512]{1,0:T(8,128)(2,1)S(1)}, s16[208,512]{1,0:T(8,128)(2,1)S(1)}, u32[]{:S(2)}, u32[]{:S(2)}) %collective-permute-start.5) | collective-permute-done | bytes 213024 | tf_op jit(solution)/shard_map/ppermute | solution.py:161
  78.0 3.5 %collective-permute-done.20.across = s16[208,512]{1,0:T(8,128)(2,1)S(1)} collective-permute-done((s16[208,512]{1,0:T(8,128)(2,1)S(1)}, s16[208,512]{1,0:T(8,128)(2,1)S(1)}, u32[]{:S(2)}, u32[]{:S(2)}) %collective-permute-start.20) | collective-permute-done | bytes 213024 | tf_op jit(solution)/shard_map/ppermute | solution.py:265
  81.5 3.3 %pick.1 = (f32[192,512]{1,0:T(8,128)}, f32[8,48,128]{2,1,0:T(8,128)S(1)}) custom-call(f32[5,192,512]{2,1,0:T(8,128)S(1)} %get-tuple-element.12.refs_0_.kept, s16[5,208,512]{2,1,0:T(8,128)(2,1)S(1)} %collective-permute-done.refs_1_.other, s16[208,512]{1,0:T(8,128)(2,1)S(1)} %collective-permute-done.5.forth, s16[208,512]{1,0:T(8,128)(2,1)S(1)} %collective-permute-done.9.back, ...), custom_call_target="tpu_custom_call" | custom-call | tf_op jit(solution)/shard_map/pick/pallas_call | solution.py:272
  84.8 14.0 %all_to_all.5.gathered = f32[8,48,128]{2,1,0:T(8,128)S(1)} all-to-all(f32[8,48,128]{2,1,0:T(8,128)S(1)} %get-tuple-element.21), channel_id=1, replica_groups=mesh['rep'=8,'fsdp'=32] {'rep'}, dimensions={0} | all-to-all | bytes 393216 | tf_op jit(solution)/shard_map/all_to_all | solution.py:291
  98.8 3.4 %decode.1 = f32[192,512]{1,0:T(8,128)} custom-call(f32[8,48,128]{2,1,0:T(8,128)S(1)} %all_to_all.5.gathered, bf16[2,192,192]{2,1,0:T(8,128)(2,1)S(1)} %copy-done.7, bf16[2,256,256]{2,1,0:T(8,128)(2,1)S(1)} %copy-done.6), custom_call_target="tpu_custom_call" | custom-call | tf_op jit(solution)/shard_map/decode/pallas_call | solution.py:292
  (73 shorter events, 10.6 us)
Async XLA Ops:
  10.6 14.5 %collective-permute-start.11 = (s16[3,208,512]{2,1,0:T(8,128)(2,1)}, s16[3,208,512]{2,1,0:T(8,128)(2,1)}, u32[]{:S(2)}, u32[]{:S(2)}) collective-permute-start(s16[3,208,512]{2,1,0:T(8,128)(2,1)} %get-tuple-element.19), channel_id=1, source_target_pairs={{0,1},{1,0},{2,3},{3,2},{4,5},{5,4},{6,7},{7,6},{8,9},{9,8},{10,11... | collective-permute-start | bytes 1916936 | tf_op jit(solution)/shard_map/ppermute | solution.py:259
  10.8 9.6 %slice-start = ((s8[9437184]{0:T(1024)(128)(4,1)}), s8[4194304]{0:T(1024)(128)(4,1)S(1)}, s32[]{:S(2)}) async-start(s8[9437184]{0:T(1024)(128)(4,1)} %bitcast.14), calls=%async_computation.1 | async-start | bytes 8388608
  10.8 9.6 %slice-start.1 = ((s8[9437184]{0:T(1024)(128)(4,1)}), s8[4194304]{0:T(1024)(128)(4,1)S(1)}, s32[]{:S(2)}) async-start(s8[9437184]{0:T(1024)(128)(4,1)} %bitcast.14), calls=%async_computation.2 | async-start | bytes 8388608
  15.6 36.8 %collective-permute-start.10 = (s16[5,208,512]{2,1,0:T(8,128)(2,1)}, s16[5,208,512]{2,1,0:T(8,128)(2,1)}, u32[]{:S(2)}, u32[]{:S(2)}) collective-permute-start(s16[5,208,512]{2,1,0:T(8,128)(2,1)} %get-tuple-element.17), channel_id=1, source_target_pairs={{0,1},{1,0},{2,3},{3,2},{4,5},{5,4},{6,7},{7,6},{8,9},{9,8},{10,11... | collective-permute-start | bytes 3194888 | tf_op jit(solution)/shard_map/ppermute | solution.py:259
  16.1 4.4 %slice-start.2 = ((s8[9437184]{0:T(1024)(128)(4,1)}), s8[1048576]{0:T(1024)(128)(4,1)S(1)}, s32[]{:S(2)}) async-start(s8[9437184]{0:T(1024)(128)(4,1)} %bitcast.14), calls=%async_computation.3 | async-start | bytes 2097152
  20.5 12.7 %collective-permute-start.1 = (s16[3,208,512]{2,1,0:T(8,128)(2,1)}, s16[3,208,512]{2,1,0:T(8,128)(2,1)S(1)}, u32[]{:S(2)}, u32[]{:S(2)}) collective-permute-start(s16[3,208,512]{2,1,0:T(8,128)(2,1)} %get-tuple-element.15), channel_id=1, source_target_pairs={{0,1},{1,0},{2,3},{3,2},{4,5},{5,4},{6,7},{7,6},{8,9},{9,8},{10,11... | collective-permute-start | bytes 1916936 | tf_op jit(solution)/shard_map/ppermute | solution.py:259
  20.5 4.6 %copy-start.2 = (f32[3,192,512]{2,1,0:T(8,128)S(1)}, f32[3,192,512]{2,1,0:T(8,128)}, u32[]{:S(2)}) copy-start(f32[3,192,512]{2,1,0:T(8,128)} %copy-done.1) | copy-start | bytes 3538948
  24.6 33.6 %collective-permute-start = (s16[5,208,512]{2,1,0:T(8,128)(2,1)S(1)}, s16[5,208,512]{2,1,0:T(8,128)(2,1)S(1)}, u32[]{:S(2)}, u32[]{:S(2)}) collective-permute-start(s16[5,208,512]{2,1,0:T(8,128)(2,1)S(1)} %get-tuple-element.13), channel_id=1, source_target_pairs={{0,1},{1,0},{2,3},{3,2},{4,5},{5,4},{6,7},{7,6},{8,9},{9,8},{10,11... | collective-permute-start | bytes 3194888 | tf_op jit(solution)/shard_map/ppermute | solution.py:259
  26.2 7.1 %copy-start.4 = (f32[3,192,512]{2,1,0:T(8,128)S(1)}, f32[3,192,512]{2,1,0:T(8,128)}, u32[]{:S(2)}) copy-start(f32[3,192,512]{2,1,0:T(8,128)} %copy-done.3) | copy-start | bytes 3538948
  26.2 10.4 %collective-permute-start.16 = (s16[208,256]{1,0:T(8,128)(2,1)S(1)}, s16[208,256]{1,0:T(8,128)(2,1)S(1)}, u32[]{:S(2)}, u32[]{:S(2)}) collective-permute-start(s16[208,256]{1,0:T(8,128)(2,1)S(1)} %hop.29), channel_id=1, source_target_pairs={{0,28},{1,29},{2,30},{3,31},{4,0},{5,1},{6,2},{7,3},{8,4},{9,5},{1... | collective-permute-start | bytes 319496 | tf_op jit(solution)/shard_map/ppermute | solution.py:159
  33.1 6.3 %collective-permute-start.12 = (s16[208,256]{1,0:T(8,128)(2,1)S(1)}, s16[208,256]{1,0:T(8,128)(2,1)S(1)}, u32[]{:S(2)}, u32[]{:S(2)}) collective-permute-start(s16[208,256]{1,0:T(8,128)(2,1)S(1)} %hop.25), channel_id=1, source_target_pairs={{0,4},{1,5},{2,6},{3,7},{4,8},{5,9},{6,10},{7,11},{8,12},{9,13},{1... | collective-permute-start | bytes 319496 | tf_op jit(solution)/shard_map/ppermute | solution.py:158
  33.3 7.7 %collective-permute-start.6 = (s16[208,256]{1,0:T(8,128)(2,1)S(1)}, s16[208,256]{1,0:T(8,128)(2,1)S(1)}, u32[]{:S(2)}, u32[]{:S(2)}) collective-permute-start(s16[208,256]{1,0:T(8,128)(2,1)S(1)} %hop.21), channel_id=1, source_target_pairs={{0,28},{1,29},{2,30},{3,31},{4,0},{5,1},{6,2},{7,3},{8,4},{9,5},{1... | collective-permute-start | bytes 319496 | tf_op jit(solution)/shard_map/ppermute | solution.py:159
  37.7 12.6 %collective-permute-start.17 = (s16[208,512]{1,0:T(8,128)(2,1)S(1)}, s16[208,512]{1,0:T(8,128)(2,1)S(1)}, u32[]{:S(2)}, u32[]{:S(2)}) collective-permute-start(s16[208,512]{1,0:T(8,128)(2,1)S(1)} %hop.30), channel_id=1, source_target_pairs={{0,28},{1,29},{2,30},{3,31},{4,0},{5,1},{6,2},{7,3},{8,4},{9,5},{1... | collective-permute-start | bytes 638984 | tf_op jit(solution)/shard_map/ppermute | solution.py:162
  40.5 14.5 %collective-permute-start.13 = (s16[208,512]{1,0:T(8,128)(2,1)S(1)}, s16[208,512]{1,0:T(8,128)(2,1)S(1)}, u32[]{:S(2)}, u32[]{:S(2)}) collective-permute-start(s16[208,512]{1,0:T(8,128)(2,1)S(1)} %hop.26), channel_id=1, source_target_pairs={{0,4},{1,5},{2,6},{3,7},{4,8},{5,9},{6,10},{7,11},{8,12},{9,13},{1... | collective-permute-start | bytes 638984 | tf_op jit(solution)/shard_map/ppermute | solution.py:161
  41.1 9.1 %collective-permute-start.2 = (s16[208,256]{1,0:T(8,128)(2,1)S(1)}, s16[208,256]{1,0:T(8,128)(2,1)S(1)}, u32[]{:S(2)}, u32[]{:S(2)}) collective-permute-start(s16[208,256]{1,0:T(8,128)(2,1)S(1)} %hop.17), channel_id=1, source_target_pairs={{0,4},{1,5},{2,6},{3,7},{4,8},{5,9},{6,10},{7,11},{8,12},{9,13},{1... | collective-permute-start | bytes 319496 | tf_op jit(solution)/shard_map/ppermute | solution.py:158
  50.1 8.0 %collective-permute-start.7 = (s16[208,512]{1,0:T(8,128)(2,1)S(1)}, s16[208,512]{1,0:T(8,128)(2,1)S(1)}, u32[]{:S(2)}, u32[]{:S(2)}) collective-permute-start(s16[208,512]{1,0:T(8,128)(2,1)S(1)} %hop.22), channel_id=1, source_target_pairs={{0,28},{1,29},{2,30},{3,31},{4,0},{5,1},{6,2},{7,3},{8,4},{9,5},{1... | collective-permute-start | bytes 638984 | tf_op jit(solution)/shard_map/ppermute | solution.py:162
  50.3 9.4 %collective-permute-start.3 = (s16[208,512]{1,0:T(8,128)(2,1)S(1)}, s16[208,512]{1,0:T(8,128)(2,1)S(1)}, u32[]{:S(2)}, u32[]{:S(2)}) collective-permute-start(s16[208,512]{1,0:T(8,128)(2,1)S(1)} %hop.18), channel_id=1, source_target_pairs={{0,4},{1,5},{2,6},{3,7},{4,8},{5,9},{6,10},{7,11},{8,12},{9,13},{1... | collective-permute-start | bytes 638984 | tf_op jit(solution)/shard_map/ppermute | solution.py:161
  53.5 9.2 %collective-permute-start.18 = (s16[208,512]{1,0:T(8,128)(2,1)S(1)}, s16[208,512]{1,0:T(8,128)(2,1)S(1)}, u32[]{:S(2)}, u32[]{:S(2)}) collective-permute-start(s16[208,512]{1,0:T(8,128)(2,1)S(1)} %hop.31), channel_id=1, source_target_pairs={{0,28},{1,29},{2,30},{3,31},{4,0},{5,1},{6,2},{7,3},{8,4},{9,5},{1... | collective-permute-start | bytes 638984 | tf_op jit(solution)/shard_map/ppermute | solution.py:162
  56.1 9.1 %collective-permute-start.14 = (s16[208,512]{1,0:T(8,128)(2,1)S(1)}, s16[208,512]{1,0:T(8,128)(2,1)S(1)}, u32[]{:S(2)}, u32[]{:S(2)}) collective-permute-start(s16[208,512]{1,0:T(8,128)(2,1)S(1)} %hop.27), channel_id=1, source_target_pairs={{0,4},{1,5},{2,6},{3,7},{4,8},{5,9},{6,10},{7,11},{8,12},{9,13},{1... | collective-permute-start | bytes 638984 | tf_op jit(solution)/shard_map/ppermute | solution.py:161
  58.3 9.5 %collective-permute-start.8 = (s16[208,512]{1,0:T(8,128)(2,1)S(1)}, s16[208,512]{1,0:T(8,128)(2,1)S(1)}, u32[]{:S(2)}, u32[]{:S(2)}) collective-permute-start(s16[208,512]{1,0:T(8,128)(2,1)S(1)} %hop.23), channel_id=1, source_target_pairs={{0,28},{1,29},{2,30},{3,31},{4,0},{5,1},{6,2},{7,3},{8,4},{9,5},{1... | collective-permute-start | bytes 638984 | tf_op jit(solution)/shard_map/ppermute | solution.py:162
  59.9 10.7 %collective-permute-start.4 = (s16[208,512]{1,0:T(8,128)(2,1)S(1)}, s16[208,512]{1,0:T(8,128)(2,1)S(1)}, u32[]{:S(2)}, u32[]{:S(2)}) collective-permute-start(s16[208,512]{1,0:T(8,128)(2,1)S(1)} %hop.19), channel_id=1, source_target_pairs={{0,4},{1,5},{2,6},{3,7},{4,8},{5,9},{6,10},{7,11},{8,12},{9,13},{1... | collective-permute-start | bytes 638984 | tf_op jit(solution)/shard_map/ppermute | solution.py:161
  63.8 8.1 %collective-permute-start.19 = (s16[208,512]{1,0:T(8,128)(2,1)S(1)}, s16[208,512]{1,0:T(8,128)(2,1)S(1)}, u32[]{:S(2)}, u32[]{:S(2)}) collective-permute-start(s16[208,512]{1,0:T(8,128)(2,1)S(1)} %hop.32), channel_id=1, source_target_pairs={{0,28},{1,29},{2,30},{3,31},{4,0},{5,1},{6,2},{7,3},{8,4},{9,5},{1... | collective-permute-start | bytes 638984 | tf_op jit(solution)/shard_map/ppermute | solution.py:162
  66.3 8.0 %collective-permute-start.15 = (s16[208,512]{1,0:T(8,128)(2,1)S(1)}, s16[208,512]{1,0:T(8,128)(2,1)S(1)}, u32[]{:S(2)}, u32[]{:S(2)}) collective-permute-start(s16[208,512]{1,0:T(8,128)(2,1)S(1)} %hop.28), channel_id=1, source_target_pairs={{0,4},{1,5},{2,6},{3,7},{4,8},{5,9},{6,10},{7,11},{8,12},{9,13},{1... | collective-permute-start | bytes 638984 | tf_op jit(solution)/shard_map/ppermute | solution.py:161
  68.0 8.1 %collective-permute-start.9 = (s16[208,512]{1,0:T(8,128)(2,1)S(1)}, s16[208,512]{1,0:T(8,128)(2,1)S(1)}, u32[]{:S(2)}, u32[]{:S(2)}) collective-permute-start(s16[208,512]{1,0:T(8,128)(2,1)S(1)} %hop.24), channel_id=1, source_target_pairs={{0,28},{1,29},{2,30},{3,31},{4,0},{5,1},{6,2},{7,3},{8,4},{9,5},{1... | collective-permute-start | bytes 638984 | tf_op jit(solution)/shard_map/ppermute | solution.py:162
  70.8 5.3 %copy-start.11 = (s32[1,3,8,128]{3,2,1,0:T(8,128)S(1)}, s32[1,3,8,128]{3,2,1,0:T(8,128)}, u32[]{:S(2)}) copy-start(s32[1,3,8,128]{3,2,1,0:T(8,128)} %param.13) | copy-start | bytes 36868
  70.8 10.7 %copy-start.6 = (bf16[2,256,256]{2,1,0:T(8,128)(2,1)S(1)}, bf16[2,256,256]{2,1,0:T(8,128)(2,1)}, u32[]{:S(2)}) copy-start(bf16[2,256,256]{2,1,0:T(8,128)(2,1)} %constant.74.clone.cols) | copy-start | bytes 786436
  70.8 10.7 %copy-start.7 = (bf16[2,192,192]{2,1,0:T(8,128)(2,1)S(1)}, bf16[2,192,192]{2,1,0:T(8,128)(2,1)}, u32[]{:S(2)}) copy-start(bf16[2,192,192]{2,1,0:T(8,128)(2,1)} %constant.73.clone.rows_t) | copy-start | bytes 442372
  70.8 10.6 %copy-start.8 = (f32[1,192,512]{2,1,0:T(8,128)S(1)}, f32[1,192,512]{2,1,0:T(8,128)}, u32[]{:S(2)}) copy-start(f32[1,192,512]{2,1,0:T(8,128)} %param.12) | copy-start | bytes 1179652
  70.8 10.6 %copy-start.9 = (bf16[2,256,256]{2,1,0:T(8,128)(2,1)S(1)}, bf16[2,256,256]{2,1,0:T(8,128)(2,1)}, u32[]{:S(2)}) copy-start(bf16[2,256,256]{2,1,0:T(8,128)(2,1)} %constant.75.clone.cols_t) | copy-start | bytes 786436
  70.8 10.6 %copy-start.10 = (bf16[2,192,192]{2,1,0:T(8,128)(2,1)S(1)}, bf16[2,192,192]{2,1,0:T(8,128)(2,1)}, u32[]{:S(2)}) copy-start(bf16[2,192,192]{2,1,0:T(8,128)(2,1)} %constant.72.clone.rows) | copy-start | bytes 442372
  70.8 7.1 %collective-permute-start.5 = (s16[208,512]{1,0:T(8,128)(2,1)S(1)}, s16[208,512]{1,0:T(8,128)(2,1)S(1)}, u32[]{:S(2)}, u32[]{:S(2)}) collective-permute-start(s16[208,512]{1,0:T(8,128)(2,1)S(1)} %hop.20), channel_id=1, source_target_pairs={{0,4},{1,5},{2,6},{3,7},{4,8},{5,9},{6,10},{7,11},{8,12},{9,13},{1... | collective-permute-start | bytes 638984 | tf_op jit(solution)/shard_map/ppermute | solution.py:161
  75.5 5.9 %collective-permute-start.20 = (s16[208,512]{1,0:T(8,128)(2,1)S(1)}, s16[208,512]{1,0:T(8,128)(2,1)S(1)}, u32[]{:S(2)}, u32[]{:S(2)}) collective-permute-start(s16[208,512]{1,0:T(8,128)(2,1)S(1)} %hop.33), channel_id=1, source_target_pairs={{0,2},{1,3},{2,0},{3,1},{4,6},{5,7},{6,4},{7,5},{8,10},{9,11},{10,... | collective-permute-start | bytes 638984 | tf_op jit(solution)/shard_map/ppermute | solution.py:265
  (4 other events, 6.9 us)

commit v3 on v1

--- a/solution.py
+++ b/solution.py
@@ -12,6 +12,11 @@
 SLOTS = 128
 BF = jnp.bfloat16
 F32 = jnp.float32
+I16 = jnp.int16
+HEAD = 16
+RINGS = 8
+ROWS = 192
+BOTH = 2 * ROWS
 
 
 def cosine_table(side):
@@ -54,8 +59,224 @@
     return jnp.concatenate(pieces, axis=1)
 
 
-def pick_kernel(grad, momentum, places, rows, rows_t, cols, cols_t, new_moment, payload, coef, sparse):
-    moment = 0.9 * momentum[...] + grad[...]
+def encode(x, out):
+    top = jnp.max(jnp.abs(x), axis=0, keepdims=True)
+    code = jnp.ceil(128.0 * jnp.log2(jnp.maximum(top, 1e-30))) + 1.0
+    scale = 32767.0 * jnp.exp2(code * (-1.0 / 128.0))
+    height = x.shape[0]
+    out[:height, :] = jnp.round(x * scale).astype(jnp.int32).astype(I16)
+    out[height:, :] = jnp.broadcast_to(code, (HEAD, x.shape[1])).astype(jnp.int32).astype(I16)
+
+
+def decode(ref):
+    height = ref.shape[0] - HEAD
+    code = ref[height:, :].astype(jnp.int32).astype(F32)[:1, :]
+    scale = jnp.exp2(code * (1.0 / 128.0)) * (1.0 / 32767.0)
+    return ref[:height, :].astype(jnp.int32).astype(F32) * scale
+
+
+def place():
+    me = lax.axis_index("fsdp")
+    return me // 4, lax.rem(me // 2, 2), lax.rem(me, 2)
+
+
+def route(move):
+    pairs = []
+    for source in range(4 * RINGS):
+        z, y, core = move(source // 4, (source // 2) % 2, source % 2)
+        pairs.append((source, ((z % RINGS) * 2 + y) * 2 + core))
+    return pairs
+
+
+ALONG = route(lambda z, y, c: (z + 1 - 2 * c, y, c))
+ASLANT = route(lambda z, y, c: (z + 1 - 2 * c, 1 - y, c))
+BESIDE = route(lambda z, y, c: (z, 1 - y, c))
+WITHIN = route(lambda z, y, c: (z, y, 1 - c))
+
+
+def product(left, right):
+    return lax.dot_general(left, right, (((0,), (0,)), ((), ())), preferred_element_type=F32)
+
+
+def load_blocks(steps, swap, inputs, grads, blocks, whole, sems):
+    z, y, core = place()
+    target = 1 - y if swap else y
+    copies = [pltpu.make_async_copy(grads, whole, sems.at[len(steps)])]
+    for n, step in enumerate(steps):
+        block = lax.rem(z + step * (1 - 2 * core) + RINGS, RINGS) * 2 + target
+        columns = pl.ds(pl.multiple_of(block * BOTH, BOTH), BOTH)
+        copies.append(pltpu.make_async_copy(inputs.at[:, columns], blocks.at[n], sems.at[n]))
+    for copy in copies:
+        copy.start()
+    copies[0].wait()
+    return core, copies[1:]
+
+
+AWAY = (4, -3, -2, -1, 0)
+KEPT = (3, 2, 1)
+
+
+def away_kernel(swap, inputs, grads, _, keep4, keep0, away, blocks, whole, both, sems):
+    core, copies = load_blocks(AWAY, swap, inputs, grads, blocks, whole, sems)
+    half = keep4.shape[1]
+    copies[0].wait()
+    both[...] = product(blocks[0], whole[...])
+    keep4[...] = both[:, pl.ds(pl.multiple_of(core * half, half), half)]
+    other = both[:, pl.ds(pl.multiple_of((1 - core) * half, half), half)]
+    encode(other[:ROWS], away.at[0, :, :half])
+    encode(other[ROWS:], away.at[0, :, half:])
+    for n in (1, 2, 3):
+        copies[n].wait()
+        total = product(blocks[n], whole[...])
+        encode(total[:ROWS], away.at[2 * n - 1])
+        encode(total[ROWS:], away.at[2 * n])
+    copies[4].wait()
+    both[...] = product(blocks[4], whole[...])
+    keep0[...] = both[pl.ds(pl.multiple_of(core * ROWS, ROWS), ROWS), :]
+    encode(both[pl.ds(pl.multiple_of((1 - core) * ROWS, ROWS), ROWS), :], away.at[7])
+
+
+def kept_kernel(swap, inputs, grads, _, keep3, keep2, keep1, blocks, whole, sems):
+    _, copies = load_blocks(KEPT, swap, inputs, grads, blocks, whole, sems)
+    for n, keep in enumerate((keep3, keep2, keep1)):
+        copies[n].wait()
+        keep[...] = product(blocks[n], whole[...])
+
+
+def partial_sums(kernel, swap, inputs, grads, after, steps, outs, scratch, name):
+    tokens, breadth = grads.shape
+    return pl.pallas_call(
+        lambda *refs: kernel(swap, *refs),
+        in_specs=[pl.BlockSpec(memory_space=pl.ANY)] * 3,
+        out_shape=[jax.ShapeDtypeStruct(*out) for out in outs],
+        scratch_shapes=[
+            pltpu.VMEM((steps, tokens, BOTH), BF),
+            pltpu.VMEM((tokens, breadth), BF),
+            *scratch,
+            pltpu.SemaphoreType.DMA((steps + 1,)),
+        ],
+        compiler_params=pltpu.CompilerParams(vmem_limit_bytes=56 << 20),
+        cost_estimate=pl.CostEstimate(
+            flops=steps * 6 * BOTH * tokens * breadth,
+            bytes_accessed=steps * (2 * BOTH * tokens + 2 * BOTH * breadth),
+            transcendentals=0,
+        ),
+        name=name,
+    )(inputs, grads, after)
+
+
+def away_sums(swap, inputs, grads, after):
+    breadth = grads.shape[1]
+    outs = [((BOTH, breadth // 2), F32), ((ROWS, breadth), F32), ((8, ROWS + HEAD, breadth), I16)]
+    return partial_sums(away_kernel, swap, inputs, grads, after, len(AWAY), outs, [pltpu.VMEM((BOTH, breadth), F32)], "away")
+
+
+def kept_sums(swap, inputs, grads, after):
+    outs = [((BOTH, grads.shape[1]), F32)] * 3
+    return partial_sums(kept_kernel, swap, inputs, grads, after, len(KEPT), outs, [], "kept")
+
+
+ANYWHERE = "any"
+
+
+def call_local(kernel, args, specs, outs, name, scratch=()):
+    def spec(arg, cut):
+        if cut == ANYWHERE:
+            return pl.BlockSpec(memory_space=pl.ANY)
+        block, index = cut or (arg.shape, (0,) * arg.ndim)
+        return pl.BlockSpec(block, lambda i: index)
+
+    result = pl.pallas_call(
+        kernel,
+        grid=(1,),
+        in_specs=[spec(arg, cut) for arg, cut in zip(args, specs)],
+        out_specs=[pl.BlockSpec(shape, lambda i, n=len(shape): (0,) * n) for shape, _ in outs],
+        out_shape=[jax.ShapeDtypeStruct(*out) for out in outs],
+        scratch_shapes=list(scratch),
+        compiler_params=pltpu.CompilerParams(vmem_limit_bytes=16 << 20),
+        cost_estimate=pl.CostEstimate(flops=10 * BOTH * 512, bytes_accessed=10 * BOTH * 512, transcendentals=0),
+        name=name,
+    )(*args)
+    return result
+
+
+def decode_pair(low, high):
+    return jnp.concatenate([decode(low), decode(high)], axis=0)
+
+
+def first_hop_kernel(keep, other, out):
+    half = keep.shape[1]
+    encode(keep[...] + decode_pair(other.at[:, :half], other.at[:, half:]), out)
+
+
+def second_hop_kernel(keep, low, high, arrived, _, out, total):
+    half = arrived.shape[1]
+    total[...] = keep[...] + decode_pair(low, high)
+    mine = pl.ds(pl.multiple_of(place()[2] * half, half), half)
+    total[:, mine] += decode(arrived)
+    encode(total[...], out)
+
+
+def later_hop_kernel(keep, low, high, arrived, *rest):
+    out = rest[-1]
+    encode(keep[...] + decode_pair(low, high) + decode(arrived), out)
+
+
+def own_kernel(keep, other, out):
+    encode(keep[...] + decode(other), out)
+
+
+def meet_kernel(straight, aslant, keep, other, beside, kept, away, total):
+    core = place()[2]
+    total[...] = decode(straight) + decode(aslant)
+    kept[...] = total[pl.ds(pl.multiple_of(core * ROWS, ROWS), ROWS), :] + keep[...] + decode(other) + decode(beside)
+    encode(total[pl.ds(pl.multiple_of((1 - core) * ROWS, ROWS), ROWS), :], away)
+
+
+def replica_sum(inputs, grads):
+    breadth = grads.shape[1]
+    tall, short = BOTH + HEAD, ROWS + HEAD
+
+    def send(array, pairs):
+        return lax.ppermute(array, "fsdp", pairs)
+
+    def unit(n):
+        return (None, short, breadth), (n, 0, 0)
+
+    def first_hop(keep, other):
+        return call_local(first_hop_kernel, (keep, other), (None, unit(0)), [((tall, breadth // 2), I16)], "hop1")[0]
+
+    def later_hop(step, keep, other, arrived, after):
+        first = 2 * step - 3
+        scratch = [pltpu.VMEM((BOTH, breadth), F32)] if step == 2 else []
+        return call_local(
+            second_hop_kernel if step == 2 else later_hop_kernel,
+            (keep, other, other, arrived, after), (None, unit(first), unit(first + 1), None, ANYWHERE),
+            [((tall, breadth), I16)], "hop%d" % step, scratch)[0]
+
+    keep4_a, keep0_a, away = away_sums(True, inputs, grads, inputs)
+    other_a = send(away, WITHIN)
+    keep4_b, keep0_b, away = away_sums(False, inputs, grads, away)
+    other_b = send(away, WITHIN)
+    ring_a = first_hop(keep4_a, other_a)
+    ring_b = first_hop(keep4_b, other_b)
+    kept_a = kept_sums(True, inputs, grads, ring_a)
+    kept_b = kept_sums(False, inputs, grads, ring_b)
+    own_a = call_local(own_kernel, (keep0_a, other_a), (None, unit(7)), [((short, breadth), I16)], "own")[0]
+    beside = send(own_a, BESIDE)
+    for step in (2, 3, 4):
+        ring_a = later_hop(step, kept_a[step - 2], other_a, send(ring_a, ALONG), own_a)
+        ring_b = later_hop(step, kept_b[step - 2], other_b, send(ring_b, ALONG), own_a)
+    ring_a, ring_b = send(ring_a, ASLANT), send(ring_b, ALONG)
+    kept, away = call_local(
+        meet_kernel, (ring_b, ring_a, keep0_b, other_b, beside), (None, None, None, unit(7), None),
+        [((ROWS, breadth), F32), ((short, breadth), I16)], "meet", [pltpu.VMEM((BOTH, breadth), F32)])
+    return kept, send(away, WITHIN)
+
+
+def pick_kernel(kept, other, momentum, places, rows, rows_t, cols, cols_t, new_moment, payload, coef, sparse):
+    grad = kept[...] + decode(other)
+    moment = 0.9 * momentum[...] + grad
     coef[...] = right_product(left_product(rows, moment), cols_t)
     tile_rows, tile_cols = grad.shape[0] // CH, grad.shape[1] // CH
     group = 4
@@ -122,10 +343,7 @@
     tiles = (height // CH) * (breadth // CH)
     live = lax.broadcasted_iota(jnp.int32, indices.shape[1:], 2) < counts[0]
     places = jnp.where(live, indices[0], -1).reshape(tiles, SLOTS)
-    gradient = lax.psum_scatter(
-        lax.dot_general(activations[0], out_grads[0], (((0,), (0,)), ((), ())), preferred_element_type=F32),
-        "fsdp", scatter_dimension=0, tiled=True,
-    )
+    kept, other = replica_sum(activations[0], out_grads[0])
     new_moment, payload = pl.pallas_call(
         pick_kernel,
         out_shape=[
@@ -135,7 +353,7 @@
         scratch_shapes=[pltpu.VMEM((height, breadth), F32), pltpu.VMEM((height, breadth), F32)],
         compiler_params=pltpu.CompilerParams(vmem_limit_bytes=32 << 20),
         name="pick",
-    )(gradient, momentum[0], places, rows, rows_t, cols, cols_t)
+    )(kept, other, momentum[0], places, rows, rows_t, cols, cols_t)
     gathered = lax.all_to_all(payload, "rep", 0, 0)
     step_dir = pl.pallas_call(
         decode_kernel,

time: 202 us -> 86.1 us (0.43)
  waiting for transfers between devices: 154 us -> 22 us
  Pallas kernels: 6.46 us -> 28.9 us
  starting transfers between devices: 0.04 us -> 19.9 us
  between operations: 14.8 us -> 1.57 us
  matrix products: 11.8 us -> 0 us
    reduce_scatter x1 -> x0, waiting for transfers between devices: 154 us -> none  [body(): lax.psum_scatter(lax.dot_general(activations[0], out_grads[0], (((0,), (0...]
    pallas_call x0 -> x14, Pallas kernels: none -> 22.3 us  [the longest x4 19.1 us: partial_sums(): pl.pallas_call(lambda *refs: kernel(swap, *refs), in_specs=[pl.BlockSpec(...]
    ppermute x0 -> x12, waiting for transfers between devices: none -> 22 us  [send(): return lax.ppermute(array, 'fsdp', pairs)]
    ppermute x0 -> x12, starting transfers between devices: none -> 19.9 us  [send(): return lax.ppermute(array, 'fsdp', pairs)]
    dot_general x1 -> x0, matrix products: 11.8 us -> none  [body(): lax.dot_general(activations[0], out_grads[0], (((0,), (0,)), ((), ())), p...]
  transfers between devices with their start and end apart: 1 -> 12, of which waited for: 1 -> 6; matrix products, arithmetic and copies ran while one was open for 0% -> 0% of each run, Pallas kernels for 0% -> 19%
where the time goes in v3:
time: 86.1 us; the launch traced here: 85.8 us
  Pallas kernels  28.9 us (34%)
  waiting for transfers between devices  22 us (26%)
  starting transfers between devices  19.9 us (23%)
  blocking collectives  13.4 us (16%)
  between operations  1.57 us (2%)
    ppermute x12, waiting for transfers between devices, send(): return lax.ppermute(array, 'fsdp', pairs)  22 us
    ppermute x12, starting transfers between devices, send(): return lax.ppermute(array, 'fsdp', pairs)  19.9 us
    pallas_call x4, Pallas kernels, partial_sums(): pl.pallas_call(lambda *refs: kernel(swap, *refs), in_specs=[pl.BlockSpec(...  19.1 us
    all_to_all x1, blocking collectives, body(): gathered = lax.all_to_all(payload, 'rep', 0, 0)  13.4 us
    pallas_call x1, Pallas kernels, body(): pl.pallas_call(decode_kernel, out_shape=jax.ShapeDtypeStruct((height, bre...  3.37 us
    pallas_call x10, Pallas kernels, call_local(): pl.pallas_call(kernel, grid=(1,), in_specs=[spec(arg, cut) for arg, cut i...  3.26 us
    pallas_call x1, Pallas kernels, body(): pl.pallas_call(pick_kernel, out_shape=[jax.ShapeDtypeStruct((height, brea...  3.17 us
  transfers between devices with their start and end apart: 12, of which 6 were waited for; matrix products, arithmetic and copies ran while one was open for 0% of the time, Pallas kernels for 19%

profile of v3, /device:TPU:1, one launch (start us, length us, event | category | flops | bytes accessed | tf_op | source)
XLA Modules:
  0.0 85.8 jit_solution(999841339302449706)
XLA Ops:
  0.6 5.7 %away.2 = (f32[384,256]{1,0:T(8,128)}, f32[192,512]{1,0:T(8,128)}, s16[8,208,512]{2,1,0:T(8,128)(2,1)}) custom-call(bf16[768,6144]{1,0:T(8,128)(2,1)} %bitcast.9, bf16[768,512]{1,0:T(8,128)(2,1)} %bitcast.14, bf16[768,6144]{1,0:T(8,128)(2,1)} %bitcast.10), custom_call_target="tpu_custom_call" | custom-call | flops 4529848320 | bytes 4915200 | tf_op jit(solution)/shard_map/away/pallas_call | solution.py:148
  6.4 3.3 %collective-permute-start.2 = (s16[8,208,512]{2,1,0:T(8,128)(2,1)}, s16[8,208,512]{2,1,0:T(8,128)(2,1)S(1)}, u32[]{:S(2)}, u32[]{:S(2)}) collective-permute-start(s16[8,208,512]{2,1,0:T(8,128)(2,1)} %get-tuple-element.18.refs_2_), channel_id=1, source_target_pairs={{0,1},{1,0},{2,3},{3,2},{4,5},{5,4},{6,7},{7,6},{8,9},{9,8},{10,11... | collective-permute-start | bytes 5111816 | tf_op jit(solution)/shard_map/ppermute | solution.py:241
  9.7 5.7 %away.3 = (f32[384,256]{1,0:T(8,128)}, f32[192,512]{1,0:T(8,128)}, s16[8,208,512]{2,1,0:T(8,128)(2,1)}) custom-call(bf16[768,6144]{1,0:T(8,128)(2,1)} %bitcast.11, bf16[768,512]{1,0:T(8,128)(2,1)} %bitcast.15, s16[8,208,512]{2,1,0:T(8,128)(2,1)} %get-tuple-element.18.refs_2_), custom_call_target="tpu_custom_call" | custom-call | flops 4529848320 | bytes 4915200 | tf_op jit(solution)/shard_map/away/pallas_call | solution.py:148
  15.5 0.1 hop1.3.refs_2_
  15.7 3.9 %collective-permute-start.6 = (s16[400,256]{1,0:T(8,128)(2,1)S(1)}, s16[400,256]{1,0:T(8,128)(2,1)S(1)}, u32[]{:S(2)}, u32[]{:S(2)}) collective-permute-start(s16[400,256]{1,0:T(8,128)(2,1)S(1)} %hop1.3.refs_2_), channel_id=1, source_target_pairs={{0,4},{1,29},{2,6},{3,31},{4,8},{5,1},{6,10},{7,3},{8,12},{9,5},{1... | collective-permute-start | bytes 614408 | tf_op jit(solution)/shard_map/ppermute | solution.py:241
  19.6 3.8 %kept.3 = (f32[384,512]{1,0:T(8,128)}, f32[384,512]{1,0:T(8,128)}, f32[384,512]{1,0:T(8,128)}) custom-call(bf16[768,6144]{1,0:T(8,128)(2,1)} %bitcast.12, bf16[768,512]{1,0:T(8,128)(2,1)} %bitcast.16, s16[400,256]{1,0:T(8,128)(2,1)} %copy-done.1), custom_call_target="tpu_custom_call" | custom-call | flops 2717908992 | bytes 2949120 | tf_op jit(solution)/shard_map/kept/pallas_call | solution.py:148
  23.5 0.8 collective-permute-start.1
  24.5 3.9 %kept.2 = (f32[384,512]{1,0:T(8,128)}, f32[384,512]{1,0:T(8,128)}, f32[384,512]{1,0:T(8,128)}) custom-call(bf16[768,6144]{1,0:T(8,128)(2,1)} %bitcast.13, bf16[768,512]{1,0:T(8,128)(2,1)} %bitcast.17, s16[400,256]{1,0:T(8,128)(2,1)} %copy-done.2), custom_call_target="tpu_custom_call" | custom-call | flops 2717908992 | bytes 2949120 | tf_op jit(solution)/shard_map/kept/pallas_call | solution.py:148
  28.5 0.5 hop2.3
  28.9 0.8 collective-permute-start.7
  29.7 0.5 hop2.2
  30.2 0.8 collective-permute-start.3
  31.0 5.1 %collective-permute-done.7.arrived = s16[400,512]{1,0:T(8,128)(2,1)S(1)} collective-permute-done((s16[400,512]{1,0:T(8,128)(2,1)S(1)}, s16[400,512]{1,0:T(8,128)(2,1)S(1)}, u32[]{:S(2)}, u32[]{:S(2)}) %collective-permute-start.7) | collective-permute-done | bytes 409632 | tf_op jit(solution)/shard_map/ppermute | solution.py:241
  36.1 0.3 hop3.3
  36.4 1.9 %collective-permute-start.8 = (s16[400,512]{1,0:T(8,128)(2,1)S(1)}, s16[400,512]{1,0:T(8,128)(2,1)S(1)}, u32[]{:S(2)}, u32[]{:S(2)}) collective-permute-start(s16[400,512]{1,0:T(8,128)(2,1)S(1)} %hop3.3), channel_id=1, source_target_pairs={{0,4},{1,29},{2,6},{3,31},{4,8},{5,1},{6,10},{7,3},{8,12},{9,5},{1... | collective-permute-start | bytes 1228808 | tf_op jit(solution)/shard_map/ppermute | solution.py:241
  38.3 1.9 %collective-permute-done.3.arrived = s16[400,512]{1,0:T(8,128)(2,1)S(1)} collective-permute-done((s16[400,512]{1,0:T(8,128)(2,1)S(1)}, s16[400,512]{1,0:T(8,128)(2,1)S(1)}, u32[]{:S(2)}, u32[]{:S(2)}) %collective-permute-start.3) | collective-permute-done | bytes 409632 | tf_op jit(solution)/shard_map/ppermute | solution.py:241
  40.3 0.3 hop3.2
  40.6 2.0 %collective-permute-start.4 = (s16[400,512]{1,0:T(8,128)(2,1)S(1)}, s16[400,512]{1,0:T(8,128)(2,1)S(1)}, u32[]{:S(2)}, u32[]{:S(2)}) collective-permute-start(s16[400,512]{1,0:T(8,128)(2,1)S(1)} %hop3.2), channel_id=1, source_target_pairs={{0,4},{1,29},{2,6},{3,31},{4,8},{5,1},{6,10},{7,3},{8,12},{9,5},{1... | collective-permute-start | bytes 1228808 | tf_op jit(solution)/shard_map/ppermute | solution.py:241
  42.6 2.3 %collective-permute-done.8.arrived = s16[400,512]{1,0:T(8,128)(2,1)S(1)} collective-permute-done((s16[400,512]{1,0:T(8,128)(2,1)S(1)}, s16[400,512]{1,0:T(8,128)(2,1)S(1)}, u32[]{:S(2)}, u32[]{:S(2)}) %collective-permute-start.8) | collective-permute-done | bytes 409632 | tf_op jit(solution)/shard_map/ppermute | solution.py:241
  44.9 0.3 hop4.3
  45.2 2.7 %collective-permute-start.9 = (s16[400,512]{1,0:T(8,128)(2,1)S(1)}, s16[400,512]{1,0:T(8,128)(2,1)S(1)}, u32[]{:S(2)}, u32[]{:S(2)}) collective-permute-start(s16[400,512]{1,0:T(8,128)(2,1)S(1)} %hop4.3), channel_id=1, source_target_pairs={{0,6},{1,31},{2,4},{3,29},{4,10},{5,3},{6,8},{7,1},{8,14},{9,7},{1... | collective-permute-start | bytes 1228808 | tf_op jit(solution)/shard_map/ppermute | solution.py:241
  48.0 1.3 %collective-permute-done.4.arrived = s16[400,512]{1,0:T(8,128)(2,1)S(1)} collective-permute-done((s16[400,512]{1,0:T(8,128)(2,1)S(1)}, s16[400,512]{1,0:T(8,128)(2,1)S(1)}, u32[]{:S(2)}, u32[]{:S(2)}) %collective-permute-start.4) | collective-permute-done | bytes 409632 | tf_op jit(solution)/shard_map/ppermute | solution.py:241
  49.3 0.3 hop4.2
  49.7 1.7 %collective-permute-start.5 = (s16[400,512]{1,0:T(8,128)(2,1)S(1)}, s16[400,512]{1,0:T(8,128)(2,1)S(1)}, u32[]{:S(2)}, u32[]{:S(2)}) collective-permute-start(s16[400,512]{1,0:T(8,128)(2,1)S(1)} %hop4.2), channel_id=1, source_target_pairs={{0,4},{1,29},{2,6},{3,31},{4,8},{5,1},{6,10},{7,3},{8,12},{9,5},{1... | collective-permute-start | bytes 1228808 | tf_op jit(solution)/shard_map/ppermute | solution.py:241
  51.4 1.3 %collective-permute-start.10 = (s16[208,512]{1,0:T(8,128)(2,1)S(1)}, s16[208,512]{1,0:T(8,128)(2,1)S(1)}, u32[]{:S(2)}, u32[]{:S(2)}) collective-permute-start(s16[208,512]{1,0:T(8,128)(2,1)S(1)} %own.1._.rest_0_), channel_id=1, source_target_pairs={{0,2},{1,3},{2,0},{3,1},{4,6},{5,7},{6,4},{7,5},{8,10},{9,11},{10,... | collective-permute-start | bytes 638984 | tf_op jit(solution)/shard_map/ppermute | solution.py:241
  53.4 10.2 %collective-permute-done.10.beside = s16[208,512]{1,0:T(8,128)(2,1)S(1)} collective-permute-done((s16[208,512]{1,0:T(8,128)(2,1)S(1)}, s16[208,512]{1,0:T(8,128)(2,1)S(1)}, u32[]{:S(2)}, u32[]{:S(2)}) %collective-permute-start.10) | collective-permute-done | bytes 213024 | tf_op jit(solution)/shard_map/ppermute | solution.py:241
  63.6 0.7 meet.1
  64.3 0.5 collective-permute-start.11
  64.8 1.1 %collective-permute-done.11.other = s16[208,512]{1,0:T(8,128)(2,1)S(1)} collective-permute-done((s16[208,512]{1,0:T(8,128)(2,1)S(1)}, s16[208,512]{1,0:T(8,128)(2,1)S(1)}, u32[]{:S(2)}, u32[]{:S(2)}) %collective-permute-start.11) | collective-permute-done | bytes 213024 | tf_op jit(solution)/shard_map/ppermute | solution.py:241
  65.9 3.2 %pick.1 = (f32[192,512]{1,0:T(8,128)}, f32[8,48,128]{2,1,0:T(8,128)S(1)}) custom-call(f32[192,512]{1,0:T(8,128)S(1)} %get-tuple-element.30.kept, s16[208,512]{1,0:T(8,128)(2,1)S(1)} %collective-permute-done.11.other, f32[192,512]{1,0:T(8,128)S(1)} %bitcast.8, s32[24,128]{1,0:T(8,128)S(1)} %bitcast_select_fusion.places, bf16[2,192,192]{2,1,0:T(8,128)(2,1)S(1)} %copy-done.16, ...), custom_call_target="tpu_custom_call" | custom-call | tf_op jit(solution)/shard_map/pick/pallas_call | solution.py:347
  69.1 13.4 %all_to_all.5.gathered = f32[8,48,128]{2,1,0:T(8,128)S(1)} all-to-all(f32[8,48,128]{2,1,0:T(8,128)S(1)} %get-tuple-element.33), channel_id=1, replica_groups=mesh['rep'=8,'fsdp'=32] {'rep'}, dimensions={0} | all-to-all | bytes 393216 | tf_op jit(solution)/shard_map/all_to_all | solution.py:357
  82.5 3.4 %decode.1 = f32[192,512]{1,0:T(8,128)} custom-call(f32[8,48,128]{2,1,0:T(8,128)S(1)} %all_to_all.5.gathered, bf16[2,192,192]{2,1,0:T(8,128)(2,1)S(1)} %copy-done.9, bf16[2,256,256]{2,1,0:T(8,128)(2,1)S(1)} %copy-done), custom_call_target="tpu_custom_call" | custom-call | tf_op jit(solution)/shard_map/decode/pallas_call | solution.py:358
  (47 shorter events, 0.5 us)
Async XLA Ops:
  6.4 9.2 %copy-start.13 = (f32[384,256]{1,0:T(8,128)S(1)}, f32[384,256]{1,0:T(8,128)}, u32[]{:S(2)}) copy-start(f32[384,256]{1,0:T(8,128)} %get-tuple-element.25.keep) | copy-start | bytes 1179652
  6.4 9.1 %collective-permute-start.2 = (s16[8,208,512]{2,1,0:T(8,128)(2,1)}, s16[8,208,512]{2,1,0:T(8,128)(2,1)S(1)}, u32[]{:S(2)}, u32[]{:S(2)}) collective-permute-start(s16[8,208,512]{2,1,0:T(8,128)(2,1)} %get-tuple-element.18.refs_2_), channel_id=1, source_target_pairs={{0,1},{1,0},{2,3},{3,2},{4,5},{5,4},{6,7},{7,6},{8,9},{9,8},{10,11... | collective-permute-start | bytes 5111816 | tf_op jit(solution)/shard_map/ppermute | solution.py:241
  15.4 8.0 %collective-permute-start = (s16[8,208,512]{2,1,0:T(8,128)(2,1)}, s16[8,208,512]{2,1,0:T(8,128)(2,1)S(1)}, u32[]{:S(2)}, u32[]{:S(2)}) collective-permute-start(s16[8,208,512]{2,1,0:T(8,128)(2,1)} %get-tuple-element.20), channel_id=1, source_target_pairs={{0,1},{1,0},{2,3},{3,2},{4,5},{5,4},{6,7},{7,6},{8,9},{9,8},{10,11... | collective-permute-start | bytes 5111816 | tf_op jit(solution)/shard_map/ppermute | solution.py:241
  15.7 3.9 %copy-start.1 = (s16[400,256]{1,0:T(8,128)(2,1)}, s16[400,256]{1,0:T(8,128)(2,1)S(1)}, u32[]{:S(2)}) copy-start(s16[400,256]{1,0:T(8,128)(2,1)S(1)} %hop1.3.refs_2_) | copy-start | bytes 614404
  15.7 7.7 %copy-start.12 = (f32[384,256]{1,0:T(8,128)S(1)}, f32[384,256]{1,0:T(8,128)}, u32[]{:S(2)}) copy-start(f32[384,256]{1,0:T(8,128)} %get-tuple-element.19.keep) | copy-start | bytes 1179652
  15.7 12.7 %collective-permute-start.6 = (s16[400,256]{1,0:T(8,128)(2,1)S(1)}, s16[400,256]{1,0:T(8,128)(2,1)S(1)}, u32[]{:S(2)}, u32[]{:S(2)}) collective-permute-start(s16[400,256]{1,0:T(8,128)(2,1)S(1)} %hop1.3.refs_2_), channel_id=1, source_target_pairs={{0,4},{1,29},{2,6},{3,31},{4,8},{5,1},{6,10},{7,3},{8,12},{9,5},{1... | collective-permute-start | bytes 614408 | tf_op jit(solution)/shard_map/ppermute | solution.py:241
  23.4 1.0 %copy-start.11 = (f32[192,512]{1,0:T(8,128)S(1)}, f32[192,512]{1,0:T(8,128)}, u32[]{:S(2)}) copy-start(f32[192,512]{1,0:T(8,128)} %get-tuple-element.24.keep) | copy-start | bytes 1179652
  23.5 1.0 %copy-start.2 = (s16[400,256]{1,0:T(8,128)(2,1)}, s16[400,256]{1,0:T(8,128)(2,1)S(1)}, u32[]{:S(2)}) copy-start(s16[400,256]{1,0:T(8,128)(2,1)S(1)} %hop1.2.refs_2_) | copy-start | bytes 614404
  23.5 6.2 %collective-permute-start.1 = (s16[400,256]{1,0:T(8,128)(2,1)S(1)}, s16[400,256]{1,0:T(8,128)(2,1)S(1)}, u32[]{:S(2)}, u32[]{:S(2)}) collective-permute-start(s16[400,256]{1,0:T(8,128)(2,1)S(1)} %hop1.2.refs_2_), channel_id=1, source_target_pairs={{0,4},{1,29},{2,6},{3,31},{4,8},{5,1},{6,10},{7,3},{8,12},{9,5},{1... | collective-permute-start | bytes 614408 | tf_op jit(solution)/shard_map/ppermute | solution.py:241
  24.5 3.9 %copy-start.7 = (f32[384,512]{1,0:T(8,128)S(1)}, f32[384,512]{1,0:T(8,128)}, u32[]{:S(2)}) copy-start(f32[384,512]{1,0:T(8,128)} %get-tuple-element.28.keep) | copy-start | bytes 2359300
  28.4 1.3 %copy-start.8 = (f32[384,512]{1,0:T(8,128)S(1)}, f32[384,512]{1,0:T(8,128)}, u32[]{:S(2)}) copy-start(f32[384,512]{1,0:T(8,128)} %get-tuple-element.23.keep) | copy-start | bytes 2359300
  28.9 7.2 %collective-permute-start.7 = (s16[400,512]{1,0:T(8,128)(2,1)S(1)}, s16[400,512]{1,0:T(8,128)(2,1)S(1)}, u32[]{:S(2)}, u32[]{:S(2)}) collective-permute-start(s16[400,512]{1,0:T(8,128)(2,1)S(1)} %hop2.3), channel_id=1, source_target_pairs={{0,4},{1,29},{2,6},{3,31},{4,8},{5,1},{6,10},{7,3},{8,12},{9,5},{1... | collective-permute-start | bytes 1228808 | tf_op jit(solution)/shard_map/ppermute | solution.py:241
  29.7 6.4 %copy-start.5 = (f32[384,512]{1,0:T(8,128)S(1)}, f32[384,512]{1,0:T(8,128)}, u32[]{:S(2)}) copy-start(f32[384,512]{1,0:T(8,128)} %get-tuple-element.27.keep) | copy-start | bytes 2359300
  30.2 10.0 %collective-permute-start.3 = (s16[400,512]{1,0:T(8,128)(2,1)S(1)}, s16[400,512]{1,0:T(8,128)(2,1)S(1)}, u32[]{:S(2)}, u32[]{:S(2)}) collective-permute-start(s16[400,512]{1,0:T(8,128)(2,1)S(1)} %hop2.2), channel_id=1, source_target_pairs={{0,4},{1,29},{2,6},{3,31},{4,8},{5,1},{6,10},{7,3},{8,12},{9,5},{1... | collective-permute-start | bytes 1228808 | tf_op jit(solution)/shard_map/ppermute | solution.py:241
  36.1 4.1 %copy-start.6 = (f32[384,512]{1,0:T(8,128)S(1)}, f32[384,512]{1,0:T(8,128)}, u32[]{:S(2)}) copy-start(f32[384,512]{1,0:T(8,128)} %get-tuple-element.22.keep) | copy-start | bytes 2359300
  36.4 8.4 %collective-permute-start.8 = (s16[400,512]{1,0:T(8,128)(2,1)S(1)}, s16[400,512]{1,0:T(8,128)(2,1)S(1)}, u32[]{:S(2)}, u32[]{:S(2)}) collective-permute-start(s16[400,512]{1,0:T(8,128)(2,1)S(1)} %hop3.3), channel_id=1, source_target_pairs={{0,4},{1,29},{2,6},{3,31},{4,8},{5,1},{6,10},{7,3},{8,12},{9,5},{1... | collective-permute-start | bytes 1228808 | tf_op jit(solution)/shard_map/ppermute | solution.py:241
  40.3 4.6 %copy-start.3 = (f32[384,512]{1,0:T(8,128)S(1)}, f32[384,512]{1,0:T(8,128)}, u32[]{:S(2)}) copy-start(f32[384,512]{1,0:T(8,128)} %get-tuple-element.26.keep) | copy-start | bytes 2359300
  40.6 8.7 %collective-permute-start.4 = (s16[400,512]{1,0:T(8,128)(2,1)S(1)}, s16[400,512]{1,0:T(8,128)(2,1)S(1)}, u32[]{:S(2)}, u32[]{:S(2)}) collective-permute-start(s16[400,512]{1,0:T(8,128)(2,1)S(1)} %hop3.2), channel_id=1, source_target_pairs={{0,4},{1,29},{2,6},{3,31},{4,8},{5,1},{6,10},{7,3},{8,12},{9,5},{1... | collective-permute-start | bytes 1228808 | tf_op jit(solution)/shard_map/ppermute | solution.py:241
  44.9 4.4 %copy-start.4 = (f32[384,512]{1,0:T(8,128)S(1)}, f32[384,512]{1,0:T(8,128)}, u32[]{:S(2)}) copy-start(f32[384,512]{1,0:T(8,128)} %get-tuple-element.21.keep) | copy-start | bytes 2359300
  45.2 18.4 %collective-permute-start.9 = (s16[400,512]{1,0:T(8,128)(2,1)S(1)}, s16[400,512]{1,0:T(8,128)(2,1)S(1)}, u32[]{:S(2)}, u32[]{:S(2)}) collective-permute-start(s16[400,512]{1,0:T(8,128)(2,1)S(1)} %hop4.3), channel_id=1, source_target_pairs={{0,6},{1,31},{2,4},{3,29},{4,10},{5,3},{6,8},{7,1},{8,14},{9,7},{1... | collective-permute-start | bytes 1228808 | tf_op jit(solution)/shard_map/ppermute | solution.py:241
  49.3 14.3 %copy-start.10 = (f32[192,512]{1,0:T(8,128)S(1)}, f32[192,512]{1,0:T(8,128)}, u32[]{:S(2)}) copy-start(f32[192,512]{1,0:T(8,128)} %get-tuple-element.29.keep) | copy-start | bytes 1179652
  49.6 15.2 %copy-start.17 = (s32[1,3,8,128]{3,2,1,0:T(8,128)S(1)}, s32[1,3,8,128]{3,2,1,0:T(8,128)}, u32[]{:S(2)}) copy-start(s32[1,3,8,128]{3,2,1,0:T(8,128)} %param.12) | copy-start | bytes 36868
  49.6 16.3 %copy-start = (bf16[2,256,256]{2,1,0:T(8,128)(2,1)S(1)}, bf16[2,256,256]{2,1,0:T(8,128)(2,1)}, u32[]{:S(2)}) copy-start(bf16[2,256,256]{2,1,0:T(8,128)(2,1)} %constant.12.clone.cols) | copy-start | bytes 786436
  49.6 16.2 %copy-start.9 = (bf16[2,192,192]{2,1,0:T(8,128)(2,1)S(1)}, bf16[2,192,192]{2,1,0:T(8,128)(2,1)}, u32[]{:S(2)}) copy-start(bf16[2,192,192]{2,1,0:T(8,128)(2,1)} %constant.11.clone.rows_t) | copy-start | bytes 442372
  49.6 16.2 %copy-start.14 = (f32[1,192,512]{2,1,0:T(8,128)S(1)}, f32[1,192,512]{2,1,0:T(8,128)}, u32[]{:S(2)}) copy-start(f32[1,192,512]{2,1,0:T(8,128)} %param.11) | copy-start | bytes 1179652
  49.7 16.2 %copy-start.15 = (bf16[2,256,256]{2,1,0:T(8,128)(2,1)S(1)}, bf16[2,256,256]{2,1,0:T(8,128)(2,1)}, u32[]{:S(2)}) copy-start(bf16[2,256,256]{2,1,0:T(8,128)(2,1)} %constant.13.clone.cols_t) | copy-start | bytes 786436
  49.7 16.2 %copy-start.16 = (bf16[2,192,192]{2,1,0:T(8,128)(2,1)S(1)}, bf16[2,192,192]{2,1,0:T(8,128)(2,1)}, u32[]{:S(2)}) copy-start(bf16[2,192,192]{2,1,0:T(8,128)(2,1)} %constant.10.clone.rows) | copy-start | bytes 442372
  49.7 13.9 %collective-permute-start.5 = (s16[400,512]{1,0:T(8,128)(2,1)S(1)}, s16[400,512]{1,0:T(8,128)(2,1)S(1)}, u32[]{:S(2)}, u32[]{:S(2)}) collective-permute-start(s16[400,512]{1,0:T(8,128)(2,1)S(1)} %hop4.2), channel_id=1, source_target_pairs={{0,4},{1,29},{2,6},{3,31},{4,8},{5,1},{6,10},{7,3},{8,12},{9,5},{1... | collective-permute-start | bytes 1228808 | tf_op jit(solution)/shard_map/ppermute | solution.py:241
  51.4 12.2 %collective-permute-start.10 = (s16[208,512]{1,0:T(8,128)(2,1)S(1)}, s16[208,512]{1,0:T(8,128)(2,1)S(1)}, u32[]{:S(2)}, u32[]{:S(2)}) collective-permute-start(s16[208,512]{1,0:T(8,128)(2,1)S(1)} %own.1._.rest_0_), channel_id=1, source_target_pairs={{0,2},{1,3},{2,0},{3,1},{4,6},{5,7},{6,4},{7,5},{8,10},{9,11},{10,... | collective-permute-start | bytes 638984 | tf_op jit(solution)/shard_map/ppermute | solution.py:241
  64.3 1.6 %collective-permute-start.11 = (s16[208,512]{1,0:T(8,128)(2,1)S(1)}, s16[208,512]{1,0:T(8,128)(2,1)S(1)}, u32[]{:S(2)}, u32[]{:S(2)}) collective-permute-start(s16[208,512]{1,0:T(8,128)(2,1)S(1)} %get-tuple-element.31), channel_id=1, source_target_pairs={{0,1},{1,0},{2,3},{3,2},{4,5},{5,4},{6,7},{7,6},{8,9},{9,8},{10,11... | collective-permute-start | bytes 638984 | tf_op jit(solution)/shard_map/ppermute | solution.py:241

commit v4 on v3

--- a/solution.py
+++ b/solution.py
@@ -98,62 +98,82 @@
     return lax.dot_general(left, right, (((0,), (0,)), ((), ())), preferred_element_type=F32)
 
 
-def load_blocks(steps, swap, inputs, grads, blocks, whole, sems):
+def blocks_in_turn(steps, swap, inputs, grads, blocks, whole, sems):
     z, y, core = place()
     target = 1 - y if swap else y
-    copies = [pltpu.make_async_copy(grads, whole, sems.at[len(steps)])]
-    for n, step in enumerate(steps):
-        block = lax.rem(z + step * (1 - 2 * core) + RINGS, RINGS) * 2 + target
+
+    def load(n):
+        block = lax.rem(z + steps[n] * (1 - 2 * core) + RINGS, RINGS) * 2 + target
         columns = pl.ds(pl.multiple_of(block * BOTH, BOTH), BOTH)
-        copies.append(pltpu.make_async_copy(inputs.at[:, columns], blocks.at[n], sems.at[n]))
-    for copy in copies:
-        copy.start()
-    copies[0].wait()
-    return core, copies[1:]
-
-
-AWAY = (4, -3, -2, -1, 0)
+        return pltpu.make_async_copy(inputs.at[:, columns], blocks.at[n], sems.at[n])
+
+    first = pltpu.make_async_copy(grads, whole, sems.at[len(steps)])
+    first.start()
+    load(0).start()
+    load(1).start()
+    first.wait()
+    for n in range(len(steps)):
+        load(n).wait()
+        if n + 2 < len(steps):
+            load(n + 2).start()
+        yield product(blocks[n], whole[...])
+
+
+EARLY = (4, -3)
+LATE = (-2, -1, 0)
 KEPT = (3, 2, 1)
 
 
-def away_kernel(swap, inputs, grads, _, keep4, keep0, away, blocks, whole, both, sems):
-    core, copies = load_blocks(AWAY, swap, inputs, grads, blocks, whole, sems)
+def early_kernel(swap, inputs, grads, _, keep4, away, blocks, whole, sems, both):
+    core = place()[2]
     half = keep4.shape[1]
-    copies[0].wait()
-    both[...] = product(blocks[0], whole[...])
+    turns = blocks_in_turn(EARLY, swap, inputs, grads, blocks, whole, sems)
+    both[...] = next(turns)
     keep4[...] = both[:, pl.ds(pl.multiple_of(core * half, half), half)]
     other = both[:, pl.ds(pl.multiple_of((1 - core) * half, half), half)]
     encode(other[:ROWS], away.at[0, :, :half])
     encode(other[ROWS:], away.at[0, :, half:])
-    for n in (1, 2, 3):
-        copies[n].wait()
-        total = product(blocks[n], whole[...])
-        encode(total[:ROWS], away.at[2 * n - 1])
-        encode(total[ROWS:], away.at[2 * n])
-    copies[4].wait()
-    both[...] = product(blocks[4], whole[...])
+    total = next(turns)
+    encode(total[:ROWS], away.at[1])
+    encode(total[ROWS:], away.at[2])
+
+
+def late_kernel(swap, inputs, grads, _, keep0, *refs):
+    away, (blocks, whole, sems, both) = refs[:5], refs[5:]
+    core = place()[2]
+    turns = blocks_in_turn(LATE, swap, inputs, grads, blocks, whole, sems)
+    for n in range(2):
+        total = next(turns)
+        encode(total[:ROWS], away[2 * n])
+        encode(total[ROWS:], away[2 * n + 1])
+    both[...] = next(turns)
     keep0[...] = both[pl.ds(pl.multiple_of(core * ROWS, ROWS), ROWS), :]
-    encode(both[pl.ds(pl.multiple_of((1 - core) * ROWS, ROWS), ROWS), :], away.at[7])
-
-
-def kept_kernel(swap, inputs, grads, _, keep3, keep2, keep1, blocks, whole, sems):
-    _, copies = load_blocks(KEPT, swap, inputs, grads, blocks, whole, sems)
-    for n, keep in enumerate((keep3, keep2, keep1)):
-        copies[n].wait()
-        keep[...] = product(blocks[n], whole[...])
-
-
-def partial_sums(kernel, swap, inputs, grads, after, steps, outs, scratch, name):
+    encode(both[pl.ds(pl.multiple_of((1 - core) * ROWS, ROWS), ROWS), :], away[4])
+
+
+def kept_kernel(swap, inputs, grads, _, keep3, keep2, keep1, blocks, whole, sems, sums, out_sems):
+    keeps = (keep3, keep2, keep1)
+    copies = []
+    for n, total in enumerate(blocks_in_turn(KEPT, swap, inputs, grads, blocks, whole, sems)):
+        sums[n] = total
+        copies.append(pltpu.make_async_copy(sums.at[n], keeps[n], out_sems.at[n]))
+        copies[n].start()
+    for copy in copies:
+        copy.wait()
+
+
+def partial_sums(kernel, swap, inputs, grads, after, steps, outs, out_spec, scratch, name):
     tokens, breadth = grads.shape
     return pl.pallas_call(
         lambda *refs: kernel(swap, *refs),
         in_specs=[pl.BlockSpec(memory_space=pl.ANY)] * 3,
+        out_specs=[out_spec] * len(outs),
         out_shape=[jax.ShapeDtypeStruct(*out) for out in outs],
         scratch_shapes=[
             pltpu.VMEM((steps, tokens, BOTH), BF),
             pltpu.VMEM((tokens, breadth), BF),
+            pltpu.SemaphoreType.DMA((steps + 1,)),
             *scratch,
-            pltpu.SemaphoreType.DMA((steps + 1,)),
         ],
         compiler_params=pltpu.CompilerParams(vmem_limit_bytes=56 << 20),
         cost_estimate=pl.CostEstimate(
@@ -165,15 +185,25 @@
     )(inputs, grads, after)
 
 
-def away_sums(swap, inputs, grads, after):
+def early_sums(swap, inputs, grads, after):
     breadth = grads.shape[1]
-    outs = [((BOTH, breadth // 2), F32), ((ROWS, breadth), F32), ((8, ROWS + HEAD, breadth), I16)]
-    return partial_sums(away_kernel, swap, inputs, grads, after, len(AWAY), outs, [pltpu.VMEM((BOTH, breadth), F32)], "away")
+    outs = [((BOTH, breadth // 2), F32), ((3, ROWS + HEAD, breadth), I16)]
+    return partial_sums(early_kernel, swap, inputs, grads, after, len(EARLY), outs,
+                        pl.BlockSpec(memory_space=pltpu.VMEM), [pltpu.VMEM((BOTH, breadth), F32)], "early")
+
+
+def late_sums(swap, inputs, grads, after):
+    breadth = grads.shape[1]
+    outs = [((ROWS, breadth), F32)] + [((ROWS + HEAD, breadth), I16)] * 5
+    return partial_sums(late_kernel, swap, inputs, grads, after, len(LATE), outs,
+                        pl.BlockSpec(memory_space=pltpu.VMEM), [pltpu.VMEM((BOTH, breadth), F32)], "late")
 
 
 def kept_sums(swap, inputs, grads, after):
-    outs = [((BOTH, grads.shape[1]), F32)] * 3
-    return partial_sums(kept_kernel, swap, inputs, grads, after, len(KEPT), outs, [], "kept")
+    breadth = grads.shape[1]
+    return partial_sums(kept_kernel, swap, inputs, grads, after, len(KEPT), [((BOTH, breadth), F32)] * 3,
+                        pl.BlockSpec(memory_space=pl.ANY),
+                        [pltpu.VMEM((3, BOTH, breadth), F32), pltpu.SemaphoreType.DMA((3,))], "kept")
 
 
 ANYWHERE = "any"
@@ -246,61 +276,77 @@
     def first_hop(keep, other):
         return call_local(first_hop_kernel, (keep, other), (None, unit(0)), [((tall, breadth // 2), I16)], "hop1")[0]
 
-    def later_hop(step, keep, other, arrived, after):
-        first = 2 * step - 3
+    def later_hop(step, keep, early, late, arrived, after):
+        if step == 2:
+            others, cuts = (early, early), (unit(1), unit(2))
+        else:
+            others, cuts = late[2 * step - 6:2 * step - 4], (None, None)
         scratch = [pltpu.VMEM((BOTH, breadth), F32)] if step == 2 else []
         return call_local(
             second_hop_kernel if step == 2 else later_hop_kernel,
-            (keep, other, other, arrived, after), (None, unit(first), unit(first + 1), None, ANYWHERE),
+            (keep, *others, arrived, after), (None, *cuts, None, ANYWHERE),
             [((tall, breadth), I16)], "hop%d" % step, scratch)[0]
 
-    keep4_a, keep0_a, away = away_sums(True, inputs, grads, inputs)
-    other_a = send(away, WITHIN)
-    keep4_b, keep0_b, away = away_sums(False, inputs, grads, away)
-    other_b = send(away, WITHIN)
-    ring_a = first_hop(keep4_a, other_a)
-    ring_b = first_hop(keep4_b, other_b)
+    keep4_a, away = early_sums(True, inputs, grads, inputs)
+    early_a = send(away, WITHIN)
+    keep4_b, away = early_sums(False, inputs, grads, away)
+    early_b = send(away, WITHIN)
+    ring_a = first_hop(keep4_a, early_a)
+    ring_b = first_hop(keep4_b, early_b)
     kept_a = kept_sums(True, inputs, grads, ring_a)
-    kept_b = kept_sums(False, inputs, grads, ring_b)
-    own_a = call_local(own_kernel, (keep0_a, other_a), (None, unit(7)), [((short, breadth), I16)], "own")[0]
+    kept_b = kept_sums(False, inputs, grads, kept_a[0])
+    ring_a = later_hop(2, kept_a[0], early_a, None, send(ring_a, ALONG), kept_a[0])
+    ring_b = later_hop(2, kept_b[0], early_b, None, send(ring_b, ALONG), kept_b[0])
+    keep0_a, *away = late_sums(True, inputs, grads, ring_a)
+    late_a = [send(part, WITHIN) for part in away]
+    keep0_b, *away = late_sums(False, inputs, grads, ring_b)
+    late_b = [send(part, WITHIN) for part in away]
+    own_a = call_local(own_kernel, (keep0_a, late_a[4]), (None, None), [((short, breadth), I16)], "own")[0]
     beside = send(own_a, BESIDE)
-    for step in (2, 3, 4):
-        ring_a = later_hop(step, kept_a[step - 2], other_a, send(ring_a, ALONG), own_a)
-        ring_b = later_hop(step, kept_b[step - 2], other_b, send(ring_b, ALONG), own_a)
+    ring_a = later_hop(3, kept_a[1], None, late_a, send(ring_a, ALONG), own_a)
+    ring_b = later_hop(3, kept_b[1], None, late_b, send(ring_b, ALONG), own_a)
+    ring_a = later_hop(4, kept_a[2], None, late_a, send(ring_a, ALONG), own_a)
+    ring_b = later_hop(4, kept_b[2], None, late_b, send(ring_b, ALONG), beside)
     ring_a, ring_b = send(ring_a, ASLANT), send(ring_b, ALONG)
     kept, away = call_local(
-        meet_kernel, (ring_b, ring_a, keep0_b, other_b, beside), (None, None, None, unit(7), None),
+        meet_kernel, (ring_b, ring_a, keep0_b, late_b[4], beside), (None,) * 5,
         [((ROWS, breadth), F32), ((short, breadth), I16)], "meet", [pltpu.VMEM((BOTH, breadth), F32)])
     return kept, send(away, WITHIN)
+
+
+def spread(row, height):
+    return jnp.concatenate([jnp.broadcast_to(row, (HEAD, row.shape[1])).astype(BF)] * (height // HEAD), axis=0)
+
+
+def row_numbers(height, width):
+    return lax.broadcasted_iota(jnp.int32, (height, width), 0).astype(F32).astype(BF)
 
 
 def pick_kernel(kept, other, momentum, places, rows, rows_t, cols, cols_t, new_moment, payload, coef, sparse):
     grad = kept[...] + decode(other)
     moment = 0.9 * momentum[...] + grad
     coef[...] = right_product(left_product(rows, moment), cols_t)
-    tile_rows, tile_cols = grad.shape[0] // CH, grad.shape[1] // CH
+    tile_rows, tile_cols = momentum.shape[0] // CH, momentum.shape[1] // CH
     group = 4
     tiles = tile_rows * tile_cols
+    width = group * SLOTS
+    numbers = row_numbers(group * CH, width)
+    one, none = jnp.ones((), BF), jnp.zeros((), BF)
     for i in range(tile_rows):
         for h in range(tile_cols // group):
             first = i * tile_cols + h * group
             part = [places[first + n:first + n + 1, :] for n in range(group)]
-            flat = jnp.concatenate(part, axis=1)
-            row_code = flat >> 6
-            col_code = jnp.concatenate([(p & 63) + CH * n for n, p in enumerate(part)], axis=1)
-            width = group * SLOTS
-            in_col = lax.broadcasted_iota(jnp.int32, (group * CH, width), 0) == col_code
-            in_row = lax.broadcasted_iota(jnp.int32, (CH, width), 0) == row_code
-            col_hot = jnp.where(in_col, 1.0, 0.0).astype(BF)
-            row_hot = jnp.where(in_row, 1.0, 0.0).astype(BF)
+            row_code = (jnp.concatenate(part, axis=1) >> 6).astype(F32)
+            col_code = jnp.concatenate([(p & 63) + CH * n for n, p in enumerate(part)], axis=1).astype(F32)
+            col_hot = jnp.where(numbers == spread(col_code, group * CH), one, none)
+            row_hot = jnp.where(numbers[:CH] == spread(row_code, CH), one, none)
             block = coef[i * CH:(i + 1) * CH, h * group * CH:(h + 1) * group * CH]
             high, low = split(block)
-            spread = dot(high, col_hot) + dot(low, col_hot)
-            value = jnp.sum(jnp.where(in_row, spread, 0.0), axis=0, keepdims=True)
+            chosen = dot(high, col_hot) + dot(low, col_hot)
+            value = jnp.sum(chosen * row_hot.astype(F32), axis=0, keepdims=True)
             for n in range(group):
-                one = value[:, n * SLOTS:(n + 1) * SLOTS]
                 for r in range(payload.shape[0]):
-                    payload[r, first + n:first + n + 1, :] = one
+                    payload[r, first + n:first + n + 1, :] = value[:, n * SLOTS:(n + 1) * SLOTS]
             sparse[i * CH:(i + 1) * CH, h * group * CH:(h + 1) * group * CH] = block * dot_nt(row_hot, col_hot)
     for r in range(payload.shape[0]):
         payload[r, tiles:, :] = places[...].astype(F32)
@@ -311,19 +357,23 @@
     reps = gathered.shape[0]
     tiles = gathered.shape[1] // 2
     tile_cols = total.shape[1] // CH
+    numbers = row_numbers(CH, SLOTS)
+    one, none = jnp.ones((), BF), jnp.zeros((), BF)
+    parts = []
+    for r in range(reps):
+        high, low = split(gathered[r, :tiles, :])
+        place = gathered[r, tiles:, :].astype(jnp.int32)
+        parts.append([high.astype(F32), low.astype(F32), (place >> 6).astype(F32), (place & 63).astype(F32)])
     for pair in range(tiles // 2):
         blocks = []
         for t in (2 * pair, 2 * pair + 1):
             highs, lows, hots = [], [], []
             for r in range(reps):
-                value = gathered[r, t:t + 1, :]
-                place = gathered[r, tiles + t:tiles + t + 1, :].astype(jnp.int32)
-                in_row = lax.broadcasted_iota(jnp.int32, (CH, SLOTS), 0) == (place >> 6)
-                in_col = lax.broadcasted_iota(jnp.int32, (CH, SLOTS), 0) == (place & 63)
-                high, low = split(value)
-                highs.append(jnp.where(in_row, high.astype(F32), 0.0).astype(BF))
-                lows.append(jnp.where(in_row, low.astype(F32), 0.0).astype(BF))
-                hots.append(jnp.where(in_col, 1.0, 0.0).astype(BF))
+                high, low, row_code, col_code = (spread(part[t:t + 1, :], CH) for part in parts[r])
+                in_row = numbers == row_code
+                highs.append(jnp.where(in_row, high, none))
+                lows.append(jnp.where(in_row, low, none))
+                hots.append(jnp.where(numbers == col_code, one, none))
             both = jnp.concatenate([jnp.concatenate(highs, axis=1), jnp.concatenate(lows, axis=1)], axis=0)
             out = dot_nt(both, jnp.concatenate(hots, axis=1))
             blocks.append(out[:CH] + out[CH:])

time: 86.1 us -> 85.6 us (level)
  waiting for transfers between devices: 22 us -> 11.2 us
  starting transfers between devices: 19.9 us -> 26.7 us
  Pallas kernels: 28.9 us -> 32 us
    ppermute x12 -> x22, waiting for transfers between devices: 22 us -> 11.2 us  [send(): return lax.ppermute(array, 'fsdp', pairs)]
    ppermute x12 -> x22, starting transfers between devices: 19.9 us -> 26.7 us  [send(): return lax.ppermute(array, 'fsdp', pairs)]
    pallas_call x4 -> x6, Pallas kernels: 19.1 us -> 22.4 us  [partial_sums(): pl.pallas_call(lambda *refs: kernel(swap, *refs), in_specs=[pl.BlockSpec(...]
  transfers between devices with their start and end apart: 12 -> 22, of which waited for: 6 -> 7; matrix products, arithmetic and copies ran while one was open for 0% -> 0% of each run, Pallas kernels for 19% -> 25%
where the time goes in v4:
time: 85.6 us; the launch traced here: 85.3 us
  Pallas kernels  32 us (37%)
  starting transfers between devices  26.7 us (31%)
  blocking collectives  13.7 us (16%)
  waiting for transfers between devices  11.2 us (13%)
  between operations  1.67 us (2%)
    ppermute x22, starting transfers between devices, send(): return lax.ppermute(array, 'fsdp', pairs)  26.7 us
    pallas_call x6, Pallas kernels, partial_sums(): pl.pallas_call(lambda *refs: kernel(swap, *refs), in_specs=[pl.BlockSpec(...  22.4 us
    all_to_all x1, blocking collectives, body(): gathered = lax.all_to_all(payload, 'rep', 0, 0)  13.7 us
    ppermute x22, waiting for transfers between devices, send(): return lax.ppermute(array, 'fsdp', pairs)  11.2 us
    pallas_call x10, Pallas kernels, call_local(): pl.pallas_call(kernel, grid=(1,), in_specs=[spec(arg, cut) for arg, cut i...  3.28 us
    pallas_call x1, Pallas kernels, body(): pl.pallas_call(pick_kernel, out_shape=[jax.ShapeDtypeStruct((height, brea...  3.13 us
    pallas_call x1, Pallas kernels, body(): pl.pallas_call(decode_kernel, out_shape=jax.ShapeDtypeStruct((height, bre...  3.12 us
  transfers between devices with their start and end apart: 22, of which 7 were waited for; matrix products, arithmetic and copies ran while one was open for 0% of the time, Pallas kernels for 25%

profile of v4, /device:TPU:1, one launch (start us, length us, event | category | flops | bytes accessed | tf_op | source)
XLA Modules:
  0.0 85.3 jit_solution(13792011894950892279)
XLA Ops:
  0.6 3.5 %early.2 = (f32[384,256]{1,0:T(8,128)}, s16[3,208,512]{2,1,0:T(8,128)(2,1)}) custom-call(bf16[768,6144]{1,0:T(8,128)(2,1)} %bitcast.9, bf16[768,512]{1,0:T(8,128)(2,1)} %bitcast.16, bf16[768,6144]{1,0:T(8,128)(2,1)} %bitcast.10), custom_call_target="tpu_custom_call" | custom-call | flops 1811939328 | bytes 1966080 | tf_op jit(solution)/shard_map/early/pallas_call | solution.py:167
  4.1 3.3 %collective-permute-start = (s16[3,208,512]{2,1,0:T(8,128)(2,1)}, s16[3,208,512]{2,1,0:T(8,128)(2,1)S(1)}, u32[]{:S(2)}, u32[]{:S(2)}) collective-permute-start(s16[3,208,512]{2,1,0:T(8,128)(2,1)} %get-tuple-element.29.refs_2_), channel_id=1, source_target_pairs={{0,1},{1,0},{2,3},{3,2},{4,5},{5,4},{6,7},{7,6},{8,9},{9,8},{10,11... | collective-permute-start | bytes 1916936 | tf_op jit(solution)/shard_map/ppermute | solution.py:271
  7.4 3.4 %early.3 = (f32[384,256]{1,0:T(8,128)}, s16[3,208,512]{2,1,0:T(8,128)(2,1)}) custom-call(bf16[768,6144]{1,0:T(8,128)(2,1)} %bitcast.11, bf16[768,512]{1,0:T(8,128)(2,1)} %bitcast.17, s16[3,208,512]{2,1,0:T(8,128)(2,1)} %get-tuple-element.29.refs_2_), custom_call_target="tpu_custom_call" | custom-call | flops 1811939328 | bytes 1966080 | tf_op jit(solution)/shard_map/early/pallas_call | solution.py:167
  11.2 3.9 %collective-permute-start.8 = (s16[400,256]{1,0:T(8,128)(2,1)S(1)}, s16[400,256]{1,0:T(8,128)(2,1)S(1)}, u32[]{:S(2)}, u32[]{:S(2)}) collective-permute-start(s16[400,256]{1,0:T(8,128)(2,1)S(1)} %hop1.2.refs_2_), channel_id=1, source_target_pairs={{0,4},{1,29},{2,6},{3,31},{4,8},{5,1},{6,10},{7,3},{8,12},{9,5},{1... | collective-permute-start | bytes 614408 | tf_op jit(solution)/shard_map/ppermute | solution.py:271
  15.1 3.9 %kept.2 = (f32[384,512]{1,0:T(8,128)}, f32[384,512]{1,0:T(8,128)}, f32[384,512]{1,0:T(8,128)}) custom-call(bf16[768,6144]{1,0:T(8,128)(2,1)} %bitcast.12, bf16[768,512]{1,0:T(8,128)(2,1)} %bitcast.18, s16[400,256]{1,0:T(8,128)(2,1)} %copy-done.5), custom_call_target="tpu_custom_call" | custom-call | flops 2717908992 | bytes 2949120 | tf_op jit(solution)/shard_map/kept/pallas_call | solution.py:167
  19.1 0.8 collective-permute-start.2
  19.9 3.9 %kept.3 = (f32[384,512]{1,0:T(8,128)}, f32[384,512]{1,0:T(8,128)}, f32[384,512]{1,0:T(8,128)}) custom-call(bf16[768,6144]{1,0:T(8,128)(2,1)} %bitcast.13, bf16[768,512]{1,0:T(8,128)(2,1)} %bitcast.19, f32[384,512]{1,0:T(8,128)} %get-tuple-element.30.refs_2_.keep._), custom_call_target="tpu_custom_call" | custom-call | flops 2717908992 | bytes 2949120 | tf_op jit(solution)/shard_map/kept/pallas_call | solution.py:167
  23.8 0.5 hop2.3.refs_2_
  24.3 0.8 collective-permute-start.17
  25.1 3.9 %late.3 = (f32[192,512]{1,0:T(8,128)}, s16[208,512]{1,0:T(8,128)(2,1)}, s16[208,512]{1,0:T(8,128)(2,1)}, s16[208,512]{1,0:T(8,128)(2,1)}, s16[208,512]{1,0:T(8,128)(2,1)}, /*index=5*/s16[208,512]{1,0:T(8,128)(2,1)}) custom-call(bf16[768,6144]{1,0:T(8,128)(2,1)} %bitcast.14, bf16[768,512]{1,0:T(8,128)(2,1)} %bitcast.20, s16[400,512]{1,0:T(8,128)(2,1)} %copy-done.2), custom_call_target="tpu_custom_call" | custom-call | flops 2717908992 | bytes 2949120 | tf_op jit(solution)/shard_map/late/pallas_call | solution.py:167
  29.2 0.5 collective-permute-start.15
  29.8 0.5 hop2.2.refs_2_
  30.4 1.0 %collective-permute-start.7 = (s16[400,512]{1,0:T(8,128)(2,1)S(1)}, s16[400,512]{1,0:T(8,128)(2,1)S(1)}, u32[]{:S(2)}, u32[]{:S(2)}) collective-permute-start(s16[400,512]{1,0:T(8,128)(2,1)S(1)} %hop2.2.refs_2_), channel_id=1, source_target_pairs={{0,4},{1,29},{2,6},{3,31},{4,8},{5,1},{6,10},{7,3},{8,12},{9,5},{1... | collective-permute-start | bytes 1228808 | tf_op jit(solution)/shard_map/ppermute | solution.py:271
  31.4 3.9 %late.2 = (f32[192,512]{1,0:T(8,128)}, s16[208,512]{1,0:T(8,128)(2,1)}, s16[208,512]{1,0:T(8,128)(2,1)}, s16[208,512]{1,0:T(8,128)(2,1)}, s16[208,512]{1,0:T(8,128)(2,1)}, /*index=5*/s16[208,512]{1,0:T(8,128)(2,1)}) custom-call(bf16[768,6144]{1,0:T(8,128)(2,1)} %bitcast.15, bf16[768,512]{1,0:T(8,128)(2,1)} %bitcast.21, s16[400,512]{1,0:T(8,128)(2,1)} %copy-done.3), custom_call_target="tpu_custom_call" | custom-call | flops 2717908992 | bytes 2949120 | tf_op jit(solution)/shard_map/late/pallas_call | solution.py:167
  35.3 1.7 %collective-permute-start.5 = (s16[208,512]{1,0:T(8,128)(2,1)}, s16[208,512]{1,0:T(8,128)(2,1)S(1)}, u32[]{:S(2)}, u32[]{:S(2)}) collective-permute-start(s16[208,512]{1,0:T(8,128)(2,1)} %get-tuple-element.38), channel_id=1, source_target_pairs={{0,1},{1,0},{2,3},{3,2},{4,5},{5,4},{6,7},{7,6},{8,9},{9,8},{10,11... | collective-permute-start | bytes 638984 | tf_op jit(solution)/shard_map/ppermute | solution.py:271
  38.3 1.1 %collective-permute-start.18 = (s16[400,512]{1,0:T(8,128)(2,1)S(1)}, s16[400,512]{1,0:T(8,128)(2,1)S(1)}, u32[]{:S(2)}, u32[]{:S(2)}) collective-permute-start(s16[400,512]{1,0:T(8,128)(2,1)S(1)} %hop3.3), channel_id=1, source_target_pairs={{0,4},{1,29},{2,6},{3,31},{4,8},{5,1},{6,10},{7,3},{8,12},{9,5},{1... | collective-permute-start | bytes 1228808 | tf_op jit(solution)/shard_map/ppermute | solution.py:271
  39.7 0.4 collective-permute-start.10
  40.1 1.2 %collective-permute-start.3 = (s16[208,512]{1,0:T(8,128)(2,1)}, s16[208,512]{1,0:T(8,128)(2,1)S(1)}, u32[]{:S(2)}, u32[]{:S(2)}) collective-permute-start(s16[208,512]{1,0:T(8,128)(2,1)} %get-tuple-element.35), channel_id=1, source_target_pairs={{0,1},{1,0},{2,3},{3,2},{4,5},{5,4},{6,7},{7,6},{8,9},{9,8},{10,11... | collective-permute-start | bytes 638984 | tf_op jit(solution)/shard_map/ppermute | solution.py:271
  41.3 1.4 %collective-permute-start.11 = (s16[208,512]{1,0:T(8,128)(2,1)S(1)}, s16[208,512]{1,0:T(8,128)(2,1)S(1)}, u32[]{:S(2)}, u32[]{:S(2)}) collective-permute-start(s16[208,512]{1,0:T(8,128)(2,1)S(1)} %own.1.rest_0_), channel_id=1, source_target_pairs={{0,2},{1,3},{2,0},{3,1},{4,6},{5,7},{6,4},{7,5},{8,10},{9,11},{10,... | collective-permute-start | bytes 638984 | tf_op jit(solution)/shard_map/ppermute | solution.py:271
  42.7 2.7 %collective-permute-done.18.arrived = s16[400,512]{1,0:T(8,128)(2,1)S(1)} collective-permute-done((s16[400,512]{1,0:T(8,128)(2,1)S(1)}, s16[400,512]{1,0:T(8,128)(2,1)S(1)}, u32[]{:S(2)}, u32[]{:S(2)}) %collective-permute-start.18) | collective-permute-done | bytes 409632 | tf_op jit(solution)/shard_map/ppermute | solution.py:271
  45.7 3.1 %collective-permute-start.19 = (s16[400,512]{1,0:T(8,128)(2,1)S(1)}, s16[400,512]{1,0:T(8,128)(2,1)S(1)}, u32[]{:S(2)}, u32[]{:S(2)}) collective-permute-start(s16[400,512]{1,0:T(8,128)(2,1)S(1)} %hop4.3), channel_id=1, source_target_pairs={{0,6},{1,31},{2,4},{3,29},{4,10},{5,3},{6,8},{7,1},{8,14},{9,7},{1... | collective-permute-start | bytes 1228808 | tf_op jit(solution)/shard_map/ppermute | solution.py:271
  48.8 1.0 %collective-permute-done.10.arrived = s16[400,512]{1,0:T(8,128)(2,1)S(1)} collective-permute-done((s16[400,512]{1,0:T(8,128)(2,1)S(1)}, s16[400,512]{1,0:T(8,128)(2,1)S(1)}, u32[]{:S(2)}, u32[]{:S(2)}) %collective-permute-start.10) | collective-permute-done | bytes 409632 | tf_op jit(solution)/shard_map/ppermute | solution.py:271
  50.1 2.1 %collective-permute-start.12 = (s16[400,512]{1,0:T(8,128)(2,1)S(1)}, s16[400,512]{1,0:T(8,128)(2,1)S(1)}, u32[]{:S(2)}, u32[]{:S(2)}) collective-permute-start(s16[400,512]{1,0:T(8,128)(2,1)S(1)} %hop4.2), channel_id=1, source_target_pairs={{0,4},{1,29},{2,6},{3,31},{4,8},{5,1},{6,10},{7,3},{8,12},{9,5},{1... | collective-permute-start | bytes 1228808 | tf_op jit(solution)/shard_map/ppermute | solution.py:271
  52.1 0.6 collective-permute-start.20
  53.8 3.3 %collective-permute-done.19.aslant = s16[400,512]{1,0:T(8,128)(2,1)S(1)} collective-permute-done((s16[400,512]{1,0:T(8,128)(2,1)S(1)}, s16[400,512]{1,0:T(8,128)(2,1)S(1)}, u32[]{:S(2)}, u32[]{:S(2)}) %collective-permute-start.19) | collective-permute-done | bytes 409632 | tf_op jit(solution)/shard_map/ppermute | solution.py:271
  57.1 2.5 %collective-permute-done.12.straight = s16[400,512]{1,0:T(8,128)(2,1)S(1)} collective-permute-done((s16[400,512]{1,0:T(8,128)(2,1)S(1)}, s16[400,512]{1,0:T(8,128)(2,1)S(1)}, u32[]{:S(2)}, u32[]{:S(2)}) %collective-permute-start.12) | collective-permute-done | bytes 409632 | tf_op jit(solution)/shard_map/ppermute | solution.py:271
  59.6 0.7 meet.1
  60.3 4.0 %collective-permute-start.21 = (s16[208,512]{1,0:T(8,128)(2,1)S(1)}, s16[208,512]{1,0:T(8,128)(2,1)S(1)}, u32[]{:S(2)}, u32[]{:S(2)}) collective-permute-start(s16[208,512]{1,0:T(8,128)(2,1)S(1)} %get-tuple-element.51), channel_id=1, source_target_pairs={{0,1},{1,0},{2,3},{3,2},{4,5},{5,4},{6,7},{7,6},{8,9},{9,8},{10,11... | collective-permute-start | bytes 638984 | tf_op jit(solution)/shard_map/ppermute | solution.py:271
  64.2 1.1 %collective-permute-done.21.other = s16[208,512]{1,0:T(8,128)(2,1)S(1)} collective-permute-done((s16[208,512]{1,0:T(8,128)(2,1)S(1)}, s16[208,512]{1,0:T(8,128)(2,1)S(1)}, u32[]{:S(2)}, u32[]{:S(2)}) %collective-permute-start.21) | collective-permute-done | bytes 213024 | tf_op jit(solution)/shard_map/ppermute | solution.py:271
  65.3 3.1 %pick.1 = (f32[192,512]{1,0:T(8,128)}, f32[8,48,128]{2,1,0:T(8,128)S(1)}) custom-call(f32[192,512]{1,0:T(8,128)S(1)} %get-tuple-element.50.kept, s16[208,512]{1,0:T(8,128)(2,1)S(1)} %collective-permute-done.21.other, f32[192,512]{1,0:T(8,128)S(1)} %bitcast.8, s32[24,128]{1,0:T(8,128)S(1)} %bitcast_select_fusion.places, bf16[2,192,192]{2,1,0:T(8,128)(2,1)S(1)} %copy-done.17, ...), custom_call_target="tpu_custom_call" | custom-call | tf_op jit(solution)/shard_map/pick/pallas_call | solution.py:397
  68.5 13.7 %all_to_all.5.gathered = f32[8,48,128]{2,1,0:T(8,128)S(1)} all-to-all(f32[8,48,128]{2,1,0:T(8,128)S(1)} %get-tuple-element.53), channel_id=1, replica_groups=mesh['rep'=8,'fsdp'=32] {'rep'}, dimensions={0} | all-to-all | bytes 393216 | tf_op jit(solution)/shard_map/all_to_all | solution.py:407
  82.2 3.1 %decode.1 = f32[192,512]{1,0:T(8,128)} custom-call(f32[8,48,128]{2,1,0:T(8,128)S(1)} %all_to_all.5.gathered, bf16[2,192,192]{2,1,0:T(8,128)(2,1)S(1)} %copy-done.6, bf16[2,256,256]{2,1,0:T(8,128)(2,1)S(1)} %copy-done.4), custom_call_target="tpu_custom_call" | custom-call | tf_op jit(solution)/shard_map/decode/pallas_call | solution.py:408
  (75 shorter events, 3.4 us)
Async XLA Ops:
  4.1 6.9 %collective-permute-start = (s16[3,208,512]{2,1,0:T(8,128)(2,1)}, s16[3,208,512]{2,1,0:T(8,128)(2,1)S(1)}, u32[]{:S(2)}, u32[]{:S(2)}) collective-permute-start(s16[3,208,512]{2,1,0:T(8,128)(2,1)} %get-tuple-element.29.refs_2_), channel_id=1, source_target_pairs={{0,1},{1,0},{2,3},{3,2},{4,5},{5,4},{6,7},{7,6},{8,9},{9,8},{10,11... | collective-permute-start | bytes 1916936 | tf_op jit(solution)/shard_map/ppermute | solution.py:271
  10.9 8.1 %collective-permute-start.1 = (s16[3,208,512]{2,1,0:T(8,128)(2,1)}, s16[3,208,512]{2,1,0:T(8,128)(2,1)S(1)}, u32[]{:S(2)}, u32[]{:S(2)}) collective-permute-start(s16[3,208,512]{2,1,0:T(8,128)(2,1)} %get-tuple-element.33), channel_id=1, source_target_pairs={{0,1},{1,0},{2,3},{3,2},{4,5},{5,4},{6,7},{7,6},{8,9},{9,8},{10,11... | collective-permute-start | bytes 1916936 | tf_op jit(solution)/shard_map/ppermute | solution.py:271
  11.2 12.7 %collective-permute-start.8 = (s16[400,256]{1,0:T(8,128)(2,1)S(1)}, s16[400,256]{1,0:T(8,128)(2,1)S(1)}, u32[]{:S(2)}, u32[]{:S(2)}) collective-permute-start(s16[400,256]{1,0:T(8,128)(2,1)S(1)} %hop1.2.refs_2_), channel_id=1, source_target_pairs={{0,4},{1,29},{2,6},{3,31},{4,8},{5,1},{6,10},{7,3},{8,12},{9,5},{1... | collective-permute-start | bytes 614408 | tf_op jit(solution)/shard_map/ppermute | solution.py:271
  19.1 10.7 %collective-permute-start.2 = (s16[400,256]{1,0:T(8,128)(2,1)S(1)}, s16[400,256]{1,0:T(8,128)(2,1)S(1)}, u32[]{:S(2)}, u32[]{:S(2)}) collective-permute-start(s16[400,256]{1,0:T(8,128)(2,1)S(1)} %hop1.3), channel_id=1, source_target_pairs={{0,4},{1,29},{2,6},{3,31},{4,8},{5,1},{6,10},{7,3},{8,12},{9,5},{1... | collective-permute-start | bytes 614408 | tf_op jit(solution)/shard_map/ppermute | solution.py:271
  24.3 13.1 %collective-permute-start.17 = (s16[400,512]{1,0:T(8,128)(2,1)S(1)}, s16[400,512]{1,0:T(8,128)(2,1)S(1)}, u32[]{:S(2)}, u32[]{:S(2)}) collective-permute-start(s16[400,512]{1,0:T(8,128)(2,1)S(1)} %hop2.3.refs_2_), channel_id=1, source_target_pairs={{0,4},{1,29},{2,6},{3,31},{4,8},{5,1},{6,10},{7,3},{8,12},{9,5},{1... | collective-permute-start | bytes 1228808 | tf_op jit(solution)/shard_map/ppermute | solution.py:271
  29.1 6.2 %collective-permute-start.9 = (s16[208,512]{1,0:T(8,128)(2,1)}, s16[208,512]{1,0:T(8,128)(2,1)S(1)}, u32[]{:S(2)}, u32[]{:S(2)}) collective-permute-start(s16[208,512]{1,0:T(8,128)(2,1)} %get-tuple-element.41), channel_id=1, source_target_pairs={{0,1},{1,0},{2,3},{3,2},{4,5},{5,4},{6,7},{7,6},{8,9},{9,8},{10,11... | collective-permute-start | bytes 638984 | tf_op jit(solution)/shard_map/ppermute | solution.py:271
  29.2 7.8 %collective-permute-start.15 = (s16[208,512]{1,0:T(8,128)(2,1)}, s16[208,512]{1,0:T(8,128)(2,1)S(1)}, u32[]{:S(2)}, u32[]{:S(2)}) collective-permute-start(s16[208,512]{1,0:T(8,128)(2,1)} %get-tuple-element.46), channel_id=1, source_target_pairs={{0,1},{1,0},{2,3},{3,2},{4,5},{5,4},{6,7},{7,6},{8,9},{9,8},{10,11... | collective-permute-start | bytes 638984 | tf_op jit(solution)/shard_map/ppermute | solution.py:271
  29.7 7.4 %collective-permute-start.16 = (s16[208,512]{1,0:T(8,128)(2,1)}, s16[208,512]{1,0:T(8,128)(2,1)S(1)}, u32[]{:S(2)}, u32[]{:S(2)}) collective-permute-start(s16[208,512]{1,0:T(8,128)(2,1)} %get-tuple-element.47), channel_id=1, source_target_pairs={{0,1},{1,0},{2,3},{3,2},{4,5},{5,4},{6,7},{7,6},{8,9},{9,8},{10,11... | collective-permute-start | bytes 638984 | tf_op jit(solution)/shard_map/ppermute | solution.py:271
  29.8 15.5 %copy-start.8 = (f32[384,512]{1,0:T(8,128)S(1)}, f32[384,512]{1,0:T(8,128)}, u32[]{:S(2)}) copy-start(f32[384,512]{1,0:T(8,128)} %get-tuple-element.42.keep) | copy-start | bytes 2359300
  30.3 19.4 %copy-start.7 = (f32[384,512]{1,0:T(8,128)S(1)}, f32[384,512]{1,0:T(8,128)}, u32[]{:S(2)}) copy-start(f32[384,512]{1,0:T(8,128)} %get-tuple-element.31.keep) | copy-start | bytes 2359300
  30.3 33.9 %copy-start.18 = (s32[1,3,8,128]{3,2,1,0:T(8,128)S(1)}, s32[1,3,8,128]{3,2,1,0:T(8,128)}, u32[]{:S(2)}) copy-start(s32[1,3,8,128]{3,2,1,0:T(8,128)} %param.12) | copy-start | bytes 36868
  30.3 35.0 %copy-start.4 = (bf16[2,256,256]{2,1,0:T(8,128)(2,1)S(1)}, bf16[2,256,256]{2,1,0:T(8,128)(2,1)}, u32[]{:S(2)}) copy-start(bf16[2,256,256]{2,1,0:T(8,128)(2,1)} %constant.12.clone.cols) | copy-start | bytes 786436
  30.3 35.0 %copy-start.6 = (bf16[2,192,192]{2,1,0:T(8,128)(2,1)S(1)}, bf16[2,192,192]{2,1,0:T(8,128)(2,1)}, u32[]{:S(2)}) copy-start(bf16[2,192,192]{2,1,0:T(8,128)(2,1)} %constant.11.clone.rows_t) | copy-start | bytes 442372
  30.3 35.0 %copy-start.15 = (f32[1,192,512]{2,1,0:T(8,128)S(1)}, f32[1,192,512]{2,1,0:T(8,128)}, u32[]{:S(2)}) copy-start(f32[1,192,512]{2,1,0:T(8,128)} %param.11) | copy-start | bytes 1179652
  30.4 35.0 %copy-start.16 = (bf16[2,256,256]{2,1,0:T(8,128)(2,1)S(1)}, bf16[2,256,256]{2,1,0:T(8,128)(2,1)}, u32[]{:S(2)}) copy-start(bf16[2,256,256]{2,1,0:T(8,128)(2,1)} %constant.13.clone.cols_t) | copy-start | bytes 786436
  30.4 35.0 %copy-start.17 = (bf16[2,192,192]{2,1,0:T(8,128)(2,1)S(1)}, bf16[2,192,192]{2,1,0:T(8,128)(2,1)}, u32[]{:S(2)}) copy-start(bf16[2,192,192]{2,1,0:T(8,128)(2,1)} %constant.10.clone.rows) | copy-start | bytes 442372
  30.4 8.9 %collective-permute-start.7 = (s16[400,512]{1,0:T(8,128)(2,1)S(1)}, s16[400,512]{1,0:T(8,128)(2,1)S(1)}, u32[]{:S(2)}, u32[]{:S(2)}) collective-permute-start(s16[400,512]{1,0:T(8,128)(2,1)S(1)} %hop2.2.refs_2_), channel_id=1, source_target_pairs={{0,4},{1,29},{2,6},{3,31},{4,8},{5,1},{6,10},{7,3},{8,12},{9,5},{1... | collective-permute-start | bytes 1228808 | tf_op jit(solution)/shard_map/ppermute | solution.py:271
  35.3 16.9 %copy-start.19 = (s16[208,512]{1,0:T(8,128)(2,1)S(1)}, s16[208,512]{1,0:T(8,128)(2,1)}, u32[]{:S(2)}) copy-start(s16[208,512]{1,0:T(8,128)(2,1)} %get-tuple-element.49) | copy-start | bytes 638980
  35.3 24.3 %copy-start.12 = (f32[192,512]{1,0:T(8,128)S(1)}, f32[192,512]{1,0:T(8,128)}, u32[]{:S(2)}) copy-start(f32[192,512]{1,0:T(8,128)} %get-tuple-element.48.keep) | copy-start | bytes 1179652
  35.3 3.0 %collective-permute-start.5 = (s16[208,512]{1,0:T(8,128)(2,1)}, s16[208,512]{1,0:T(8,128)(2,1)S(1)}, u32[]{:S(2)}, u32[]{:S(2)}) collective-permute-start(s16[208,512]{1,0:T(8,128)(2,1)} %get-tuple-element.38), channel_id=1, source_target_pairs={{0,1},{1,0},{2,3},{3,2},{4,5},{5,4},{6,7},{7,6},{8,9},{9,8},{10,11... | collective-permute-start | bytes 638984 | tf_op jit(solution)/shard_map/ppermute | solution.py:271
  37.0 2.4 %collective-permute-start.6 = (s16[208,512]{1,0:T(8,128)(2,1)}, s16[208,512]{1,0:T(8,128)(2,1)S(1)}, u32[]{:S(2)}, u32[]{:S(2)}) collective-permute-start(s16[208,512]{1,0:T(8,128)(2,1)} %get-tuple-element.39), channel_id=1, source_target_pairs={{0,1},{1,0},{2,3},{3,2},{4,5},{5,4},{6,7},{7,6},{8,9},{9,8},{10,11... | collective-permute-start | bytes 638984 | tf_op jit(solution)/shard_map/ppermute | solution.py:271
  37.1 4.2 %collective-permute-start.13 = (s16[208,512]{1,0:T(8,128)(2,1)}, s16[208,512]{1,0:T(8,128)(2,1)S(1)}, u32[]{:S(2)}, u32[]{:S(2)}) collective-permute-start(s16[208,512]{1,0:T(8,128)(2,1)} %get-tuple-element.43), channel_id=1, source_target_pairs={{0,1},{1,0},{2,3},{3,2},{4,5},{5,4},{6,7},{7,6},{8,9},{9,8},{10,11... | collective-permute-start | bytes 638984 | tf_op jit(solution)/shard_map/ppermute | solution.py:271
  37.5 3.8 %collective-permute-start.14 = (s16[208,512]{1,0:T(8,128)(2,1)S(1)}, s16[208,512]{1,0:T(8,128)(2,1)S(1)}, u32[]{:S(2)}, u32[]{:S(2)}) collective-permute-start(s16[208,512]{1,0:T(8,128)(2,1)S(1)} %copy-done.20), channel_id=1, source_target_pairs={{0,1},{1,0},{2,3},{3,2},{4,5},{5,4},{6,7},{7,6},{8,9},{9,8},{10,11... | collective-permute-start | bytes 638984 | tf_op jit(solution)/shard_map/ppermute | solution.py:271
  38.3 7.1 %collective-permute-start.18 = (s16[400,512]{1,0:T(8,128)(2,1)S(1)}, s16[400,512]{1,0:T(8,128)(2,1)S(1)}, u32[]{:S(2)}, u32[]{:S(2)}) collective-permute-start(s16[400,512]{1,0:T(8,128)(2,1)S(1)} %hop3.3), channel_id=1, source_target_pairs={{0,4},{1,29},{2,6},{3,31},{4,8},{5,1},{6,10},{7,3},{8,12},{9,5},{1... | collective-permute-start | bytes 1228808 | tf_op jit(solution)/shard_map/ppermute | solution.py:271
  39.7 10.1 %collective-permute-start.10 = (s16[400,512]{1,0:T(8,128)(2,1)S(1)}, s16[400,512]{1,0:T(8,128)(2,1)S(1)}, u32[]{:S(2)}, u32[]{:S(2)}) collective-permute-start(s16[400,512]{1,0:T(8,128)(2,1)S(1)} %hop3.2), channel_id=1, source_target_pairs={{0,4},{1,29},{2,6},{3,31},{4,8},{5,1},{6,10},{7,3},{8,12},{9,5},{1... | collective-permute-start | bytes 1228808 | tf_op jit(solution)/shard_map/ppermute | solution.py:271
  40.1 8.6 %collective-permute-start.3 = (s16[208,512]{1,0:T(8,128)(2,1)}, s16[208,512]{1,0:T(8,128)(2,1)S(1)}, u32[]{:S(2)}, u32[]{:S(2)}) collective-permute-start(s16[208,512]{1,0:T(8,128)(2,1)} %get-tuple-element.35), channel_id=1, source_target_pairs={{0,1},{1,0},{2,3},{3,2},{4,5},{5,4},{6,7},{7,6},{8,9},{9,8},{10,11... | collective-permute-start | bytes 638984 | tf_op jit(solution)/shard_map/ppermute | solution.py:271
  41.3 7.5 %collective-permute-start.4 = (s16[208,512]{1,0:T(8,128)(2,1)}, s16[208,512]{1,0:T(8,128)(2,1)S(1)}, u32[]{:S(2)}, u32[]{:S(2)}) collective-permute-start(s16[208,512]{1,0:T(8,128)(2,1)} %get-tuple-element.36), channel_id=1, source_target_pairs={{0,1},{1,0},{2,3},{3,2},{4,5},{5,4},{6,7},{7,6},{8,9},{9,8},{10,11... | collective-permute-start | bytes 638984 | tf_op jit(solution)/shard_map/ppermute | solution.py:271
  41.3 7.4 %collective-permute-start.11 = (s16[208,512]{1,0:T(8,128)(2,1)S(1)}, s16[208,512]{1,0:T(8,128)(2,1)S(1)}, u32[]{:S(2)}, u32[]{:S(2)}) collective-permute-start(s16[208,512]{1,0:T(8,128)(2,1)S(1)} %own.1.rest_0_), channel_id=1, source_target_pairs={{0,2},{1,3},{2,0},{3,1},{4,6},{5,7},{6,4},{7,5},{8,10},{9,11},{10,... | collective-permute-start | bytes 638984 | tf_op jit(solution)/shard_map/ppermute | solution.py:271
  45.7 11.4 %collective-permute-start.19 = (s16[400,512]{1,0:T(8,128)(2,1)S(1)}, s16[400,512]{1,0:T(8,128)(2,1)S(1)}, u32[]{:S(2)}, u32[]{:S(2)}) collective-permute-start(s16[400,512]{1,0:T(8,128)(2,1)S(1)} %hop4.3), channel_id=1, source_target_pairs={{0,6},{1,31},{2,4},{3,29},{4,10},{5,3},{6,8},{7,1},{8,14},{9,7},{1... | collective-permute-start | bytes 1228808 | tf_op jit(solution)/shard_map/ppermute | solution.py:271
  50.1 9.5 %collective-permute-start.12 = (s16[400,512]{1,0:T(8,128)(2,1)S(1)}, s16[400,512]{1,0:T(8,128)(2,1)S(1)}, u32[]{:S(2)}, u32[]{:S(2)}) collective-permute-start(s16[400,512]{1,0:T(8,128)(2,1)S(1)} %hop4.2), channel_id=1, source_target_pairs={{0,4},{1,29},{2,6},{3,31},{4,8},{5,1},{6,10},{7,3},{8,12},{9,5},{1... | collective-permute-start | bytes 1228808 | tf_op jit(solution)/shard_map/ppermute | solution.py:271
  52.1 1.7 %collective-permute-start.20 = (s16[208,512]{1,0:T(8,128)(2,1)S(1)}, s16[208,512]{1,0:T(8,128)(2,1)S(1)}, u32[]{:S(2)}, u32[]{:S(2)}) collective-permute-start(s16[208,512]{1,0:T(8,128)(2,1)S(1)} %copy-done.19), channel_id=1, source_target_pairs={{0,1},{1,0},{2,3},{3,2},{4,5},{5,4},{6,7},{7,6},{8,9},{9,8},{10,11... | collective-permute-start | bytes 638984 | tf_op jit(solution)/shard_map/ppermute | solution.py:271
  60.3 5.0 %collective-permute-start.21 = (s16[208,512]{1,0:T(8,128)(2,1)S(1)}, s16[208,512]{1,0:T(8,128)(2,1)S(1)}, u32[]{:S(2)}, u32[]{:S(2)}) collective-permute-start(s16[208,512]{1,0:T(8,128)(2,1)S(1)} %get-tuple-element.51), channel_id=1, source_target_pairs={{0,1},{1,0},{2,3},{3,2},{4,5},{5,4},{6,7},{7,6},{8,9},{9,8},{10,11... | collective-permute-start | bytes 638984 | tf_op jit(solution)/shard_map/ppermute | solution.py:271
  (11 other events, 67.5 us)

commit v5 on v4

--- a/solution.py
+++ b/solution.py
@@ -47,15 +47,19 @@
 
 def left_product(table, x):
     high, low = split(x)
-    return dot(table[0], high) + (dot(table[0], low) + dot(table[1], high))
+    height = table.shape[1]
+    both = dot(jnp.concatenate([table[0], table[1]], axis=0), high)
+    return both[:height] + (both[height:] + dot(table[0], low))
 
 
 def right_product(x, table):
     width = table.shape[-1]
+    height = x.shape[0]
     pieces = []
     for start in range(0, x.shape[1], width):
         high, low = split(x[:, start:start + width])
-        pieces.append(dot(high, table[0]) + (dot(low, table[0]) + dot(high, table[1])))
+        both = dot(jnp.concatenate([high, low], axis=0), table[0])
+        pieces.append(both[:height] + (both[height:] + dot(high, table[1])))
     return jnp.concatenate(pieces, axis=1)
 
 
@@ -98,112 +102,150 @@
     return lax.dot_general(left, right, (((0,), (0,)), ((), ())), preferred_element_type=F32)
 
 
-def blocks_in_turn(steps, swap, inputs, grads, blocks, whole, sems):
-    z, y, core = place()
-    target = 1 - y if swap else y
-
-    def load(n):
-        block = lax.rem(z + steps[n] * (1 - 2 * core) + RINGS, RINGS) * 2 + target
-        columns = pl.ds(pl.multiple_of(block * BOTH, BOTH), BOTH)
-        return pltpu.make_async_copy(inputs.at[:, columns], blocks.at[n], sems.at[n])
-
-    first = pltpu.make_async_copy(grads, whole, sems.at[len(steps)])
-    first.start()
-    load(0).start()
-    load(1).start()
-    first.wait()
-    for n in range(len(steps)):
-        load(n).wait()
-        if n + 2 < len(steps):
-            load(n + 2).start()
-        yield product(blocks[n], whole[...])
-
-
 EARLY = (4, -3)
 LATE = (-2, -1, 0)
 KEPT = (3, 2, 1)
 
 
-def early_kernel(swap, inputs, grads, _, keep4, away, blocks, whole, sems, both):
-    core = place()[2]
+def loads(steps, swap, inputs, blocks, sems):
+    z, y, core = place()
+    target = 1 - y if swap else y
+    copies = []
+    for n, step in enumerate(steps):
+        block = lax.rem(z + step * (1 - 2 * core) + RINGS, RINGS) * 2 + target
+        columns = pl.ds(pl.multiple_of(block * BOTH, BOTH), BOTH)
+        copies.append(pltpu.make_async_copy(inputs.at[:, columns], blocks.at[n], sems.at[n]))
+    return copies
+
+
+def early_part(core, blocks, grads, keep4, away, both, ready=None):
     half = keep4.shape[1]
-    turns = blocks_in_turn(EARLY, swap, inputs, grads, blocks, whole, sems)
-    both[...] = next(turns)
+    both[...] = product(blocks[0], grads[...])
     keep4[...] = both[:, pl.ds(pl.multiple_of(core * half, half), half)]
     other = both[:, pl.ds(pl.multiple_of((1 - core) * half, half), half)]
     encode(other[:ROWS], away.at[0, :, :half])
     encode(other[ROWS:], away.at[0, :, half:])
-    total = next(turns)
+    if ready is not None:
+        ready.wait()
+    total = product(blocks[1], grads[...])
     encode(total[:ROWS], away.at[1])
     encode(total[ROWS:], away.at[2])
 
 
-def late_kernel(swap, inputs, grads, _, keep0, *refs):
-    away, (blocks, whole, sems, both) = refs[:5], refs[5:]
+def first_kernel(inputs, grads, keep4, away, kept_grads, ahead, blocks, both, sems, ahead_sems, grad_sem):
+    whole = pltpu.make_async_copy(grads, kept_grads, grad_sem)
+    mine = loads(EARLY, True, inputs, blocks, sems)
+    more = loads(EARLY, False, inputs, ahead, ahead_sems)
+    whole.start()
+    mine[0].start()
+    mine[1].start()
+    whole.wait()
+    mine[0].wait()
+    for copy in more:
+        copy.start()
+    early_part(place()[2], blocks, kept_grads, keep4, away, both, mine[1])
+    for copy in more:
+        copy.wait()
+
+
+def early_kernel(inputs, grads, blocks, _, keep4, away, ahead, both, sems):
+    more = loads(KEPT, True, inputs, ahead, sems)
+    for copy in more:
+        copy.start()
+    early_part(place()[2], blocks, grads, keep4, away, both)
+    for copy in more:
+        copy.wait()
+
+
+def kept_kernel(then, inputs, grads, blocks, _, *refs):
+    keeps, (ahead, sums, out_sems, sems) = refs[:3], refs[3:]
+    more = loads(*then, inputs, ahead, sems)
+    for copy in more:
+        copy.start()
+    copies = []
+    for n, keep in enumerate(keeps):
+        sums[n] = product(blocks[n], grads[...])
+        copies.append(pltpu.make_async_copy(sums.at[n], keep, out_sems.at[n]))
+        copies[n].start()
+    for copy in copies + more:
+        copy.wait()
+
+
+def late_kernel(then, inputs, grads, blocks, _, keep0, *refs):
+    away, refs = refs[:5], refs[5:]
+    more = loads(*then, inputs, refs[0], refs[2]) if then else []
+    both = refs[1] if then else refs[0]
+    for copy in more:
+        copy.start()
     core = place()[2]
-    turns = blocks_in_turn(LATE, swap, inputs, grads, blocks, whole, sems)
     for n in range(2):
-        total = next(turns)
+        total = product(blocks[n], grads[...])
         encode(total[:ROWS], away[2 * n])
         encode(total[ROWS:], away[2 * n + 1])
-    both[...] = next(turns)
+    both[...] = product(blocks[2], grads[...])
     keep0[...] = both[pl.ds(pl.multiple_of(core * ROWS, ROWS), ROWS), :]
     encode(both[pl.ds(pl.multiple_of((1 - core) * ROWS, ROWS), ROWS), :], away[4])
-
-
-def kept_kernel(swap, inputs, grads, _, keep3, keep2, keep1, blocks, whole, sems, sums, out_sems):
-    keeps = (keep3, keep2, keep1)
-    copies = []
-    for n, total in enumerate(blocks_in_turn(KEPT, swap, inputs, grads, blocks, whole, sems)):
-        sums[n] = total
-        copies.append(pltpu.make_async_copy(sums.at[n], keeps[n], out_sems.at[n]))
-        copies[n].start()
-    for copy in copies:
+    for copy in more:
         copy.wait()
 
 
-def partial_sums(kernel, swap, inputs, grads, after, steps, outs, out_spec, scratch, name):
-    tokens, breadth = grads.shape
+def partial_sums(kernel, args, outs, scratch, steps, name):
+    tokens, breadth = args[1][0].shape
     return pl.pallas_call(
-        lambda *refs: kernel(swap, *refs),
-        in_specs=[pl.BlockSpec(memory_space=pl.ANY)] * 3,
-        out_specs=[out_spec] * len(outs),
-        out_shape=[jax.ShapeDtypeStruct(*out) for out in outs],
-        scratch_shapes=[
-            pltpu.VMEM((steps, tokens, BOTH), BF),
-            pltpu.VMEM((tokens, breadth), BF),
-            pltpu.SemaphoreType.DMA((steps + 1,)),
-            *scratch,
-        ],
-        compiler_params=pltpu.CompilerParams(vmem_limit_bytes=56 << 20),
+        kernel,
+        in_specs=[pl.BlockSpec(memory_space=space) for _, space in args],
+        out_specs=[pl.BlockSpec(memory_space=space) for _, _, space in outs],
+        out_shape=[jax.ShapeDtypeStruct(shape, kind) for shape, kind, _ in outs],
+        scratch_shapes=scratch,
+        compiler_params=pltpu.CompilerParams(vmem_limit_bytes=46 << 20),
         cost_estimate=pl.CostEstimate(
             flops=steps * 6 * BOTH * tokens * breadth,
             bytes_accessed=steps * (2 * BOTH * tokens + 2 * BOTH * breadth),
             transcendentals=0,
         ),
         name=name,
-    )(inputs, grads, after)
-
-
-def early_sums(swap, inputs, grads, after):
-    breadth = grads.shape[1]
-    outs = [((BOTH, breadth // 2), F32), ((3, ROWS + HEAD, breadth), I16)]
-    return partial_sums(early_kernel, swap, inputs, grads, after, len(EARLY), outs,
-                        pl.BlockSpec(memory_space=pltpu.VMEM), [pltpu.VMEM((BOTH, breadth), F32)], "early")
-
-
-def late_sums(swap, inputs, grads, after):
-    breadth = grads.shape[1]
-    outs = [((ROWS, breadth), F32)] + [((ROWS + HEAD, breadth), I16)] * 5
-    return partial_sums(late_kernel, swap, inputs, grads, after, len(LATE), outs,
-                        pl.BlockSpec(memory_space=pltpu.VMEM), [pltpu.VMEM((BOTH, breadth), F32)], "late")
-
-
-def kept_sums(swap, inputs, grads, after):
-    breadth = grads.shape[1]
-    return partial_sums(kept_kernel, swap, inputs, grads, after, len(KEPT), [((BOTH, breadth), F32)] * 3,
-                        pl.BlockSpec(memory_space=pl.ANY),
-                        [pltpu.VMEM((3, BOTH, breadth), F32), pltpu.SemaphoreType.DMA((3,))], "kept")
+    )(*(array for array, _ in args))
+
+
+def all_sums(inputs, grads):
+    tokens, breadth = grads.shape
+    vmem = pltpu.VMEM
+    tall, short = (BOTH, breadth), (ROWS + HEAD, breadth)
+
+    def fetched(steps):
+        return ((len(steps), tokens, BOTH), BF, vmem)
+
+    def sems(steps):
+        return pltpu.SemaphoreType.DMA((len(steps),))
+
+    early = [((BOTH, breadth // 2), F32, vmem), ((3, *short), I16, vmem)]
+    kept = [(tall, F32, pl.ANY)] * 3
+    late = [((ROWS, breadth), F32, vmem)] + [(short, I16, vmem)] * 5
+    both = vmem(tall, F32)
+
+    def args(blocks, behind):
+        return (inputs, pl.ANY), (held, vmem), (blocks, vmem), (behind, pl.ANY)
+
+    keep4, away, held, ahead = partial_sums(
+        first_kernel, ((inputs, pl.ANY), (grads, pl.ANY)), early + [(grads.shape, BF, vmem), fetched(EARLY)],
+        [vmem((len(EARLY), tokens, BOTH), BF), both, sems(EARLY), sems(EARLY), pltpu.SemaphoreType.DMA], 3, "early")
+    behind = yield keep4, away
+    keep4, away, ahead = partial_sums(
+        early_kernel, args(ahead, behind), early + [fetched(KEPT)], [both, sems(KEPT)], 2, "early")
+    behind = yield keep4, away
+    sums = [vmem((3, *tall), F32), sems(KEPT)]
+    *keeps, ahead = partial_sums(
+        lambda *refs: kept_kernel((KEPT, False), *refs), args(ahead, behind), kept + [fetched(KEPT)], sums + [sems(KEPT)], 3, "kept")
+    behind = yield keeps
+    *keeps, ahead = partial_sums(
+        lambda *refs: kept_kernel((LATE, True), *refs), args(ahead, behind), kept + [fetched(LATE)], sums + [sems(LATE)], 3, "kept")
+    behind = yield keeps
+    keep0, *away, ahead = partial_sums(
+        lambda *refs: late_kernel((LATE, False), *refs), args(ahead, behind), late + [fetched(LATE)], [both, sems(LATE)], 3, "late")
+    behind = yield keep0, away
+    keep0, *away = partial_sums(
+        lambda *refs: late_kernel(None, *refs), args(ahead, behind), late, [both], 3, "late")
+    yield keep0, away
 
 
 ANYWHERE = "any"
@@ -287,19 +329,20 @@
             (keep, *others, arrived, after), (None, *cuts, None, ANYWHERE),
             [((tall, breadth), I16)], "hop%d" % step, scratch)[0]
 
-    keep4_a, away = early_sums(True, inputs, grads, inputs)
+    sums = all_sums(inputs, grads)
+    keep4_a, away = next(sums)
     early_a = send(away, WITHIN)
-    keep4_b, away = early_sums(False, inputs, grads, away)
+    keep4_b, away = sums.send(away)
     early_b = send(away, WITHIN)
     ring_a = first_hop(keep4_a, early_a)
     ring_b = first_hop(keep4_b, early_b)
-    kept_a = kept_sums(True, inputs, grads, ring_a)
-    kept_b = kept_sums(False, inputs, grads, kept_a[0])
+    kept_a = sums.send(ring_a)
+    kept_b = sums.send(kept_a[0])
     ring_a = later_hop(2, kept_a[0], early_a, None, send(ring_a, ALONG), kept_a[0])
     ring_b = later_hop(2, kept_b[0], early_b, None, send(ring_b, ALONG), kept_b[0])
-    keep0_a, *away = late_sums(True, inputs, grads, ring_a)
+    keep0_a, away = sums.send(ring_a)
     late_a = [send(part, WITHIN) for part in away]
-    keep0_b, *away = late_sums(False, inputs, grads, ring_b)
+    keep0_b, away = sums.send(ring_b)
     late_b = [send(part, WITHIN) for part in away]
     own_a = call_local(own_kernel, (keep0_a, late_a[4]), (None, None), [((short, breadth), I16)], "own")[0]
     beside = send(own_a, BESIDE)
@@ -342,7 +385,8 @@
             row_hot = jnp.where(numbers[:CH] == spread(row_code, CH), one, none)
             block = coef[i * CH:(i + 1) * CH, h * group * CH:(h + 1) * group * CH]
             high, low = split(block)
-            chosen = dot(high, col_hot) + dot(low, col_hot)
+            chosen = dot(jnp.concatenate([high, low], axis=0), col_hot)
+            chosen = chosen[:CH] + chosen[CH:]
             value = jnp.sum(chosen * row_hot.astype(F32), axis=0, keepdims=True)
             for n in range(group):
                 for r in range(payload.shape[0]):
@@ -370,13 +414,13 @@
             highs, lows, hots = [], [], []
             for r in range(reps):
                 high, low, row_code, col_code = (spread(part[t:t + 1, :], CH) for part in parts[r])
-                in_row = numbers == row_code
-                highs.append(jnp.where(in_row, high, none))
-                lows.append(jnp.where(in_row, low, none))
-                hots.append(jnp.where(numbers == col_code, one, none))
+                in_col = numbers == col_code
+                highs.append(jnp.where(in_col, high, none))
+                lows.append(jnp.where(in_col, low, none))
+                hots.append(jnp.where(numbers == row_code, one, none))
             both = jnp.concatenate([jnp.concatenate(highs, axis=1), jnp.concatenate(lows, axis=1)], axis=0)
-            out = dot_nt(both, jnp.concatenate(hots, axis=1))
-            blocks.append(out[:CH] + out[CH:])
+            out = dot_nt(jnp.concatenate(hots, axis=1), both)
+            blocks.append(out[:, :CH] + out[:, CH:])
         i, j = (2 * pair) // tile_cols, (2 * pair) % tile_cols
         total[i * CH:(i + 1) * CH, j * CH:(j + 2) * CH] = jnp.concatenate(blocks, axis=1)
     decoded = right_product(left_product(rows_t, total[...]), cols)

time: 85.6 us -> 82.6 us (0.965)
  Pallas kernels: 32 us -> 21.7 us
  waiting for transfers between devices: 11.2 us -> 16.2 us
  local copies, waits for them, and re-layouts: 0.11 us -> 1.16 us
  blocking collectives: 13.7 us -> 14.6 us
    pallas_call x6, Pallas kernels: 22.4 us -> 12.1 us  [partial_sums(): pl.pallas_call(kernel, in_specs=[pl.BlockSpec(memory_space=space) for _,...]
    ppermute x22, waiting for transfers between devices: 11.2 us -> 16.2 us  [send(): return lax.ppermute(array, 'fsdp', pairs)]
    unnamed x42 -> x14, local copies, waits for them, and re-layouts: 0.11 us -> 1.16 us
    all_to_all x1, blocking collectives: 13.7 us -> 14.6 us  [body(): gathered = lax.all_to_all(payload, 'rep', 0, 0)]
  transfers between devices with their start and end apart: 22 -> 22, of which waited for: 7 -> 6; matrix products, arithmetic and copies ran while one was open for 0% -> 0% of each run, Pallas kernels for 25% -> 15%
where the time goes in v5:
time: 82.6 us; the launch traced here: 82.3 us
  starting transfers between devices  27.1 us (33%)
  Pallas kernels  21.7 us (26%)
  waiting for transfers between devices  16.2 us (20%)
  blocking collectives  14.6 us (18%)
  between operations  1.51 us (2%)
  local copies, waits for them, and re-layouts  1.16 us (1%)
    ppermute x22, starting transfers between devices, send(): return lax.ppermute(array, 'fsdp', pairs)  27.1 us
    ppermute x22, waiting for transfers between devices, send(): return lax.ppermute(array, 'fsdp', pairs)  16.2 us
    all_to_all x1, blocking collectives, body(): gathered = lax.all_to_all(payload, 'rep', 0, 0)  14.6 us
    pallas_call x6, Pallas kernels, partial_sums(): pl.pallas_call(kernel, in_specs=[pl.BlockSpec(memory_space=space) for _,...  12.1 us
    pallas_call x1, Pallas kernels, body(): pl.pallas_call(decode_kernel, out_shape=jax.ShapeDtypeStruct((height, bre...  3.66 us
    pallas_call x10, Pallas kernels, call_local(): pl.pallas_call(kernel, grid=(1,), in_specs=[spec(arg, cut) for arg, cut i...  3.26 us
    pallas_call x1, Pallas kernels, body(): pl.pallas_call(pick_kernel, out_shape=[jax.ShapeDtypeStruct((height, brea...  2.67 us
  transfers between devices with their start and end apart: 22, of which 6 were waited for; matrix products, arithmetic and copies ran while one was open for 0% of the time, Pallas kernels for 15%

profile of v5, /device:TPU:1, one launch (start us, length us, event | category | flops | bytes accessed | tf_op | source)
XLA Modules:
  0.0 82.3 jit_solution(11675694253199664584)
XLA Ops:
  0.6 1.1 %copy-done.1 = bf16[1,768,512]{2,1,0:T(8,128)(2,1)S(1)} copy-done((bf16[1,768,512]{2,1,0:T(8,128)(2,1)S(1)}, bf16[1,768,512]{2,1,0:T(8,128)(2,1)}, u32[]{:S(2)}) %copy-start.1) | copy-done | bytes 786456
  1.8 2.5 %early.2 = (f32[384,256]{1,0:T(8,128)S(1)}, s16[3,208,512]{2,1,0:T(8,128)(2,1)S(1)}, bf16[768,512]{1,0:T(8,128)(2,1)S(1)}, bf16[2,768,384]{2,1,0:T(8,128)(2,1)S(1)}) custom-call(bf16[768,6144]{1,0:T(8,128)(2,1)} %bitcast.10, bf16[768,512]{1,0:T(8,128)(2,1)S(1)} %bitcast.8), custom_call_target="tpu_custom_call" | custom-call | flops 2717908992 | bytes 2949120 | tf_op jit(solution)/shard_map/early/pallas_call | solution.py:194
  4.2 3.3 %collective-permute-start = (s16[3,208,512]{2,1,0:T(8,128)(2,1)S(1)}, s16[3,208,512]{2,1,0:T(8,128)(2,1)S(1)}, u32[]{:S(2)}, u32[]{:S(2)}) collective-permute-start(s16[3,208,512]{2,1,0:T(8,128)(2,1)S(1)} %get-tuple-element.36._), channel_id=1, source_target_pairs={{0,1},{1,0},{2,3},{3,2},{4,5},{5,4},{6,7},{7,6},{8,9},{9,8},{10,11... | collective-permute-start | bytes 1916936 | tf_op jit(solution)/shard_map/ppermute | solution.py:313
  7.6 2.2 %early.3 = (f32[384,256]{1,0:T(8,128)S(1)}, s16[3,208,512]{2,1,0:T(8,128)(2,1)S(1)}, bf16[3,768,384]{2,1,0:T(8,128)(2,1)S(1)}) custom-call(bf16[768,6144]{1,0:T(8,128)(2,1)} %bitcast.11, bf16[768,512]{1,0:T(8,128)(2,1)S(1)} %get-tuple-element.34.grads.refs_1_, bf16[2,768,384]{2,1,0:T(8,128)(2,1)S(1)} %get-tuple-element.35.blocks, ...), custom_call_target="tpu_custom_call" | custom-call | flops 1811939328 | bytes 1966080 | tf_op jit(solution)/shard_map/early/pallas_call | solution.py:194
  10.0 3.9 %collective-permute-start.1 = (s16[400,256]{1,0:T(8,128)(2,1)S(1)}, s16[400,256]{1,0:T(8,128)(2,1)S(1)}, u32[]{:S(2)}, u32[]{:S(2)}) collective-permute-start(s16[400,256]{1,0:T(8,128)(2,1)S(1)} %hop1.2.refs_3_), channel_id=1, source_target_pairs={{0,4},{1,29},{2,6},{3,31},{4,8},{5,1},{6,10},{7,3},{8,12},{9,5},{1... | collective-permute-start | bytes 614408 | tf_op jit(solution)/shard_map/ppermute | solution.py:313
  14.1 1.9 %collective-permute-start.3 = (s16[400,256]{1,0:T(8,128)(2,1)S(1)}, s16[400,256]{1,0:T(8,128)(2,1)S(1)}, u32[]{:S(2)}, u32[]{:S(2)}) collective-permute-start(s16[400,256]{1,0:T(8,128)(2,1)S(1)} %hop1.3), channel_id=1, source_target_pairs={{0,4},{1,29},{2,6},{3,31},{4,8},{5,1},{6,10},{7,3},{8,12},{9,5},{1... | collective-permute-start | bytes 614408 | tf_op jit(solution)/shard_map/ppermute | solution.py:313
  16.0 1.7 %kept.2 = (f32[384,512]{1,0:T(8,128)S(1)}, f32[384,512]{1,0:T(8,128)S(1)}, f32[384,512]{1,0:T(8,128)S(1)}, bf16[3,768,384]{2,1,0:T(8,128)(2,1)S(1)}) custom-call(bf16[768,6144]{1,0:T(8,128)(2,1)} %bitcast.12, bf16[768,512]{1,0:T(8,128)(2,1)S(1)} %get-tuple-element.34.grads.refs_1_, bf16[3,768,384]{2,1,0:T(8,128)(2,1)S(1)} %get-tuple-element.37.refs_2_, ...), custom_call_target="tpu_custom_call" | custom-call | flops 2717908992 | bytes 2949120 | tf_op jit(solution)/shard_map/kept/pallas_call | solution.py:194
  17.7 1.7 %kept.3 = (f32[384,512]{1,0:T(8,128)S(1)}, f32[384,512]{1,0:T(8,128)S(1)}, f32[384,512]{1,0:T(8,128)S(1)}, bf16[3,768,384]{2,1,0:T(8,128)(2,1)S(1)}) custom-call(bf16[768,6144]{1,0:T(8,128)(2,1)} %bitcast.13, bf16[768,512]{1,0:T(8,128)(2,1)S(1)} %get-tuple-element.34.grads.refs_1_, bf16[3,768,384]{2,1,0:T(8,128)(2,1)S(1)} %get-tuple-element.39.refs_2_, ...), custom_call_target="tpu_custom_call" | custom-call | flops 2717908992 | bytes 2949120 | tf_op jit(solution)/shard_map/kept/pallas_call | solution.py:194
  19.5 0.5 hop2.2.refs_3_
  19.9 0.8 collective-permute-start.17
  20.8 0.5 hop2.3.refs_3_
  21.2 1.3 %collective-permute-start.8 = (s16[400,512]{1,0:T(8,128)(2,1)S(1)}, s16[400,512]{1,0:T(8,128)(2,1)S(1)}, u32[]{:S(2)}, u32[]{:S(2)}) collective-permute-start(s16[400,512]{1,0:T(8,128)(2,1)S(1)} %hop2.3.refs_3_), channel_id=1, source_target_pairs={{0,4},{1,29},{2,6},{3,31},{4,8},{5,1},{6,10},{7,3},{8,12},{9,5},{1... | collective-permute-start | bytes 1228808 | tf_op jit(solution)/shard_map/ppermute | solution.py:313
  22.5 2.7 %late.2 = (f32[192,512]{1,0:T(8,128)S(1)}, s16[208,512]{1,0:T(8,128)(2,1)S(1)}, s16[208,512]{1,0:T(8,128)(2,1)S(1)}, s16[208,512]{1,0:T(8,128)(2,1)S(1)}, s16[20...) custom-call(bf16[768,6144]{1,0:T(8,128)(2,1)} %bitcast.14, ...), custom_call_target="tpu_custom_call" | custom-call | flops 2717908992 | bytes 2949120 | tf_op jit(solution)/shard_map/late/pallas_call | solution.py:194
  25.3 0.5 collective-permute-start.15
  25.9 1.3 %late.3 = (f32[192,512]{1,0:T(8,128)S(1)}, s16[208,512]{1,0:T(8,128)(2,1)S(1)}, s16[208,512]{1,0:T(8,128)(2,1)S(1)}, s16[208,512]{1,0:T(8,128)(2,1)S(1)}, s16[20...) custom-call(bf16[768,6144]{1,0:T(8,128)(2,1)} %bitcast.15, bf16[768,512]{1,0:T(8,128)(2,1)S(1)} %get-tuple-element.34.grads.refs_1_, ...), custom_call_target="tpu_custom_call" | custom-call | flops 2717908992 | bytes 2949120 | tf_op jit(solution)/shard_map/late/pallas_call | solution.py:194
  27.3 0.5 collective-permute-start.6
  28.9 1.6 %collective-permute-start.18 = (s16[400,512]{1,0:T(8,128)(2,1)S(1)}, s16[400,512]{1,0:T(8,128)(2,1)S(1)}, u32[]{:S(2)}, u32[]{:S(2)}) collective-permute-start(s16[400,512]{1,0:T(8,128)(2,1)S(1)} %hop3.3), channel_id=1, source_target_pairs={{0,4},{1,29},{2,6},{3,31},{4,8},{5,1},{6,10},{7,3},{8,12},{9,5},{1... | collective-permute-start | bytes 1228808 | tf_op jit(solution)/shard_map/ppermute | solution.py:313
  30.5 1.1 %collective-permute-done.8.arrived = s16[400,512]{1,0:T(8,128)(2,1)S(1)} collective-permute-done((s16[400,512]{1,0:T(8,128)(2,1)S(1)}, s16[400,512]{1,0:T(8,128)(2,1)S(1)}, u32[]{:S(2)}, u32[]{:S(2)}) %collective-permute-start.8) | collective-permute-done | bytes 409632 | tf_op jit(solution)/shard_map/ppermute | solution.py:313
  31.8 1.7 %collective-permute-start.10 = (s16[400,512]{1,0:T(8,128)(2,1)S(1)}, s16[400,512]{1,0:T(8,128)(2,1)S(1)}, u32[]{:S(2)}, u32[]{:S(2)}) collective-permute-start(s16[400,512]{1,0:T(8,128)(2,1)S(1)} %hop3.2), channel_id=1, source_target_pairs={{0,4},{1,29},{2,6},{3,31},{4,8},{5,1},{6,10},{7,3},{8,12},{9,5},{1... | collective-permute-start | bytes 1228808 | tf_op jit(solution)/shard_map/ppermute | solution.py:313
  33.6 0.5 collective-permute-start.5
  34.1 1.3 %collective-permute-start.11 = (s16[208,512]{1,0:T(8,128)(2,1)S(1)}, s16[208,512]{1,0:T(8,128)(2,1)S(1)}, u32[]{:S(2)}, u32[]{:S(2)}) collective-permute-start(s16[208,512]{1,0:T(8,128)(2,1)S(1)} %own.1.rest_0_), channel_id=1, source_target_pairs={{0,2},{1,3},{2,0},{3,1},{4,6},{5,7},{6,4},{7,5},{8,10},{9,11},{10,... | collective-permute-start | bytes 638984 | tf_op jit(solution)/shard_map/ppermute | solution.py:313
  35.4 0.6 collective-permute-done.18.arrived
  36.4 3.5 %collective-permute-start.19 = (s16[400,512]{1,0:T(8,128)(2,1)S(1)}, s16[400,512]{1,0:T(8,128)(2,1)S(1)}, u32[]{:S(2)}, u32[]{:S(2)}) collective-permute-start(s16[400,512]{1,0:T(8,128)(2,1)S(1)} %hop4.3), channel_id=1, source_target_pairs={{0,6},{1,31},{2,4},{3,29},{4,10},{5,3},{6,8},{7,1},{8,14},{9,7},{1... | collective-permute-start | bytes 1228808 | tf_op jit(solution)/shard_map/ppermute | solution.py:313
  39.9 8.8 %collective-permute-done.11.rest_0_.beside = s16[208,512]{1,0:T(8,128)(2,1)S(1)} collective-permute-done((s16[208,512]{1,0:T(8,128)(2,1)S(1)}, s16[208,512]{1,0:T(8,128)(2,1)S(1)}, u32[]{:S(2)}, u32[]{:S(2)}) %collective-permute-start.11) | collective-permute-done | bytes 213024 | tf_op jit(solution)/shard_map/ppermute | solution.py:313
  49.1 1.8 %collective-permute-start.20 = (s16[208,512]{1,0:T(8,128)(2,1)S(1)}, s16[208,512]{1,0:T(8,128)(2,1)S(1)}, u32[]{:S(2)}, u32[]{:S(2)}) collective-permute-start(s16[208,512]{1,0:T(8,128)(2,1)S(1)} %get-tuple-element.61), channel_id=1, source_target_pairs={{0,1},{1,0},{2,3},{3,2},{4,5},{5,4},{6,7},{7,6},{8,9},{9,8},{10,11... | collective-permute-start | bytes 638984 | tf_op jit(solution)/shard_map/ppermute | solution.py:313
  52.0 4.2 %collective-permute-done.12.straight = s16[400,512]{1,0:T(8,128)(2,1)S(1)} collective-permute-done((s16[400,512]{1,0:T(8,128)(2,1)S(1)}, s16[400,512]{1,0:T(8,128)(2,1)S(1)}, u32[]{:S(2)}, u32[]{:S(2)}) %collective-permute-start.12) | collective-permute-done | bytes 409632 | tf_op jit(solution)/shard_map/ppermute | solution.py:313
  56.2 0.7 meet.1
  56.9 3.4 %collective-permute-start.21 = (s16[208,512]{1,0:T(8,128)(2,1)S(1)}, s16[208,512]{1,0:T(8,128)(2,1)S(1)}, u32[]{:S(2)}, u32[]{:S(2)}) collective-permute-start(s16[208,512]{1,0:T(8,128)(2,1)S(1)} %get-tuple-element.63), channel_id=1, source_target_pairs={{0,1},{1,0},{2,3},{3,2},{4,5},{5,4},{6,7},{7,6},{8,9},{9,8},{10,11... | collective-permute-start | bytes 638984 | tf_op jit(solution)/shard_map/ppermute | solution.py:313
  60.2 1.1 %collective-permute-done.21.other = s16[208,512]{1,0:T(8,128)(2,1)S(1)} collective-permute-done((s16[208,512]{1,0:T(8,128)(2,1)S(1)}, s16[208,512]{1,0:T(8,128)(2,1)S(1)}, u32[]{:S(2)}, u32[]{:S(2)}) %collective-permute-start.21) | collective-permute-done | bytes 213024 | tf_op jit(solution)/shard_map/ppermute | solution.py:313
  61.4 2.7 %pick.1 = (f32[192,512]{1,0:T(8,128)}, f32[8,48,128]{2,1,0:T(8,128)S(1)}) custom-call(f32[192,512]{1,0:T(8,128)S(1)} %get-tuple-element.62.kept, s16[208,512]{1,0:T(8,128)(2,1)S(1)} %collective-permute-done.21.other, f32[192,512]{1,0:T(8,128)S(1)} %bitcast.9, s32[24,128]{1,0:T(8,128)S(1)} %bitcast_select_fusion.places, bf16[2,192,192]{2,1,0:T(8,128)(2,1)S(1)} %copy-done.5, ...), custom_call_target="tpu_custom_call" | custom-call | tf_op jit(solution)/shard_map/pick/pallas_call | solution.py:441
  64.0 14.6 %all_to_all.5.gathered = f32[8,48,128]{2,1,0:T(8,128)S(1)} all-to-all(f32[8,48,128]{2,1,0:T(8,128)S(1)} %get-tuple-element.65), channel_id=1, replica_groups=mesh['rep'=8,'fsdp'=32] {'rep'}, dimensions={0} | all-to-all | bytes 393216 | tf_op jit(solution)/shard_map/all_to_all | solution.py:451
  78.7 3.7 %decode.1 = f32[192,512]{1,0:T(8,128)} custom-call(f32[8,48,128]{2,1,0:T(8,128)S(1)} %all_to_all.5.gathered, bf16[2,192,192]{2,1,0:T(8,128)(2,1)S(1)} %copy-done.2, bf16[2,256,256]{2,1,0:T(8,128)(2,1)S(1)} %copy-done), custom_call_target="tpu_custom_call" | custom-call | tf_op jit(solution)/shard_map/decode/pallas_call | solution.py:452
  (47 shorter events, 3.2 us)
Async XLA Ops:
  0.6 1.1 %copy-start.1 = (bf16[1,768,512]{2,1,0:T(8,128)(2,1)S(1)}, bf16[1,768,512]{2,1,0:T(8,128)(2,1)}, u32[]{:S(2)}) copy-start(bf16[1,768,512]{2,1,0:T(8,128)(2,1)} %param.10) | copy-start | bytes 2359300
  4.2 5.7 %collective-permute-start = (s16[3,208,512]{2,1,0:T(8,128)(2,1)S(1)}, s16[3,208,512]{2,1,0:T(8,128)(2,1)S(1)}, u32[]{:S(2)}, u32[]{:S(2)}) collective-permute-start(s16[3,208,512]{2,1,0:T(8,128)(2,1)S(1)} %get-tuple-element.36._), channel_id=1, source_target_pairs={{0,1},{1,0},{2,3},{3,2},{4,5},{5,4},{6,7},{7,6},{8,9},{9,8},{10,11... | collective-permute-start | bytes 1916936 | tf_op jit(solution)/shard_map/ppermute | solution.py:313
  9.8 4.2 %collective-permute-start.2 = (s16[3,208,512]{2,1,0:T(8,128)(2,1)S(1)}, s16[3,208,512]{2,1,0:T(8,128)(2,1)S(1)}, u32[]{:S(2)}, u32[]{:S(2)}) collective-permute-start(s16[3,208,512]{2,1,0:T(8,128)(2,1)S(1)} %get-tuple-element.45), channel_id=1, source_target_pairs={{0,1},{1,0},{2,3},{3,2},{4,5},{5,4},{6,7},{7,6},{8,9},{9,8},{10,11... | collective-permute-start | bytes 1916936 | tf_op jit(solution)/shard_map/ppermute | solution.py:313
  10.0 9.4 %collective-permute-start.1 = (s16[400,256]{1,0:T(8,128)(2,1)S(1)}, s16[400,256]{1,0:T(8,128)(2,1)S(1)}, u32[]{:S(2)}, u32[]{:S(2)}) collective-permute-start(s16[400,256]{1,0:T(8,128)(2,1)S(1)} %hop1.2.refs_3_), channel_id=1, source_target_pairs={{0,4},{1,29},{2,6},{3,31},{4,8},{5,1},{6,10},{7,3},{8,12},{9,5},{1... | collective-permute-start | bytes 614408 | tf_op jit(solution)/shard_map/ppermute | solution.py:313
  14.1 6.7 %collective-permute-start.3 = (s16[400,256]{1,0:T(8,128)(2,1)S(1)}, s16[400,256]{1,0:T(8,128)(2,1)S(1)}, u32[]{:S(2)}, u32[]{:S(2)}) collective-permute-start(s16[400,256]{1,0:T(8,128)(2,1)S(1)} %hop1.3), channel_id=1, source_target_pairs={{0,4},{1,29},{2,6},{3,31},{4,8},{5,1},{6,10},{7,3},{8,12},{9,5},{1... | collective-permute-start | bytes 614408 | tf_op jit(solution)/shard_map/ppermute | solution.py:313
  19.9 8.3 %collective-permute-start.17 = (s16[400,512]{1,0:T(8,128)(2,1)S(1)}, s16[400,512]{1,0:T(8,128)(2,1)S(1)}, u32[]{:S(2)}, u32[]{:S(2)}) collective-permute-start(s16[400,512]{1,0:T(8,128)(2,1)S(1)} %hop2.2.refs_3_), channel_id=1, source_target_pairs={{0,4},{1,29},{2,6},{3,31},{4,8},{5,1},{6,10},{7,3},{8,12},{9,5},{1... | collective-permute-start | bytes 1228808 | tf_op jit(solution)/shard_map/ppermute | solution.py:313
  21.2 10.3 %collective-permute-start.8 = (s16[400,512]{1,0:T(8,128)(2,1)S(1)}, s16[400,512]{1,0:T(8,128)(2,1)S(1)}, u32[]{:S(2)}, u32[]{:S(2)}) collective-permute-start(s16[400,512]{1,0:T(8,128)(2,1)S(1)} %hop2.3.refs_3_), channel_id=1, source_target_pairs={{0,4},{1,29},{2,6},{3,31},{4,8},{5,1},{6,10},{7,3},{8,12},{9,5},{1... | collective-permute-start | bytes 1228808 | tf_op jit(solution)/shard_map/ppermute | solution.py:313
  25.2 2.0 %collective-permute-start.9 = (s16[208,512]{1,0:T(8,128)(2,1)S(1)}, s16[208,512]{1,0:T(8,128)(2,1)S(1)}, u32[]{:S(2)}, u32[]{:S(2)}) collective-permute-start(s16[208,512]{1,0:T(8,128)(2,1)S(1)} %get-tuple-element.53), channel_id=1, source_target_pairs={{0,1},{1,0},{2,3},{3,2},{4,5},{5,4},{6,7},{7,6},{8,9},{9,8},{10,11... | collective-permute-start | bytes 638984 | tf_op jit(solution)/shard_map/ppermute | solution.py:313
  25.3 2.4 %collective-permute-start.15 = (s16[208,512]{1,0:T(8,128)(2,1)S(1)}, s16[208,512]{1,0:T(8,128)(2,1)S(1)}, u32[]{:S(2)}, u32[]{:S(2)}) collective-permute-start(s16[208,512]{1,0:T(8,128)(2,1)S(1)} %get-tuple-element.58), channel_id=1, source_target_pairs={{0,1},{1,0},{2,3},{3,2},{4,5},{5,4},{6,7},{7,6},{8,9},{9,8},{10,11... | collective-permute-start | bytes 638984 | tf_op jit(solution)/shard_map/ppermute | solution.py:313
  25.8 2.0 %collective-permute-start.16 = (s16[208,512]{1,0:T(8,128)(2,1)S(1)}, s16[208,512]{1,0:T(8,128)(2,1)S(1)}, u32[]{:S(2)}, u32[]{:S(2)}) collective-permute-start(s16[208,512]{1,0:T(8,128)(2,1)S(1)} %get-tuple-element.59), channel_id=1, source_target_pairs={{0,1},{1,0},{2,3},{3,2},{4,5},{5,4},{6,7},{7,6},{8,9},{9,8},{10,11... | collective-permute-start | bytes 638984 | tf_op jit(solution)/shard_map/ppermute | solution.py:313
  27.3 1.6 %collective-permute-start.6 = (s16[208,512]{1,0:T(8,128)(2,1)S(1)}, s16[208,512]{1,0:T(8,128)(2,1)S(1)}, u32[]{:S(2)}, u32[]{:S(2)}) collective-permute-start(s16[208,512]{1,0:T(8,128)(2,1)S(1)} %get-tuple-element.50), channel_id=1, source_target_pairs={{0,1},{1,0},{2,3},{3,2},{4,5},{5,4},{6,7},{7,6},{8,9},{9,8},{10,11... | collective-permute-start | bytes 638984 | tf_op jit(solution)/shard_map/ppermute | solution.py:313
  27.8 2.7 %collective-permute-start.7 = (s16[208,512]{1,0:T(8,128)(2,1)S(1)}, s16[208,512]{1,0:T(8,128)(2,1)S(1)}, u32[]{:S(2)}, u32[]{:S(2)}) collective-permute-start(s16[208,512]{1,0:T(8,128)(2,1)S(1)} %get-tuple-element.51), channel_id=1, source_target_pairs={{0,1},{1,0},{2,3},{3,2},{4,5},{5,4},{6,7},{7,6},{8,9},{9,8},{10,11... | collective-permute-start | bytes 638984 | tf_op jit(solution)/shard_map/ppermute | solution.py:313
  27.9 5.7 %collective-permute-start.13 = (s16[208,512]{1,0:T(8,128)(2,1)S(1)}, s16[208,512]{1,0:T(8,128)(2,1)S(1)}, u32[]{:S(2)}, u32[]{:S(2)}) collective-permute-start(s16[208,512]{1,0:T(8,128)(2,1)S(1)} %get-tuple-element.55), channel_id=1, source_target_pairs={{0,1},{1,0},{2,3},{3,2},{4,5},{5,4},{6,7},{7,6},{8,9},{9,8},{10,11... | collective-permute-start | bytes 638984 | tf_op jit(solution)/shard_map/ppermute | solution.py:313
  28.3 5.8 %collective-permute-start.14 = (s16[208,512]{1,0:T(8,128)(2,1)S(1)}, s16[208,512]{1,0:T(8,128)(2,1)S(1)}, u32[]{:S(2)}, u32[]{:S(2)}) collective-permute-start(s16[208,512]{1,0:T(8,128)(2,1)S(1)} %get-tuple-element.56), channel_id=1, source_target_pairs={{0,1},{1,0},{2,3},{3,2},{4,5},{5,4},{6,7},{7,6},{8,9},{9,8},{10,11... | collective-permute-start | bytes 638984 | tf_op jit(solution)/shard_map/ppermute | solution.py:313
  28.9 7.2 %collective-permute-start.18 = (s16[400,512]{1,0:T(8,128)(2,1)S(1)}, s16[400,512]{1,0:T(8,128)(2,1)S(1)}, u32[]{:S(2)}, u32[]{:S(2)}) collective-permute-start(s16[400,512]{1,0:T(8,128)(2,1)S(1)} %hop3.3), channel_id=1, source_target_pairs={{0,4},{1,29},{2,6},{3,31},{4,8},{5,1},{6,10},{7,3},{8,12},{9,5},{1... | collective-permute-start | bytes 1228808 | tf_op jit(solution)/shard_map/ppermute | solution.py:313
  31.8 16.8 %collective-permute-start.10 = (s16[400,512]{1,0:T(8,128)(2,1)S(1)}, s16[400,512]{1,0:T(8,128)(2,1)S(1)}, u32[]{:S(2)}, u32[]{:S(2)}) collective-permute-start(s16[400,512]{1,0:T(8,128)(2,1)S(1)} %hop3.2), channel_id=1, source_target_pairs={{0,4},{1,29},{2,6},{3,31},{4,8},{5,1},{6,10},{7,3},{8,12},{9,5},{1... | collective-permute-start | bytes 1228808 | tf_op jit(solution)/shard_map/ppermute | solution.py:313
  33.6 6.3 %collective-permute-start.4 = (s16[208,512]{1,0:T(8,128)(2,1)S(1)}, s16[208,512]{1,0:T(8,128)(2,1)S(1)}, u32[]{:S(2)}, u32[]{:S(2)}) collective-permute-start(s16[208,512]{1,0:T(8,128)(2,1)S(1)} %get-tuple-element.47), channel_id=1, source_target_pairs={{0,1},{1,0},{2,3},{3,2},{4,5},{5,4},{6,7},{7,6},{8,9},{9,8},{10,11... | collective-permute-start | bytes 638984 | tf_op jit(solution)/shard_map/ppermute | solution.py:313
  33.6 6.3 %collective-permute-start.5 = (s16[208,512]{1,0:T(8,128)(2,1)S(1)}, s16[208,512]{1,0:T(8,128)(2,1)S(1)}, u32[]{:S(2)}, u32[]{:S(2)}) collective-permute-start(s16[208,512]{1,0:T(8,128)(2,1)S(1)} %get-tuple-element.48), channel_id=1, source_target_pairs={{0,1},{1,0},{2,3},{3,2},{4,5},{5,4},{6,7},{7,6},{8,9},{9,8},{10,11... | collective-permute-start | bytes 638984 | tf_op jit(solution)/shard_map/ppermute | solution.py:313
  34.1 14.5 %collective-permute-start.11 = (s16[208,512]{1,0:T(8,128)(2,1)S(1)}, s16[208,512]{1,0:T(8,128)(2,1)S(1)}, u32[]{:S(2)}, u32[]{:S(2)}) collective-permute-start(s16[208,512]{1,0:T(8,128)(2,1)S(1)} %own.1.rest_0_), channel_id=1, source_target_pairs={{0,2},{1,3},{2,0},{3,1},{4,6},{5,7},{6,4},{7,5},{8,10},{9,11},{10,... | collective-permute-start | bytes 638984 | tf_op jit(solution)/shard_map/ppermute | solution.py:313
  36.4 15.6 %collective-permute-start.19 = (s16[400,512]{1,0:T(8,128)(2,1)S(1)}, s16[400,512]{1,0:T(8,128)(2,1)S(1)}, u32[]{:S(2)}, u32[]{:S(2)}) collective-permute-start(s16[400,512]{1,0:T(8,128)(2,1)S(1)} %hop4.3), channel_id=1, source_target_pairs={{0,6},{1,31},{2,4},{3,29},{4,10},{5,3},{6,8},{7,1},{8,14},{9,7},{1... | collective-permute-start | bytes 1228808 | tf_op jit(solution)/shard_map/ppermute | solution.py:313
  48.6 11.6 %copy-start.6 = (s32[1,3,8,128]{3,2,1,0:T(8,128)S(1)}, s32[1,3,8,128]{3,2,1,0:T(8,128)}, u32[]{:S(2)}) copy-start(s32[1,3,8,128]{3,2,1,0:T(8,128)} %param.12) | copy-start | bytes 36868
  48.6 12.7 %copy-start = (bf16[2,256,256]{2,1,0:T(8,128)(2,1)S(1)}, bf16[2,256,256]{2,1,0:T(8,128)(2,1)}, u32[]{:S(2)}) copy-start(bf16[2,256,256]{2,1,0:T(8,128)(2,1)} %constant.12.clone.cols) | copy-start | bytes 786436
  48.6 12.7 %copy-start.2 = (bf16[2,192,192]{2,1,0:T(8,128)(2,1)S(1)}, bf16[2,192,192]{2,1,0:T(8,128)(2,1)}, u32[]{:S(2)}) copy-start(bf16[2,192,192]{2,1,0:T(8,128)(2,1)} %constant.11.clone.rows_t) | copy-start | bytes 442372
  48.6 12.7 %copy-start.3 = (f32[1,192,512]{2,1,0:T(8,128)S(1)}, f32[1,192,512]{2,1,0:T(8,128)}, u32[]{:S(2)}) copy-start(f32[1,192,512]{2,1,0:T(8,128)} %param.11) | copy-start | bytes 1179652
  48.7 12.7 %copy-start.4 = (bf16[2,256,256]{2,1,0:T(8,128)(2,1)S(1)}, bf16[2,256,256]{2,1,0:T(8,128)(2,1)}, u32[]{:S(2)}) copy-start(bf16[2,256,256]{2,1,0:T(8,128)(2,1)} %constant.13.clone.cols_t) | copy-start | bytes 786436
  48.7 12.7 %copy-start.5 = (bf16[2,192,192]{2,1,0:T(8,128)(2,1)S(1)}, bf16[2,192,192]{2,1,0:T(8,128)(2,1)}, u32[]{:S(2)}) copy-start(bf16[2,192,192]{2,1,0:T(8,128)(2,1)} %constant.10.clone.rows) | copy-start | bytes 442372
  49.0 7.2 %collective-permute-start.12 = (s16[400,512]{1,0:T(8,128)(2,1)S(1)}, s16[400,512]{1,0:T(8,128)(2,1)S(1)}, u32[]{:S(2)}, u32[]{:S(2)}) collective-permute-start(s16[400,512]{1,0:T(8,128)(2,1)S(1)} %hop4.2), channel_id=1, source_target_pairs={{0,4},{1,29},{2,6},{3,31},{4,8},{5,1},{6,10},{7,3},{8,12},{9,5},{1... | collective-permute-start | bytes 1228808 | tf_op jit(solution)/shard_map/ppermute | solution.py:313
  49.1 2.9 %collective-permute-start.20 = (s16[208,512]{1,0:T(8,128)(2,1)S(1)}, s16[208,512]{1,0:T(8,128)(2,1)S(1)}, u32[]{:S(2)}, u32[]{:S(2)}) collective-permute-start(s16[208,512]{1,0:T(8,128)(2,1)S(1)} %get-tuple-element.61), channel_id=1, source_target_pairs={{0,1},{1,0},{2,3},{3,2},{4,5},{5,4},{6,7},{7,6},{8,9},{9,8},{10,11... | collective-permute-start | bytes 638984 | tf_op jit(solution)/shard_map/ppermute | solution.py:313
  56.9 4.5 %collective-permute-start.21 = (s16[208,512]{1,0:T(8,128)(2,1)S(1)}, s16[208,512]{1,0:T(8,128)(2,1)S(1)}, u32[]{:S(2)}, u32[]{:S(2)}) collective-permute-start(s16[208,512]{1,0:T(8,128)(2,1)S(1)} %get-tuple-element.63), channel_id=1, source_target_pairs={{0,1},{1,0},{2,3},{3,2},{4,5},{5,4},{6,7},{7,6},{8,9},{9,8},{10,11... | collective-permute-start | bytes 638984 | tf_op jit(solution)/shard_map/ppermute | solution.py:313

commit v6 on v5

--- a/solution.py
+++ b/solution.py
@@ -93,7 +93,9 @@
 
 
 ALONG = route(lambda z, y, c: (z + 1 - 2 * c, y, c))
+ACROSS = route(lambda z, y, c: (z + 1 - 2 * c, y, 1 - c))
 ASLANT = route(lambda z, y, c: (z + 1 - 2 * c, 1 - y, c))
+ASLANT_ACROSS = route(lambda z, y, c: (z + 1 - 2 * c, 1 - y, 1 - c))
 BESIDE = route(lambda z, y, c: (z, 1 - y, c))
 WITHIN = route(lambda z, y, c: (z, y, 1 - c))
 
@@ -298,11 +300,11 @@
     encode(keep[...] + decode(other), out)
 
 
-def meet_kernel(straight, aslant, keep, other, beside, kept, away, total):
+def last_hop_kernel(keep, low, high, arrived, _, mine, other, total):
     core = place()[2]
-    total[...] = decode(straight) + decode(aslant)
-    kept[...] = total[pl.ds(pl.multiple_of(core * ROWS, ROWS), ROWS), :] + keep[...] + decode(other) + decode(beside)
-    encode(total[pl.ds(pl.multiple_of((1 - core) * ROWS, ROWS), ROWS), :], away)
+    total[...] = keep[...] + decode_pair(low, high) + decode(arrived)
+    encode(total[pl.ds(pl.multiple_of(core * ROWS, ROWS), ROWS), :], mine)
+    encode(total[pl.ds(pl.multiple_of((1 - core) * ROWS, ROWS), ROWS), :], other)
 
 
 def replica_sum(inputs, grads):
@@ -318,16 +320,15 @@
     def first_hop(keep, other):
         return call_local(first_hop_kernel, (keep, other), (None, unit(0)), [((tall, breadth // 2), I16)], "hop1")[0]
 
-    def later_hop(step, keep, early, late, arrived, after):
+    def later_hop(step, keep, others, arrived, after):
         if step == 2:
-            others, cuts = (early, early), (unit(1), unit(2))
+            others, cuts = (others, others), (unit(1), unit(2))
         else:
-            others, cuts = late[2 * step - 6:2 * step - 4], (None, None)
-        scratch = [pltpu.VMEM((BOTH, breadth), F32)] if step == 2 else []
-        return call_local(
-            second_hop_kernel if step == 2 else later_hop_kernel,
-            (keep, *others, arrived, after), (None, *cuts, None, ANYWHERE),
-            [((tall, breadth), I16)], "hop%d" % step, scratch)[0]
+            others, cuts = others[2 * step - 6:2 * step - 4], (None, None)
+        kernel = {2: second_hop_kernel, 3: later_hop_kernel, 4: last_hop_kernel}[step]
+        outs = [((tall, breadth), I16)] if step < 4 else [((short, breadth), I16)] * 2
+        scratch = [] if step == 3 else [pltpu.VMEM((BOTH, breadth), F32)]
+        return call_local(kernel, (keep, *others, arrived, after), (None, *cuts, None, ANYWHERE), outs, "hop%d" % step, scratch)
 
     sums = all_sums(inputs, grads)
     keep4_a, away = next(sums)
@@ -338,23 +339,22 @@
     ring_b = first_hop(keep4_b, early_b)
     kept_a = sums.send(ring_a)
     kept_b = sums.send(kept_a[0])
-    ring_a = later_hop(2, kept_a[0], early_a, None, send(ring_a, ALONG), kept_a[0])
-    ring_b = later_hop(2, kept_b[0], early_b, None, send(ring_b, ALONG), kept_b[0])
+    ring_a, = later_hop(2, kept_a[0], early_a, send(ring_a, ALONG), kept_a[0])
+    ring_b, = later_hop(2, kept_b[0], early_b, send(ring_b, ALONG), kept_b[0])
     keep0_a, away = sums.send(ring_a)
     late_a = [send(part, WITHIN) for part in away]
     keep0_b, away = sums.send(ring_b)
     late_b = [send(part, WITHIN) for part in away]
     own_a = call_local(own_kernel, (keep0_a, late_a[4]), (None, None), [((short, breadth), I16)], "own")[0]
     beside = send(own_a, BESIDE)
-    ring_a = later_hop(3, kept_a[1], None, late_a, send(ring_a, ALONG), own_a)
-    ring_b = later_hop(3, kept_b[1], None, late_b, send(ring_b, ALONG), own_a)
-    ring_a = later_hop(4, kept_a[2], None, late_a, send(ring_a, ALONG), own_a)
-    ring_b = later_hop(4, kept_b[2], None, late_b, send(ring_b, ALONG), beside)
-    ring_a, ring_b = send(ring_a, ASLANT), send(ring_b, ALONG)
-    kept, away = call_local(
-        meet_kernel, (ring_b, ring_a, keep0_b, late_b[4], beside), (None,) * 5,
-        [((ROWS, breadth), F32), ((short, breadth), I16)], "meet", [pltpu.VMEM((BOTH, breadth), F32)])
-    return kept, send(away, WITHIN)
+    ring_a, = later_hop(3, kept_a[1], late_a, send(ring_a, ALONG), own_a)
+    ring_b, = later_hop(3, kept_b[1], late_b, send(ring_b, ALONG), own_a)
+    mine_a, other_a = later_hop(4, kept_a[2], late_a, send(ring_a, ALONG), own_a)
+    mine_b, other_b = later_hop(4, kept_b[2], late_b, send(ring_b, ALONG), own_a)
+    parts = (
+        late_b[4], beside, send(mine_a, ASLANT), send(other_a, ASLANT_ACROSS), send(mine_b, ALONG), send(other_b, ACROSS),
+    )
+    return keep0_b, parts
 
 
 def spread(row, height):
@@ -365,8 +365,11 @@
     return lax.broadcasted_iota(jnp.int32, (height, width), 0).astype(F32).astype(BF)
 
 
-def pick_kernel(kept, other, momentum, places, rows, rows_t, cols, cols_t, new_moment, payload, coef, sparse):
-    grad = kept[...] + decode(other)
+def pick_kernel(kept, *refs):
+    parts, (momentum, places, rows, rows_t, cols, cols_t, new_moment, payload, coef, sparse) = refs[:6], refs[6:]
+    grad = kept[...]
+    for part in parts:
+        grad = grad + decode(part)
     moment = 0.9 * momentum[...] + grad
     coef[...] = right_product(left_product(rows, moment), cols_t)
     tile_rows, tile_cols = momentum.shape[0] // CH, momentum.shape[1] // CH
@@ -414,13 +417,13 @@
             highs, lows, hots = [], [], []
             for r in range(reps):
                 high, low, row_code, col_code = (spread(part[t:t + 1, :], CH) for part in parts[r])
-                in_col = numbers == col_code
-                highs.append(jnp.where(in_col, high, none))
-                lows.append(jnp.where(in_col, low, none))
-                hots.append(jnp.where(numbers == row_code, one, none))
+                in_row = numbers == row_code
+                highs.append(jnp.where(in_row, high, none))
+                lows.append(jnp.where(in_row, low, none))
+                hots.append(jnp.where(numbers == col_code, one, none))
             both = jnp.concatenate([jnp.concatenate(highs, axis=1), jnp.concatenate(lows, axis=1)], axis=0)
-            out = dot_nt(jnp.concatenate(hots, axis=1), both)
-            blocks.append(out[:, :CH] + out[:, CH:])
+            out = dot_nt(both, jnp.concatenate(hots, axis=1))
+            blocks.append(out[:CH] + out[CH:])
         i, j = (2 * pair) // tile_cols, (2 * pair) % tile_cols
         total[i * CH:(i + 1) * CH, j * CH:(j + 2) * CH] = jnp.concatenate(blocks, axis=1)
     decoded = right_product(left_product(rows_t, total[...]), cols)
@@ -437,7 +440,7 @@
     tiles = (height // CH) * (breadth // CH)
     live = lax.broadcasted_iota(jnp.int32, indices.shape[1:], 2) < counts[0]
     places = jnp.where(live, indices[0], -1).reshape(tiles, SLOTS)
-    kept, other = replica_sum(activations[0], out_grads[0])
+    kept, parts = replica_sum(activations[0], out_grads[0])
     new_moment, payload = pl.pallas_call(
         pick_kernel,
         out_shape=[
@@ -447,7 +450,7 @@
         scratch_shapes=[pltpu.VMEM((height, breadth), F32), pltpu.VMEM((height, breadth), F32)],
         compiler_params=pltpu.CompilerParams(vmem_limit_bytes=32 << 20),
         name="pick",
-    )(kept, other, momentum[0], places, rows, rows_t, cols, cols_t)
+    )(kept, *parts, momentum[0], places, rows, rows_t, cols, cols_t)
     gathered = lax.all_to_all(payload, "rep", 0, 0)
     step_dir = pl.pallas_call(
         decode_kernel,

time: 82.6 us -> 75.1 us (0.909)
  waiting for transfers between devices: 16.2 us -> 11.2 us
  blocking collectives: 14.6 us -> 13.6 us
    ppermute x22 -> x23, waiting for transfers between devices: 16.2 us -> 11.2 us  [send(): return lax.ppermute(array, 'fsdp', pairs)]
    all_to_all x1, blocking collectives: 14.6 us -> 13.6 us  [body(): gathered = lax.all_to_all(payload, 'rep', 0, 0)]
    ppermute x22 -> x23, starting transfers between devices: 27.1 us -> 26.3 us  [send(): return lax.ppermute(array, 'fsdp', pairs)]
    pallas_call x10 -> x9, Pallas kernels: 3.26 us -> 2.94 us  [call_local(): pl.pallas_call(kernel, grid=(1,), in_specs=[spec(arg, cut) for arg, cut i...]
  transfers between devices with their start and end apart: 22 -> 23, of which waited for: 6 -> 4; matrix products, arithmetic and copies ran while one was open for 0% -> 0% of each run, Pallas kernels for 15% -> 17%
where the time goes in v6:
time: 75.1 us; the launch traced here: 74.9 us
  starting transfers between devices  26.3 us (35%)
  Pallas kernels  21.2 us (28%)
  blocking collectives  13.6 us (18%)
  waiting for transfers between devices  11.2 us (15%)
  between operations  1.53 us (2%)
  local copies, waits for them, and re-layouts  1.15 us (2%)
    ppermute x23, starting transfers between devices, send(): return lax.ppermute(array, 'fsdp', pairs)  26.3 us
    all_to_all x1, blocking collectives, body(): gathered = lax.all_to_all(payload, 'rep', 0, 0)  13.6 us
    pallas_call x6, Pallas kernels, partial_sums(): pl.pallas_call(kernel, in_specs=[pl.BlockSpec(memory_space=space) for _,...  12.1 us
    ppermute x23, waiting for transfers between devices, send(): return lax.ppermute(array, 'fsdp', pairs)  11.2 us
    pallas_call x1, Pallas kernels, body(): pl.pallas_call(decode_kernel, out_shape=jax.ShapeDtypeStruct((height, bre...  3.13 us
    pallas_call x1, Pallas kernels, body(): pl.pallas_call(pick_kernel, out_shape=[jax.ShapeDtypeStruct((height, brea...  2.94 us
    pallas_call x9, Pallas kernels, call_local(): pl.pallas_call(kernel, grid=(1,), in_specs=[spec(arg, cut) for arg, cut i...  2.94 us
  transfers between devices with their start and end apart: 23, of which 4 were waited for; matrix products, arithmetic and copies ran while one was open for 0% of the time, Pallas kernels for 17%

profile of v6, /device:TPU:1, one launch (start us, length us, event | category | flops | bytes accessed | tf_op | source)
XLA Modules:
  0.0 74.9 jit_solution(1647180404681229353)
XLA Ops:
  0.6 1.1 %copy-done.1 = bf16[1,768,512]{2,1,0:T(8,128)(2,1)S(1)} copy-done((bf16[1,768,512]{2,1,0:T(8,128)(2,1)S(1)}, bf16[1,768,512]{2,1,0:T(8,128)(2,1)}, u32[]{:S(2)}) %copy-start.1) | copy-done | bytes 786456
  1.8 2.5 %early.2 = (f32[384,256]{1,0:T(8,128)S(1)}, s16[3,208,512]{2,1,0:T(8,128)(2,1)S(1)}, bf16[768,512]{1,0:T(8,128)(2,1)S(1)}, bf16[2,768,384]{2,1,0:T(8,128)(2,1)S(1)}) custom-call(bf16[768,6144]{1,0:T(8,128)(2,1)} %bitcast.10, bf16[768,512]{1,0:T(8,128)(2,1)S(1)} %bitcast.8), custom_call_target="tpu_custom_call" | custom-call | flops 2717908992 | bytes 2949120 | tf_op jit(solution)/shard_map/early/pallas_call | solution.py:196
  4.2 3.3 %collective-permute-start = (s16[3,208,512]{2,1,0:T(8,128)(2,1)S(1)}, s16[3,208,512]{2,1,0:T(8,128)(2,1)S(1)}, u32[]{:S(2)}, u32[]{:S(2)}) collective-permute-start(s16[3,208,512]{2,1,0:T(8,128)(2,1)S(1)} %get-tuple-element.38._), channel_id=1, source_target_pairs={{0,1},{1,0},{2,3},{3,2},{4,5},{5,4},{6,7},{7,6},{8,9},{9,8},{10,11... | collective-permute-start | bytes 1916936 | tf_op jit(solution)/shard_map/ppermute | solution.py:315
  7.6 2.2 %early.3 = (f32[384,256]{1,0:T(8,128)S(1)}, s16[3,208,512]{2,1,0:T(8,128)(2,1)S(1)}, bf16[3,768,384]{2,1,0:T(8,128)(2,1)S(1)}) custom-call(bf16[768,6144]{1,0:T(8,128)(2,1)} %bitcast.11, bf16[768,512]{1,0:T(8,128)(2,1)S(1)} %get-tuple-element.36.grads.refs_1_, bf16[2,768,384]{2,1,0:T(8,128)(2,1)S(1)} %get-tuple-element.37.blocks, ...), custom_call_target="tpu_custom_call" | custom-call | flops 1811939328 | bytes 1966080 | tf_op jit(solution)/shard_map/early/pallas_call | solution.py:196
  10.0 3.9 %collective-permute-start.1 = (s16[400,256]{1,0:T(8,128)(2,1)S(1)}, s16[400,256]{1,0:T(8,128)(2,1)S(1)}, u32[]{:S(2)}, u32[]{:S(2)}) collective-permute-start(s16[400,256]{1,0:T(8,128)(2,1)S(1)} %hop1.2.refs_3_), channel_id=1, source_target_pairs={{0,4},{1,29},{2,6},{3,31},{4,8},{5,1},{6,10},{7,3},{8,12},{9,5},{1... | collective-permute-start | bytes 614408 | tf_op jit(solution)/shard_map/ppermute | solution.py:315
  14.1 1.9 %collective-permute-start.3 = (s16[400,256]{1,0:T(8,128)(2,1)S(1)}, s16[400,256]{1,0:T(8,128)(2,1)S(1)}, u32[]{:S(2)}, u32[]{:S(2)}) collective-permute-start(s16[400,256]{1,0:T(8,128)(2,1)S(1)} %hop1.3), channel_id=1, source_target_pairs={{0,4},{1,29},{2,6},{3,31},{4,8},{5,1},{6,10},{7,3},{8,12},{9,5},{1... | collective-permute-start | bytes 614408 | tf_op jit(solution)/shard_map/ppermute | solution.py:315
  16.0 1.7 %kept.2 = (f32[384,512]{1,0:T(8,128)S(1)}, f32[384,512]{1,0:T(8,128)S(1)}, f32[384,512]{1,0:T(8,128)S(1)}, bf16[3,768,384]{2,1,0:T(8,128)(2,1)S(1)}) custom-call(bf16[768,6144]{1,0:T(8,128)(2,1)} %bitcast.12, bf16[768,512]{1,0:T(8,128)(2,1)S(1)} %get-tuple-element.36.grads.refs_1_, bf16[3,768,384]{2,1,0:T(8,128)(2,1)S(1)} %get-tuple-element.39.refs_2_, ...), custom_call_target="tpu_custom_call" | custom-call | flops 2717908992 | bytes 2949120 | tf_op jit(solution)/shard_map/kept/pallas_call | solution.py:196
  17.7 1.7 %kept.3 = (f32[384,512]{1,0:T(8,128)S(1)}, f32[384,512]{1,0:T(8,128)S(1)}, f32[384,512]{1,0:T(8,128)S(1)}, bf16[3,768,384]{2,1,0:T(8,128)(2,1)S(1)}) custom-call(bf16[768,6144]{1,0:T(8,128)(2,1)} %bitcast.13, bf16[768,512]{1,0:T(8,128)(2,1)S(1)} %get-tuple-element.36.grads.refs_1_, bf16[3,768,384]{2,1,0:T(8,128)(2,1)S(1)} %get-tuple-element.41.refs_2_, ...), custom_call_target="tpu_custom_call" | custom-call | flops 2717908992 | bytes 2949120 | tf_op jit(solution)/shard_map/kept/pallas_call | solution.py:196
  19.5 0.5 hop2.2.refs_3_
  19.9 0.8 %collective-permute-start.11 = (s16[400,512]{1,0:T(8,128)(2,1)S(1)}, s16[400,512]{1,0:T(8,128)(2,1)S(1)}, u32[]{:S(2)}, u32[]{:S(2)}) collective-permute-start(s16[400,512]{1,0:T(8,128)(2,1)S(1)} %hop2.2.refs_3_), channel_id=1, source_target_pairs={{0,4},{1,29},{2,6},{3,31},{4,8},{5,1},{6,10},{7,3},{8,12},{9,5},{1... | collective-permute-start | bytes 1228808 | tf_op jit(solution)/shard_map/ppermute | solution.py:315
  20.8 0.5 hop2.3.refs_3_
  21.2 1.3 %collective-permute-start.19 = (s16[400,512]{1,0:T(8,128)(2,1)S(1)}, s16[400,512]{1,0:T(8,128)(2,1)S(1)}, u32[]{:S(2)}, u32[]{:S(2)}) collective-permute-start(s16[400,512]{1,0:T(8,128)(2,1)S(1)} %hop2.3.refs_3_), channel_id=1, source_target_pairs={{0,4},{1,29},{2,6},{3,31},{4,8},{5,1},{6,10},{7,3},{8,12},{9,5},{1... | collective-permute-start | bytes 1228808 | tf_op jit(solution)/shard_map/ppermute | solution.py:315
  22.5 2.7 %late.2 = (f32[192,512]{1,0:T(8,128)S(1)}, s16[208,512]{1,0:T(8,128)(2,1)S(1)}, s16[208,512]{1,0:T(8,128)(2,1)S(1)}, s16[208,512]{1,0:T(8,128)(2,1)S(1)}, s16[20...) custom-call(bf16[768,6144]{1,0:T(8,128)(2,1)} %bitcast.14, ...), custom_call_target="tpu_custom_call" | custom-call | flops 2717908992 | bytes 2949120 | tf_op jit(solution)/shard_map/late/pallas_call | solution.py:196
  25.3 0.5 collective-permute-start.9
  25.9 1.3 %late.3 = (f32[192,512]{1,0:T(8,128)S(1)}, s16[208,512]{1,0:T(8,128)(2,1)S(1)}, s16[208,512]{1,0:T(8,128)(2,1)S(1)}, s16[208,512]{1,0:T(8,128)(2,1)S(1)}, s16[20...) custom-call(bf16[768,6144]{1,0:T(8,128)(2,1)} %bitcast.15, bf16[768,512]{1,0:T(8,128)(2,1)S(1)} %get-tuple-element.36.grads.refs_1_, ...), custom_call_target="tpu_custom_call" | custom-call | flops 2717908992 | bytes 2949120 | tf_op jit(solution)/shard_map/late/pallas_call | solution.py:196
  27.3 0.5 collective-permute-start.17
  28.9 1.6 %collective-permute-start.12 = (s16[400,512]{1,0:T(8,128)(2,1)S(1)}, s16[400,512]{1,0:T(8,128)(2,1)S(1)}, u32[]{:S(2)}, u32[]{:S(2)}) collective-permute-start(s16[400,512]{1,0:T(8,128)(2,1)S(1)} %hop3.2), channel_id=1, source_target_pairs={{0,4},{1,29},{2,6},{3,31},{4,8},{5,1},{6,10},{7,3},{8,12},{9,5},{1... | collective-permute-start | bytes 1228808 | tf_op jit(solution)/shard_map/ppermute | solution.py:315
  30.5 1.1 %collective-permute-done.19.arrived = s16[400,512]{1,0:T(8,128)(2,1)S(1)} collective-permute-done((s16[400,512]{1,0:T(8,128)(2,1)S(1)}, s16[400,512]{1,0:T(8,128)(2,1)S(1)}, u32[]{:S(2)}, u32[]{:S(2)}) %collective-permute-start.19) | collective-permute-done | bytes 409632 | tf_op jit(solution)/shard_map/ppermute | solution.py:315
  31.8 1.7 %collective-permute-start.20 = (s16[400,512]{1,0:T(8,128)(2,1)S(1)}, s16[400,512]{1,0:T(8,128)(2,1)S(1)}, u32[]{:S(2)}, u32[]{:S(2)}) collective-permute-start(s16[400,512]{1,0:T(8,128)(2,1)S(1)} %hop3.3), channel_id=1, source_target_pairs={{0,4},{1,29},{2,6},{3,31},{4,8},{5,1},{6,10},{7,3},{8,12},{9,5},{1... | collective-permute-start | bytes 1228808 | tf_op jit(solution)/shard_map/ppermute | solution.py:315
  33.6 0.5 collective-permute-start.16
  34.8 1.2 %collective-permute-done.12.arrived = s16[400,512]{1,0:T(8,128)(2,1)S(1)} collective-permute-done((s16[400,512]{1,0:T(8,128)(2,1)S(1)}, s16[400,512]{1,0:T(8,128)(2,1)S(1)}, u32[]{:S(2)}, u32[]{:S(2)}) %collective-permute-start.12) | collective-permute-done | bytes 409632 | tf_op jit(solution)/shard_map/ppermute | solution.py:315
  36.0 1.3 %collective-permute-start.6 = (s16[208,512]{1,0:T(8,128)(2,1)S(1)}, s16[208,512]{1,0:T(8,128)(2,1)S(1)}, u32[]{:S(2)}, u32[]{:S(2)}) collective-permute-start(s16[208,512]{1,0:T(8,128)(2,1)S(1)} %own.1.rest_0_._), channel_id=1, source_target_pairs={{0,2},{1,3},{2,0},{3,1},{4,6},{5,7},{6,4},{7,5},{8,10},{9,11},{10,... | collective-permute-start | bytes 638984 | tf_op jit(solution)/shard_map/ppermute | solution.py:315
  37.4 0.5 hop4.2
  37.9 2.4 %collective-permute-start.13 = (s16[208,512]{1,0:T(8,128)(2,1)S(1)}, s16[208,512]{1,0:T(8,128)(2,1)S(1)}, u32[]{:S(2)}, u32[]{:S(2)}) collective-permute-start(s16[208,512]{1,0:T(8,128)(2,1)S(1)} %get-tuple-element.58), channel_id=1, source_target_pairs={{0,6},{1,31},{2,4},{3,29},{4,10},{5,3},{6,8},{7,1},{8,14},{9,7},{1... | collective-permute-start | bytes 638984 | tf_op jit(solution)/shard_map/ppermute | solution.py:315
  40.3 4.1 %collective-permute-start.14 = (s16[208,512]{1,0:T(8,128)(2,1)S(1)}, s16[208,512]{1,0:T(8,128)(2,1)S(1)}, u32[]{:S(2)}, u32[]{:S(2)}) collective-permute-start(s16[208,512]{1,0:T(8,128)(2,1)S(1)} %get-tuple-element.59), channel_id=1, source_target_pairs={{0,7},{1,30},{2,5},{3,28},{4,11},{5,2},{6,9},{7,0},{8,15},{9,6},{1... | collective-permute-start | bytes 638984 | tf_op jit(solution)/shard_map/ppermute | solution.py:315
  44.4 0.5 hop4.3
  45.0 1.3 %collective-permute-start.22 = (s16[208,512]{1,0:T(8,128)(2,1)S(1)}, s16[208,512]{1,0:T(8,128)(2,1)S(1)}, u32[]{:S(2)}, u32[]{:S(2)}) collective-permute-start(s16[208,512]{1,0:T(8,128)(2,1)S(1)} %get-tuple-element.67), channel_id=1, source_target_pairs={{0,5},{1,28},{2,7},{3,30},{4,9},{5,0},{6,11},{7,2},{8,13},{9,4},{1... | collective-permute-start | bytes 638984 | tf_op jit(solution)/shard_map/ppermute | solution.py:315
  46.3 4.6 %collective-permute-done.14.refs_3_ = s16[208,512]{1,0:T(8,128)(2,1)S(1)} collective-permute-done((s16[208,512]{1,0:T(8,128)(2,1)S(1)}, s16[208,512]{1,0:T(8,128)(2,1)S(1)}, u32[]{:S(2)}, u32[]{:S(2)}) %collective-permute-start.14) | collective-permute-done | bytes 213024 | tf_op jit(solution)/shard_map/ppermute | solution.py:315
  50.9 4.3 %collective-permute-done.22.refs_5_ = s16[208,512]{1,0:T(8,128)(2,1)S(1)} collective-permute-done((s16[208,512]{1,0:T(8,128)(2,1)S(1)}, s16[208,512]{1,0:T(8,128)(2,1)S(1)}, u32[]{:S(2)}, u32[]{:S(2)}) %collective-permute-start.22) | collective-permute-done | bytes 213024 | tf_op jit(solution)/shard_map/ppermute | solution.py:315
  55.2 2.9 %pick.1 = (f32[192,512]{1,0:T(8,128)}, f32[8,48,128]{2,1,0:T(8,128)S(1)}) custom-call(f32[192,512]{1,0:T(8,128)S(1)} %get-tuple-element.48.kept, s16[208,512]{1,0:T(8,128)(2,1)S(1)} %collective-permute-done.4.refs_0_, s16[208,512]{1,0:T(8,128)(2,1)S(1)} %collective-permute-done.6.refs_1_, s16[208,512]{1,0:T(8,128)(2,1)S(1)} %collective-permute-done.13.refs_2_, ...), custom_call_target="tpu_custom_call" | custom-call | tf_op jit(solution)/shard_map/pick/pallas_call | solution.py:444
  58.1 13.6 %all_to_all.5.gathered = f32[8,48,128]{2,1,0:T(8,128)S(1)} all-to-all(f32[8,48,128]{2,1,0:T(8,128)S(1)} %get-tuple-element.69), channel_id=1, replica_groups=mesh['rep'=8,'fsdp'=32] {'rep'}, dimensions={0} | all-to-all | bytes 393216 | tf_op jit(solution)/shard_map/all_to_all | solution.py:454
  71.7 3.1 %decode.1 = f32[192,512]{1,0:T(8,128)} custom-call(f32[8,48,128]{2,1,0:T(8,128)S(1)} %all_to_all.5.gathered, bf16[2,192,192]{2,1,0:T(8,128)(2,1)S(1)} %copy-done.2, bf16[2,256,256]{2,1,0:T(8,128)(2,1)S(1)} %copy-done), custom_call_target="tpu_custom_call" | custom-call | tf_op jit(solution)/shard_map/decode/pallas_call | solution.py:455
  (48 shorter events, 2.2 us)
Async XLA Ops:
  0.6 1.1 %copy-start.1 = (bf16[1,768,512]{2,1,0:T(8,128)(2,1)S(1)}, bf16[1,768,512]{2,1,0:T(8,128)(2,1)}, u32[]{:S(2)}) copy-start(bf16[1,768,512]{2,1,0:T(8,128)(2,1)} %param.10) | copy-start | bytes 2359300
  4.2 5.7 %collective-permute-start = (s16[3,208,512]{2,1,0:T(8,128)(2,1)S(1)}, s16[3,208,512]{2,1,0:T(8,128)(2,1)S(1)}, u32[]{:S(2)}, u32[]{:S(2)}) collective-permute-start(s16[3,208,512]{2,1,0:T(8,128)(2,1)S(1)} %get-tuple-element.38._), channel_id=1, source_target_pairs={{0,1},{1,0},{2,3},{3,2},{4,5},{5,4},{6,7},{7,6},{8,9},{9,8},{10,11... | collective-permute-start | bytes 1916936 | tf_op jit(solution)/shard_map/ppermute | solution.py:315
  9.8 4.2 %collective-permute-start.2 = (s16[3,208,512]{2,1,0:T(8,128)(2,1)S(1)}, s16[3,208,512]{2,1,0:T(8,128)(2,1)S(1)}, u32[]{:S(2)}, u32[]{:S(2)}) collective-permute-start(s16[3,208,512]{2,1,0:T(8,128)(2,1)S(1)} %get-tuple-element.46), channel_id=1, source_target_pairs={{0,1},{1,0},{2,3},{3,2},{4,5},{5,4},{6,7},{7,6},{8,9},{9,8},{10,11... | collective-permute-start | bytes 1916936 | tf_op jit(solution)/shard_map/ppermute | solution.py:315
  10.0 9.4 %collective-permute-start.1 = (s16[400,256]{1,0:T(8,128)(2,1)S(1)}, s16[400,256]{1,0:T(8,128)(2,1)S(1)}, u32[]{:S(2)}, u32[]{:S(2)}) collective-permute-start(s16[400,256]{1,0:T(8,128)(2,1)S(1)} %hop1.2.refs_3_), channel_id=1, source_target_pairs={{0,4},{1,29},{2,6},{3,31},{4,8},{5,1},{6,10},{7,3},{8,12},{9,5},{1... | collective-permute-start | bytes 614408 | tf_op jit(solution)/shard_map/ppermute | solution.py:315
  14.1 6.7 %collective-permute-start.3 = (s16[400,256]{1,0:T(8,128)(2,1)S(1)}, s16[400,256]{1,0:T(8,128)(2,1)S(1)}, u32[]{:S(2)}, u32[]{:S(2)}) collective-permute-start(s16[400,256]{1,0:T(8,128)(2,1)S(1)} %hop1.3), channel_id=1, source_target_pairs={{0,4},{1,29},{2,6},{3,31},{4,8},{5,1},{6,10},{7,3},{8,12},{9,5},{1... | collective-permute-start | bytes 614408 | tf_op jit(solution)/shard_map/ppermute | solution.py:315
  19.9 8.3 %collective-permute-start.11 = (s16[400,512]{1,0:T(8,128)(2,1)S(1)}, s16[400,512]{1,0:T(8,128)(2,1)S(1)}, u32[]{:S(2)}, u32[]{:S(2)}) collective-permute-start(s16[400,512]{1,0:T(8,128)(2,1)S(1)} %hop2.2.refs_3_), channel_id=1, source_target_pairs={{0,4},{1,29},{2,6},{3,31},{4,8},{5,1},{6,10},{7,3},{8,12},{9,5},{1... | collective-permute-start | bytes 1228808 | tf_op jit(solution)/shard_map/ppermute | solution.py:315
  21.2 10.3 %collective-permute-start.19 = (s16[400,512]{1,0:T(8,128)(2,1)S(1)}, s16[400,512]{1,0:T(8,128)(2,1)S(1)}, u32[]{:S(2)}, u32[]{:S(2)}) collective-permute-start(s16[400,512]{1,0:T(8,128)(2,1)S(1)} %hop2.3.refs_3_), channel_id=1, source_target_pairs={{0,4},{1,29},{2,6},{3,31},{4,8},{5,1},{6,10},{7,3},{8,12},{9,5},{1... | collective-permute-start | bytes 1228808 | tf_op jit(solution)/shard_map/ppermute | solution.py:315
  25.2 2.0 %collective-permute-start.5 = (s16[208,512]{1,0:T(8,128)(2,1)S(1)}, s16[208,512]{1,0:T(8,128)(2,1)S(1)}, u32[]{:S(2)}, u32[]{:S(2)}) collective-permute-start(s16[208,512]{1,0:T(8,128)(2,1)S(1)} %get-tuple-element.51), channel_id=1, source_target_pairs={{0,1},{1,0},{2,3},{3,2},{4,5},{5,4},{6,7},{7,6},{8,9},{9,8},{10,11... | collective-permute-start | bytes 638984 | tf_op jit(solution)/shard_map/ppermute | solution.py:315
  25.3 2.4 %collective-permute-start.9 = (s16[208,512]{1,0:T(8,128)(2,1)S(1)}, s16[208,512]{1,0:T(8,128)(2,1)S(1)}, u32[]{:S(2)}, u32[]{:S(2)}) collective-permute-start(s16[208,512]{1,0:T(8,128)(2,1)S(1)} %get-tuple-element.56), channel_id=1, source_target_pairs={{0,1},{1,0},{2,3},{3,2},{4,5},{5,4},{6,7},{7,6},{8,9},{9,8},{10,11... | collective-permute-start | bytes 638984 | tf_op jit(solution)/shard_map/ppermute | solution.py:315
  25.8 2.0 %collective-permute-start.10 = (s16[208,512]{1,0:T(8,128)(2,1)S(1)}, s16[208,512]{1,0:T(8,128)(2,1)S(1)}, u32[]{:S(2)}, u32[]{:S(2)}) collective-permute-start(s16[208,512]{1,0:T(8,128)(2,1)S(1)} %get-tuple-element.57), channel_id=1, source_target_pairs={{0,1},{1,0},{2,3},{3,2},{4,5},{5,4},{6,7},{7,6},{8,9},{9,8},{10,11... | collective-permute-start | bytes 638984 | tf_op jit(solution)/shard_map/ppermute | solution.py:315
  27.3 1.6 %collective-permute-start.17 = (s16[208,512]{1,0:T(8,128)(2,1)S(1)}, s16[208,512]{1,0:T(8,128)(2,1)S(1)}, u32[]{:S(2)}, u32[]{:S(2)}) collective-permute-start(s16[208,512]{1,0:T(8,128)(2,1)S(1)} %get-tuple-element.64), channel_id=1, source_target_pairs={{0,1},{1,0},{2,3},{3,2},{4,5},{5,4},{6,7},{7,6},{8,9},{9,8},{10,11... | collective-permute-start | bytes 638984 | tf_op jit(solution)/shard_map/ppermute | solution.py:315
  27.8 2.7 %collective-permute-start.18 = (s16[208,512]{1,0:T(8,128)(2,1)S(1)}, s16[208,512]{1,0:T(8,128)(2,1)S(1)}, u32[]{:S(2)}, u32[]{:S(2)}) collective-permute-start(s16[208,512]{1,0:T(8,128)(2,1)S(1)} %get-tuple-element.65), channel_id=1, source_target_pairs={{0,1},{1,0},{2,3},{3,2},{4,5},{5,4},{6,7},{7,6},{8,9},{9,8},{10,11... | collective-permute-start | bytes 638984 | tf_op jit(solution)/shard_map/ppermute | solution.py:315
  27.9 5.7 %collective-permute-start.7 = (s16[208,512]{1,0:T(8,128)(2,1)S(1)}, s16[208,512]{1,0:T(8,128)(2,1)S(1)}, u32[]{:S(2)}, u32[]{:S(2)}) collective-permute-start(s16[208,512]{1,0:T(8,128)(2,1)S(1)} %get-tuple-element.53), channel_id=1, source_target_pairs={{0,1},{1,0},{2,3},{3,2},{4,5},{5,4},{6,7},{7,6},{8,9},{9,8},{10,11... | collective-permute-start | bytes 638984 | tf_op jit(solution)/shard_map/ppermute | solution.py:315
  28.3 5.8 %collective-permute-start.8 = (s16[208,512]{1,0:T(8,128)(2,1)S(1)}, s16[208,512]{1,0:T(8,128)(2,1)S(1)}, u32[]{:S(2)}, u32[]{:S(2)}) collective-permute-start(s16[208,512]{1,0:T(8,128)(2,1)S(1)} %get-tuple-element.54), channel_id=1, source_target_pairs={{0,1},{1,0},{2,3},{3,2},{4,5},{5,4},{6,7},{7,6},{8,9},{9,8},{10,11... | collective-permute-start | bytes 638984 | tf_op jit(solution)/shard_map/ppermute | solution.py:315
  28.9 7.2 %collective-permute-start.12 = (s16[400,512]{1,0:T(8,128)(2,1)S(1)}, s16[400,512]{1,0:T(8,128)(2,1)S(1)}, u32[]{:S(2)}, u32[]{:S(2)}) collective-permute-start(s16[400,512]{1,0:T(8,128)(2,1)S(1)} %hop3.2), channel_id=1, source_target_pairs={{0,4},{1,29},{2,6},{3,31},{4,8},{5,1},{6,10},{7,3},{8,12},{9,5},{1... | collective-permute-start | bytes 1228808 | tf_op jit(solution)/shard_map/ppermute | solution.py:315
  31.8 12.5 %collective-permute-start.20 = (s16[400,512]{1,0:T(8,128)(2,1)S(1)}, s16[400,512]{1,0:T(8,128)(2,1)S(1)}, u32[]{:S(2)}, u32[]{:S(2)}) collective-permute-start(s16[400,512]{1,0:T(8,128)(2,1)S(1)} %hop3.3), channel_id=1, source_target_pairs={{0,4},{1,29},{2,6},{3,31},{4,8},{5,1},{6,10},{7,3},{8,12},{9,5},{1... | collective-permute-start | bytes 1228808 | tf_op jit(solution)/shard_map/ppermute | solution.py:315
  33.6 4.3 %collective-permute-start.15 = (s16[208,512]{1,0:T(8,128)(2,1)S(1)}, s16[208,512]{1,0:T(8,128)(2,1)S(1)}, u32[]{:S(2)}, u32[]{:S(2)}) collective-permute-start(s16[208,512]{1,0:T(8,128)(2,1)S(1)} %get-tuple-element.61), channel_id=1, source_target_pairs={{0,1},{1,0},{2,3},{3,2},{4,5},{5,4},{6,7},{7,6},{8,9},{9,8},{10,11... | collective-permute-start | bytes 638984 | tf_op jit(solution)/shard_map/ppermute | solution.py:315
  33.6 6.7 %collective-permute-start.16 = (s16[208,512]{1,0:T(8,128)(2,1)S(1)}, s16[208,512]{1,0:T(8,128)(2,1)S(1)}, u32[]{:S(2)}, u32[]{:S(2)}) collective-permute-start(s16[208,512]{1,0:T(8,128)(2,1)S(1)} %get-tuple-element.62), channel_id=1, source_target_pairs={{0,1},{1,0},{2,3},{3,2},{4,5},{5,4},{6,7},{7,6},{8,9},{9,8},{10,11... | collective-permute-start | bytes 638984 | tf_op jit(solution)/shard_map/ppermute | solution.py:315
  34.1 10.9 %collective-permute-start.4 = (s16[208,512]{1,0:T(8,128)(2,1)S(1)}, s16[208,512]{1,0:T(8,128)(2,1)S(1)}, u32[]{:S(2)}, u32[]{:S(2)}) collective-permute-start(s16[208,512]{1,0:T(8,128)(2,1)S(1)} %get-tuple-element.49), channel_id=1, source_target_pairs={{0,1},{1,0},{2,3},{3,2},{4,5},{5,4},{6,7},{7,6},{8,9},{9,8},{10,11... | collective-permute-start | bytes 638984 | tf_op jit(solution)/shard_map/ppermute | solution.py:315
  36.0 10.2 %collective-permute-start.6 = (s16[208,512]{1,0:T(8,128)(2,1)S(1)}, s16[208,512]{1,0:T(8,128)(2,1)S(1)}, u32[]{:S(2)}, u32[]{:S(2)}) collective-permute-start(s16[208,512]{1,0:T(8,128)(2,1)S(1)} %own.1.rest_0_._), channel_id=1, source_target_pairs={{0,2},{1,3},{2,0},{3,1},{4,6},{5,7},{6,4},{7,5},{8,10},{9,11},{10,... | collective-permute-start | bytes 638984 | tf_op jit(solution)/shard_map/ppermute | solution.py:315
  37.3 8.9 %copy-start.6 = (s32[1,3,8,128]{3,2,1,0:T(8,128)S(1)}, s32[1,3,8,128]{3,2,1,0:T(8,128)}, u32[]{:S(2)}) copy-start(s32[1,3,8,128]{3,2,1,0:T(8,128)} %param.12) | copy-start | bytes 36868
  37.3 17.9 %copy-start = (bf16[2,256,256]{2,1,0:T(8,128)(2,1)S(1)}, bf16[2,256,256]{2,1,0:T(8,128)(2,1)}, u32[]{:S(2)}) copy-start(bf16[2,256,256]{2,1,0:T(8,128)(2,1)} %constant.12.clone.refs_10_.cols) | copy-start | bytes 786436
  37.3 17.9 %copy-start.2 = (bf16[2,192,192]{2,1,0:T(8,128)(2,1)S(1)}, bf16[2,192,192]{2,1,0:T(8,128)(2,1)}, u32[]{:S(2)}) copy-start(bf16[2,192,192]{2,1,0:T(8,128)(2,1)} %constant.11.clone.refs_9_.rows_t) | copy-start | bytes 442372
  37.3 17.9 %copy-start.3 = (f32[1,192,512]{2,1,0:T(8,128)S(1)}, f32[1,192,512]{2,1,0:T(8,128)}, u32[]{:S(2)}) copy-start(f32[1,192,512]{2,1,0:T(8,128)} %param.11) | copy-start | bytes 1179652
  37.3 17.9 %copy-start.4 = (bf16[2,256,256]{2,1,0:T(8,128)(2,1)S(1)}, bf16[2,256,256]{2,1,0:T(8,128)(2,1)}, u32[]{:S(2)}) copy-start(bf16[2,256,256]{2,1,0:T(8,128)(2,1)} %constant.13.clone.refs_11_) | copy-start | bytes 786436
  37.3 17.9 %copy-start.5 = (bf16[2,192,192]{2,1,0:T(8,128)(2,1)S(1)}, bf16[2,192,192]{2,1,0:T(8,128)(2,1)}, u32[]{:S(2)}) copy-start(bf16[2,192,192]{2,1,0:T(8,128)(2,1)} %constant.10.clone.refs_8_) | copy-start | bytes 442372
  37.9 8.4 %collective-permute-start.13 = (s16[208,512]{1,0:T(8,128)(2,1)S(1)}, s16[208,512]{1,0:T(8,128)(2,1)S(1)}, u32[]{:S(2)}, u32[]{:S(2)}) collective-permute-start(s16[208,512]{1,0:T(8,128)(2,1)S(1)} %get-tuple-element.58), channel_id=1, source_target_pairs={{0,6},{1,31},{2,4},{3,29},{4,10},{5,3},{6,8},{7,1},{8,14},{9,7},{1... | collective-permute-start | bytes 638984 | tf_op jit(solution)/shard_map/ppermute | solution.py:315
  40.3 10.6 %collective-permute-start.14 = (s16[208,512]{1,0:T(8,128)(2,1)S(1)}, s16[208,512]{1,0:T(8,128)(2,1)S(1)}, u32[]{:S(2)}, u32[]{:S(2)}) collective-permute-start(s16[208,512]{1,0:T(8,128)(2,1)S(1)} %get-tuple-element.59), channel_id=1, source_target_pairs={{0,7},{1,30},{2,5},{3,28},{4,11},{5,2},{6,9},{7,0},{8,15},{9,6},{1... | collective-permute-start | bytes 638984 | tf_op jit(solution)/shard_map/ppermute | solution.py:315
  44.9 6.0 %collective-permute-start.21 = (s16[208,512]{1,0:T(8,128)(2,1)S(1)}, s16[208,512]{1,0:T(8,128)(2,1)S(1)}, u32[]{:S(2)}, u32[]{:S(2)}) collective-permute-start(s16[208,512]{1,0:T(8,128)(2,1)S(1)} %get-tuple-element.66), channel_id=1, source_target_pairs={{0,4},{1,29},{2,6},{3,31},{4,8},{5,1},{6,10},{7,3},{8,12},{9,5},{1... | collective-permute-start | bytes 638984 | tf_op jit(solution)/shard_map/ppermute | solution.py:315
  45.0 10.2 %collective-permute-start.22 = (s16[208,512]{1,0:T(8,128)(2,1)S(1)}, s16[208,512]{1,0:T(8,128)(2,1)S(1)}, u32[]{:S(2)}, u32[]{:S(2)}) collective-permute-start(s16[208,512]{1,0:T(8,128)(2,1)S(1)} %get-tuple-element.67), channel_id=1, source_target_pairs={{0,5},{1,28},{2,7},{3,30},{4,9},{5,0},{6,11},{7,2},{8,13},{9,4},{1... | collective-permute-start | bytes 638984 | tf_op jit(solution)/shard_map/ppermute | solution.py:315

commit v7 on v6

--- a/solution.py
+++ b/solution.py
@@ -105,8 +105,8 @@
 
 
 EARLY = (4, -3)
-LATE = (-2, -1, 0)
-KEPT = (3, 2, 1)
+LATE = (-2, -1)
+KEPT = (3, 2, 1, 0)
 
 
 def loads(steps, swap, inputs, blocks, sems):
@@ -160,10 +160,14 @@
 
 
 def kept_kernel(then, inputs, grads, blocks, _, *refs):
-    keeps, (ahead, sums, out_sems, sems) = refs[:3], refs[3:]
+    keeps, (keep0, away0, ahead, sums, out_sems, both, sems) = refs[:3], refs[3:]
     more = loads(*then, inputs, ahead, sems)
     for copy in more:
         copy.start()
+    core = place()[2]
+    both[...] = product(blocks[3], grads[...])
+    keep0[...] = both[pl.ds(pl.multiple_of(core * ROWS, ROWS), ROWS), :]
+    encode(both[pl.ds(pl.multiple_of((1 - core) * ROWS, ROWS), ROWS), :], away0)
     copies = []
     for n, keep in enumerate(keeps):
         sums[n] = product(blocks[n], grads[...])
@@ -173,20 +177,15 @@
         copy.wait()
 
 
-def late_kernel(then, inputs, grads, blocks, _, keep0, *refs):
-    away, refs = refs[:5], refs[5:]
-    more = loads(*then, inputs, refs[0], refs[2]) if then else []
-    both = refs[1] if then else refs[0]
+def late_kernel(then, inputs, grads, blocks, _, *refs):
+    away, refs = refs[:4], refs[4:]
+    more = loads(*then, inputs, *refs) if then else []
     for copy in more:
         copy.start()
-    core = place()[2]
     for n in range(2):
         total = product(blocks[n], grads[...])
         encode(total[:ROWS], away[2 * n])
         encode(total[ROWS:], away[2 * n + 1])
-    both[...] = product(blocks[2], grads[...])
-    keep0[...] = both[pl.ds(pl.multiple_of(core * ROWS, ROWS), ROWS), :]
-    encode(both[pl.ds(pl.multiple_of((1 - core) * ROWS, ROWS), ROWS), :], away[4])
     for copy in more:
         copy.wait()
 
@@ -221,8 +220,8 @@
         return pltpu.SemaphoreType.DMA((len(steps),))
 
     early = [((BOTH, breadth // 2), F32, vmem), ((3, *short), I16, vmem)]
-    kept = [(tall, F32, pl.ANY)] * 3
-    late = [((ROWS, breadth), F32, vmem)] + [(short, I16, vmem)] * 5
+    kept = [(tall, F32, pl.ANY)] * 3 + [((ROWS, breadth), F32, vmem), (short, I16, vmem)]
+    late = [(short, I16, vmem)] * 4
     both = vmem(tall, F32)
 
     def args(blocks, behind):
@@ -235,19 +234,18 @@
     keep4, away, ahead = partial_sums(
         early_kernel, args(ahead, behind), early + [fetched(KEPT)], [both, sems(KEPT)], 2, "early")
     behind = yield keep4, away
-    sums = [vmem((3, *tall), F32), sems(KEPT)]
+    sums = [vmem((3, *tall), F32), pltpu.SemaphoreType.DMA((3,)), both]
     *keeps, ahead = partial_sums(
-        lambda *refs: kept_kernel((KEPT, False), *refs), args(ahead, behind), kept + [fetched(KEPT)], sums + [sems(KEPT)], 3, "kept")
+        lambda *refs: kept_kernel((KEPT, False), *refs), args(ahead, behind), kept + [fetched(KEPT)], sums + [sems(KEPT)], 4, "kept")
     behind = yield keeps
     *keeps, ahead = partial_sums(
-        lambda *refs: kept_kernel((LATE, True), *refs), args(ahead, behind), kept + [fetched(LATE)], sums + [sems(LATE)], 3, "kept")
+        lambda *refs: kept_kernel((LATE, True), *refs), args(ahead, behind), kept + [fetched(LATE)], sums + [sems(LATE)], 4, "kept")
     behind = yield keeps
-    keep0, *away, ahead = partial_sums(
-        lambda *refs: late_kernel((LATE, False), *refs), args(ahead, behind), late + [fetched(LATE)], [both, sems(LATE)], 3, "late")
-    behind = yield keep0, away
-    keep0, *away = partial_sums(
-        lambda *refs: late_kernel(None, *refs), args(ahead, behind), late, [both], 3, "late")
-    yield keep0, away
+    *away, ahead = partial_sums(
+        lambda *refs: late_kernel((LATE, False), *refs), args(ahead, behind), late + [fetched(LATE)], [sems(LATE)], 2, "late")
+    behind = yield away
+    yield partial_sums(
+        lambda *refs: late_kernel(None, *refs), args(ahead, behind), late, [], 2, "late")
 
 
 ANYWHERE = "any"
@@ -291,18 +289,21 @@
     encode(total[...], out)
 
 
-def later_hop_kernel(keep, low, high, arrived, *rest):
-    out = rest[-1]
-    encode(keep[...] + decode_pair(low, high) + decode(arrived), out)
+def join_kernel(keep, low, high, out):
+    out[...] = keep[...] + decode_pair(low, high)
+
+
+def later_hop_kernel(joined, arrived, _, out):
+    encode(joined[...] + decode(arrived), out)
 
 
 def own_kernel(keep, other, out):
     encode(keep[...] + decode(other), out)
 
 
-def last_hop_kernel(keep, low, high, arrived, _, mine, other, total):
+def last_hop_kernel(joined, arrived, _, mine, other, total):
     core = place()[2]
-    total[...] = keep[...] + decode_pair(low, high) + decode(arrived)
+    total[...] = joined[...] + decode(arrived)
     encode(total[pl.ds(pl.multiple_of(core * ROWS, ROWS), ROWS), :], mine)
     encode(total[pl.ds(pl.multiple_of((1 - core) * ROWS, ROWS), ROWS), :], other)
 
@@ -320,15 +321,22 @@
     def first_hop(keep, other):
         return call_local(first_hop_kernel, (keep, other), (None, unit(0)), [((tall, breadth // 2), I16)], "hop1")[0]
 
-    def later_hop(step, keep, others, arrived, after):
-        if step == 2:
-            others, cuts = (others, others), (unit(1), unit(2))
-        else:
-            others, cuts = others[2 * step - 6:2 * step - 4], (None, None)
-        kernel = {2: second_hop_kernel, 3: later_hop_kernel, 4: last_hop_kernel}[step]
-        outs = [((tall, breadth), I16)] if step < 4 else [((short, breadth), I16)] * 2
-        scratch = [] if step == 3 else [pltpu.VMEM((BOTH, breadth), F32)]
-        return call_local(kernel, (keep, *others, arrived, after), (None, *cuts, None, ANYWHERE), outs, "hop%d" % step, scratch)
+    def second_hop(keep, other, arrived, after):
+        return call_local(
+            second_hop_kernel, (keep, other, other, arrived, after), (None, unit(1), unit(2), None, ANYWHERE),
+            [((tall, breadth), I16)], "hop2", [pltpu.VMEM((BOTH, breadth), F32)])[0]
+
+    def join(keep, low, high):
+        return call_local(join_kernel, (keep, low, high), (None,) * 3, [((BOTH, breadth), F32)], "join")[0]
+
+    def third_hop(joined, arrived, after):
+        return call_local(
+            later_hop_kernel, (joined, arrived, after), (None, None, ANYWHERE), [((tall, breadth), I16)], "hop3")[0]
+
+    def last_hop(joined, arrived, after):
+        return call_local(
+            last_hop_kernel, (joined, arrived, after), (None, None, ANYWHERE),
+            [((short, breadth), I16)] * 2, "hop4", [pltpu.VMEM((BOTH, breadth), F32)])
 
     sums = all_sums(inputs, grads)
     keep4_a, away = next(sums)
@@ -337,24 +345,24 @@
     early_b = send(away, WITHIN)
     ring_a = first_hop(keep4_a, early_a)
     ring_b = first_hop(keep4_b, early_b)
-    kept_a = sums.send(ring_a)
-    kept_b = sums.send(kept_a[0])
-    ring_a, = later_hop(2, kept_a[0], early_a, send(ring_a, ALONG), kept_a[0])
-    ring_b, = later_hop(2, kept_b[0], early_b, send(ring_b, ALONG), kept_b[0])
-    keep0_a, away = sums.send(ring_a)
-    late_a = [send(part, WITHIN) for part in away]
-    keep0_b, away = sums.send(ring_b)
-    late_b = [send(part, WITHIN) for part in away]
-    own_a = call_local(own_kernel, (keep0_a, late_a[4]), (None, None), [((short, breadth), I16)], "own")[0]
+    *kept_a, keep0_a, away0 = sums.send(ring_a)
+    away0_a = send(away0, WITHIN)
+    *kept_b, keep0_b, away0 = sums.send(kept_a[0])
+    away0_b = send(away0, WITHIN)
+    own_a = call_local(own_kernel, (keep0_a, away0_a), (None, None), [((short, breadth), I16)], "own")[0]
     beside = send(own_a, BESIDE)
-    ring_a, = later_hop(3, kept_a[1], late_a, send(ring_a, ALONG), own_a)
-    ring_b, = later_hop(3, kept_b[1], late_b, send(ring_b, ALONG), own_a)
-    mine_a, other_a = later_hop(4, kept_a[2], late_a, send(ring_a, ALONG), own_a)
-    mine_b, other_b = later_hop(4, kept_b[2], late_b, send(ring_b, ALONG), own_a)
+    ring_a = second_hop(kept_a[0], early_a, send(ring_a, ALONG), kept_a[0])
+    ring_b = second_hop(kept_b[0], early_b, send(ring_b, ALONG), own_a)
+    late_a = [send(part, WITHIN) for part in sums.send(ring_a)]
+    late_b = [send(part, WITHIN) for part in sums.send(ring_b)]
+    ring_a = third_hop(join(kept_a[1], *late_a[:2]), send(ring_a, ALONG), own_a)
+    ring_b = third_hop(join(kept_b[1], *late_b[:2]), send(ring_b, ALONG), away0_b)
+    mine_a, other_a = last_hop(join(kept_a[2], *late_a[2:]), send(ring_a, ALONG), own_a)
+    mine_b, other_b = last_hop(join(kept_b[2], *late_b[2:]), send(ring_b, ALONG), own_a)
     parts = (
-        late_b[4], beside, send(mine_a, ASLANT), send(other_a, ASLANT_ACROSS), send(mine_b, ALONG), send(other_b, ACROSS),
+        away0_b, beside, send(mine_a, ASLANT), send(other_a, ASLANT_ACROSS), send(mine_b, ALONG), send(other_b, ACROSS),
     )
-    return keep0_b, parts
+    return keep0_b, parts, own_a
 
 
 def spread(row, height):
@@ -365,39 +373,45 @@
     return lax.broadcasted_iota(jnp.int32, (height, width), 0).astype(F32).astype(BF)
 
 
+GROUP = 4
+
+
+def hot_kernel(places, _, col_hots, row_hots, mask):
+    tile_cols = mask.shape[1] // CH
+    numbers = row_numbers(GROUP * CH, GROUP * SLOTS)
+    one, none = jnp.ones((), BF), jnp.zeros((), BF)
+    for g in range(col_hots.shape[0]):
+        part = [places[GROUP * g + n:GROUP * g + n + 1, :] for n in range(GROUP)]
+        row_code = (jnp.concatenate(part, axis=1) >> 6).astype(F32)
+        col_code = jnp.concatenate([(p & 63) + CH * n for n, p in enumerate(part)], axis=1).astype(F32)
+        col_hots[g] = jnp.where(numbers == spread(col_code, GROUP * CH), one, none)
+        row_hots[g] = jnp.where(numbers[:CH] == spread(row_code, CH), one, none)
+        i, j = (GROUP * g) // tile_cols, (GROUP * g) % tile_cols
+        mask[i * CH:(i + 1) * CH, j * CH:(j + GROUP) * CH] = dot_nt(row_hots[g], col_hots[g])
+
+
 def pick_kernel(kept, *refs):
-    parts, (momentum, places, rows, rows_t, cols, cols_t, new_moment, payload, coef, sparse) = refs[:6], refs[6:]
+    parts, refs = refs[:6], refs[6:]
+    momentum, places, col_hots, row_hots, mask, rows, rows_t, cols, cols_t, new_moment, payload, coef = refs
     grad = kept[...]
     for part in parts:
         grad = grad + decode(part)
     moment = 0.9 * momentum[...] + grad
     coef[...] = right_product(left_product(rows, moment), cols_t)
-    tile_rows, tile_cols = momentum.shape[0] // CH, momentum.shape[1] // CH
-    group = 4
-    tiles = tile_rows * tile_cols
-    width = group * SLOTS
-    numbers = row_numbers(group * CH, width)
-    one, none = jnp.ones((), BF), jnp.zeros((), BF)
-    for i in range(tile_rows):
-        for h in range(tile_cols // group):
-            first = i * tile_cols + h * group
-            part = [places[first + n:first + n + 1, :] for n in range(group)]
-            row_code = (jnp.concatenate(part, axis=1) >> 6).astype(F32)
-            col_code = jnp.concatenate([(p & 63) + CH * n for n, p in enumerate(part)], axis=1).astype(F32)
-            col_hot = jnp.where(numbers == spread(col_code, group * CH), one, none)
-            row_hot = jnp.where(numbers[:CH] == spread(row_code, CH), one, none)
-            block = coef[i * CH:(i + 1) * CH, h * group * CH:(h + 1) * group * CH]
-            high, low = split(block)
-            chosen = dot(jnp.concatenate([high, low], axis=0), col_hot)
-            chosen = chosen[:CH] + chosen[CH:]
-            value = jnp.sum(chosen * row_hot.astype(F32), axis=0, keepdims=True)
-            for n in range(group):
-                for r in range(payload.shape[0]):
-                    payload[r, first + n:first + n + 1, :] = value[:, n * SLOTS:(n + 1) * SLOTS]
-            sparse[i * CH:(i + 1) * CH, h * group * CH:(h + 1) * group * CH] = block * dot_nt(row_hot, col_hot)
+    tile_cols = momentum.shape[1] // CH
+    for g in range(col_hots.shape[0]):
+        i, j = (GROUP * g) // tile_cols, (GROUP * g) % tile_cols
+        high, low = split(coef[i * CH:(i + 1) * CH, j * CH:(j + GROUP) * CH])
+        chosen = dot(jnp.concatenate([high, low], axis=0), col_hots[g])
+        chosen = chosen[:CH] + chosen[CH:]
+        value = jnp.sum(chosen * row_hots[g].astype(F32), axis=0, keepdims=True)
+        for n in range(GROUP):
+            for r in range(payload.shape[0]):
+                payload[r, GROUP * g + n:GROUP * g + n + 1, :] = value[:, n * SLOTS:(n + 1) * SLOTS]
+    tiles = places.shape[0]
     for r in range(payload.shape[0]):
         payload[r, tiles:, :] = places[...].astype(F32)
-    new_moment[...] = moment - right_product(left_product(rows_t, sparse[...]), cols)
+    new_moment[...] = moment - right_product(left_product(rows_t, coef[...] * mask[...]), cols)
 
 
 def decode_kernel(gathered, rows_t, cols, step_dir, total):
@@ -440,17 +454,21 @@
     tiles = (height // CH) * (breadth // CH)
     live = lax.broadcasted_iota(jnp.int32, indices.shape[1:], 2) < counts[0]
     places = jnp.where(live, indices[0], -1).reshape(tiles, SLOTS)
-    kept, parts = replica_sum(activations[0], out_grads[0])
+    kept, parts, after = replica_sum(activations[0], out_grads[0])
+    groups = tiles // GROUP
+    hots = call_local(hot_kernel, (places, after), (None, ANYWHERE), [
+        ((groups, GROUP * CH, GROUP * SLOTS), BF), ((groups, CH, GROUP * SLOTS), BF), ((height, breadth), F32),
+    ], "hot")
     new_moment, payload = pl.pallas_call(
         pick_kernel,
         out_shape=[
             jax.ShapeDtypeStruct((height, breadth), F32),
             jax.ShapeDtypeStruct((reps, 2 * tiles, SLOTS), F32),
         ],
-        scratch_shapes=[pltpu.VMEM((height, breadth), F32), pltpu.VMEM((height, breadth), F32)],
+        scratch_shapes=[pltpu.VMEM((height, breadth), F32)],
         compiler_params=pltpu.CompilerParams(vmem_limit_bytes=32 << 20),
         name="pick",
-    )(kept, *parts, momentum[0], places, rows, rows_t, cols, cols_t)
+    )(kept, *parts, momentum[0], places, *hots, rows, rows_t, cols, cols_t)
     gathered = lax.all_to_all(payload, "rep", 0, 0)
     step_dir = pl.pallas_call(
         decode_kernel,

time: 75.1 us -> 78 us (1.039)
  waiting for transfers between devices: 11.2 us -> 7.6 us
  starting transfers between devices: 26.3 us -> 28.4 us
  Pallas kernels: 21.2 us -> 22.9 us
  local copies, waits for them, and re-layouts: 1.15 us -> 2.59 us
  blocking collectives: 13.6 us -> 14.5 us
    ppermute x23, waiting for transfers between devices: 11.2 us -> 7.6 us  [send(): return lax.ppermute(array, 'fsdp', pairs)]
    ppermute x23, starting transfers between devices: 26.3 us -> 28.4 us  [send(): return lax.ppermute(array, 'fsdp', pairs)]
    pallas_call x6, Pallas kernels: 12.1 us -> 13.8 us  [partial_sums(): pl.pallas_call(kernel, in_specs=[pl.BlockSpec(memory_space=space) for _,...]
    unnamed x14 -> x16, local copies, waits for them, and re-layouts: 1.15 us -> 2.59 us
    all_to_all x1, blocking collectives: 13.6 us -> 14.5 us  [body(): gathered = lax.all_to_all(payload, 'rep', 0, 0)]
    pallas_call x9 -> x14, Pallas kernels: 2.94 us -> 3.5 us  [call_local(): pl.pallas_call(kernel, grid=(1,), in_specs=[spec(arg, cut) for arg, cut i...]
  transfers between devices with their start and end apart: 23 -> 23, of which waited for: 4 -> 3; matrix products, arithmetic and copies ran while one was open for 0% -> 0% of each run, Pallas kernels for 17% -> 19%
where the time goes in v7:
time: 78 us; the launch traced here: 77.7 us
  starting transfers between devices  28.4 us (36%)
  Pallas kernels  22.9 us (29%)
  blocking collectives  14.5 us (19%)
  waiting for transfers between devices  7.6 us (10%)
  local copies, waits for them, and re-layouts  2.59 us (3%)
  between operations  1.62 us (2%)
    ppermute x23, starting transfers between devices, send(): return lax.ppermute(array, 'fsdp', pairs)  28.4 us
    all_to_all x1, blocking collectives, body(): gathered = lax.all_to_all(payload, 'rep', 0, 0)  14.5 us
    pallas_call x6, Pallas kernels, partial_sums(): pl.pallas_call(kernel, in_specs=[pl.BlockSpec(memory_space=space) for _,...  13.8 us
    ppermute x23, waiting for transfers between devices, send(): return lax.ppermute(array, 'fsdp', pairs)  7.6 us
    pallas_call x14, Pallas kernels, call_local(): pl.pallas_call(kernel, grid=(1,), in_specs=[spec(arg, cut) for arg, cut i...  3.5 us
    pallas_call x1, Pallas kernels, body(): pl.pallas_call(decode_kernel, out_shape=jax.ShapeDtypeStruct((height, bre...  3.13 us
    unnamed x16, local copies, waits for them, and re-layouts  2.59 us
    pallas_call x1, Pallas kernels, body(): pl.pallas_call(pick_kernel, out_shape=[jax.ShapeDtypeStruct((height, brea...  2.42 us
  transfers between devices with their start and end apart: 23, of which 3 were waited for; matrix products, arithmetic and copies ran while one was open for 0% of the time, Pallas kernels for 19%

profile of v7, /device:TPU:1, one launch (start us, length us, event | category | flops | bytes accessed | tf_op | source)
XLA Modules:
  0.0 77.7 jit_solution(11805997225145706952)
XLA Ops:
  0.6 1.1 %copy-done.2 = bf16[1,768,512]{2,1,0:T(8,128)(2,1)S(1)} copy-done((bf16[1,768,512]{2,1,0:T(8,128)(2,1)S(1)}, bf16[1,768,512]{2,1,0:T(8,128)(2,1)}, u32[]{:S(2)}) %copy-start.2) | copy-done | bytes 786456
  1.8 2.5 %early.2 = (f32[384,256]{1,0:T(8,128)S(1)}, s16[3,208,512]{2,1,0:T(8,128)(2,1)S(1)}, bf16[768,512]{1,0:T(8,128)(2,1)S(1)}, bf16[2,768,384]{2,1,0:T(8,128)(2,1)S(1)}) custom-call(bf16[768,6144]{1,0:T(8,128)(2,1)} %bitcast.10, bf16[768,512]{1,0:T(8,128)(2,1)S(1)} %bitcast.8), custom_call_target="tpu_custom_call" | custom-call | flops 2717908992 | bytes 2949120 | tf_op jit(solution)/shard_map/early/pallas_call | solution.py:195
  4.2 3.3 %collective-permute-start = (s16[3,208,512]{2,1,0:T(8,128)(2,1)S(1)}, s16[3,208,512]{2,1,0:T(8,128)(2,1)S(1)}, u32[]{:S(2)}, u32[]{:S(2)}) collective-permute-start(s16[3,208,512]{2,1,0:T(8,128)(2,1)S(1)} %get-tuple-element.41._), channel_id=1, source_target_pairs={{0,1},{1,0},{2,3},{3,2},{4,5},{5,4},{6,7},{7,6},{8,9},{9,8},{10,11... | collective-permute-start | bytes 1916936 | tf_op jit(solution)/shard_map/ppermute | solution.py:316
  7.6 2.4 %early.3 = (f32[384,256]{1,0:T(8,128)S(1)}, s16[3,208,512]{2,1,0:T(8,128)(2,1)S(1)}, bf16[4,768,384]{2,1,0:T(8,128)(2,1)S(1)}) custom-call(bf16[768,6144]{1,0:T(8,128)(2,1)} %bitcast.11, bf16[768,512]{1,0:T(8,128)(2,1)S(1)} %get-tuple-element.39.grads.refs_1_, bf16[2,768,384]{2,1,0:T(8,128)(2,1)S(1)} %get-tuple-element.40.blocks, ...), custom_call_target="tpu_custom_call" | custom-call | flops 1811939328 | bytes 1966080 | tf_op jit(solution)/shard_map/early/pallas_call | solution.py:195
  10.0 1.4 %copy-done.6 = bf16[4,768,384]{2,1,0:T(8,128)(2,1)} copy-done((bf16[4,768,384]{2,1,0:T(8,128)(2,1)}, bf16[4,768,384]{2,1,0:T(8,128)(2,1)S(1)}, u32[]{:S(2)}) %copy-start.6) | copy-done | bytes 2359320
  11.6 3.9 %collective-permute-start.4 = (s16[400,256]{1,0:T(8,128)(2,1)S(1)}, s16[400,256]{1,0:T(8,128)(2,1)S(1)}, u32[]{:S(2)}, u32[]{:S(2)}) collective-permute-start(s16[400,256]{1,0:T(8,128)(2,1)S(1)} %hop1.2.refs_3_), channel_id=1, source_target_pairs={{0,4},{1,29},{2,6},{3,31},{4,8},{5,1},{6,10},{7,3},{8,12},{9,5},{1... | collective-permute-start | bytes 614408 | tf_op jit(solution)/shard_map/ppermute | solution.py:316
  15.5 4.0 %kept.2 = (f32[384,512]{1,0:T(8,128)S(1)}, f32[384,512]{1,0:T(8,128)S(1)}, f32[384,512]{1,0:T(8,128)S(1)}, f32[192,512]{1,0:T(8,128)S(1)}, s16[208,512]{1,0:T(8,...) custom-call(bf16[768,6144]{1,0:T(8,128)(2,1)} %bitcast.12, bf16[768,512]{1,0:T(8,128)(2,1)S(1)} %get-tuple-element.39.grads.refs_1_, ...), custom_call_target="tpu_custom_call" | custom-call | flops 3623878656 | bytes 3932160 | tf_op jit(solution)/shard_map/kept/pallas_call | solution.py:195
  19.8 0.8 %collective-permute-start.14 = (s16[400,256]{1,0:T(8,128)(2,1)S(1)}, s16[400,256]{1,0:T(8,128)(2,1)S(1)}, u32[]{:S(2)}, u32[]{:S(2)}) collective-permute-start(s16[400,256]{1,0:T(8,128)(2,1)S(1)} %hop1.3), channel_id=1, source_target_pairs={{0,4},{1,29},{2,6},{3,31},{4,8},{5,1},{6,10},{7,3},{8,12},{9,5},{1... | collective-permute-start | bytes 614408 | tf_op jit(solution)/shard_map/ppermute | solution.py:316
  20.6 2.1 %kept.3 = (f32[384,512]{1,0:T(8,128)S(1)}, f32[384,512]{1,0:T(8,128)S(1)}, f32[384,512]{1,0:T(8,128)S(1)}, f32[192,512]{1,0:T(8,128)S(1)}, s16[208,512]{1,0:T(8,...) custom-call(bf16[768,6144]{1,0:T(8,128)(2,1)} %bitcast.13, bf16[768,512]{1,0:T(8,128)(2,1)S(1)} %get-tuple-element.39.grads.refs_1_, ...), custom_call_target="tpu_custom_call" | custom-call | flops 3623878656 | bytes 3932160 | tf_op jit(solution)/shard_map/kept/pallas_call | solution.py:195
  22.7 0.5 hop2.2.refs_3_
  23.2 1.6 %collective-permute-start.9 = (s16[400,512]{1,0:T(8,128)(2,1)S(1)}, s16[400,512]{1,0:T(8,128)(2,1)S(1)}, u32[]{:S(2)}, u32[]{:S(2)}) collective-permute-start(s16[400,512]{1,0:T(8,128)(2,1)S(1)} %hop2.2.refs_3_), channel_id=1, source_target_pairs={{0,4},{1,29},{2,6},{3,31},{4,8},{5,1},{6,10},{7,3},{8,12},{9,5},{1... | collective-permute-start | bytes 1228808 | tf_op jit(solution)/shard_map/ppermute | solution.py:316
  24.8 1.9 %late.2 = (s16[208,512]{1,0:T(8,128)(2,1)S(1)}, s16[208,512]{1,0:T(8,128)(2,1)S(1)}, s16[208,512]{1,0:T(8,128)(2,1)S(1)}, s16[208,512]{1,0:T(8,128)(2,1)S(1)}, bf16[2,768,384]{2,1,0:T(8,128)(2,1)S(1)}) custom-call(bf16[768,6144]{1,0:T(8,128)(2,1)} %bitcast.14, bf16[768,512]{1,0:T(8,128)(2,1)S(1)} %get-tuple-element.39.grads.refs_1_, ...), custom_call_target="tpu_custom_call" | custom-call | flops 1811939328 | bytes 1966080 | tf_op jit(solution)/shard_map/late/pallas_call | solution.py:195
  26.7 0.5 collective-permute-start.8
  27.4 0.5 hop2.3.refs_3_
  27.9 1.1 %collective-permute-start.19 = (s16[400,512]{1,0:T(8,128)(2,1)S(1)}, s16[400,512]{1,0:T(8,128)(2,1)S(1)}, u32[]{:S(2)}, u32[]{:S(2)}) collective-permute-start(s16[400,512]{1,0:T(8,128)(2,1)S(1)} %hop2.3.refs_3_), channel_id=1, source_target_pairs={{0,4},{1,29},{2,6},{3,31},{4,8},{5,1},{6,10},{7,3},{8,12},{9,5},{1... | collective-permute-start | bytes 1228808 | tf_op jit(solution)/shard_map/ppermute | solution.py:316
  28.9 0.9 %late.3 = (s16[208,512]{1,0:T(8,128)(2,1)S(1)}, s16[208,512]{1,0:T(8,128)(2,1)S(1)}, s16[208,512]{1,0:T(8,128)(2,1)S(1)}, s16[208,512]{1,0:T(8,128)(2,1)S(1)}) custom-call(bf16[768,6144]{1,0:T(8,128)(2,1)} %bitcast.15, bf16[768,512]{1,0:T(8,128)(2,1)S(1)} %get-tuple-element.39.grads.refs_1_, bf16[2,768,384]{2,1,0:T(8,128)(2,1)S(1)} %get-tuple-element.60.refs_2_, ...), custom_call_target="tpu_custom_call" | custom-call | flops 1811939328 | bytes 1966080 | tf_op jit(solution)/shard_map/late/pallas_call | solution.py:195
  29.9 0.8 %collective-permute-start.17 = (s16[208,512]{1,0:T(8,128)(2,1)S(1)}, s16[208,512]{1,0:T(8,128)(2,1)S(1)}, u32[]{:S(2)}, u32[]{:S(2)}) collective-permute-start(s16[208,512]{1,0:T(8,128)(2,1)S(1)} %get-tuple-element.67), channel_id=1, source_target_pairs={{0,1},{1,0},{2,3},{3,2},{4,5},{5,4},{6,7},{7,6},{8,9},{9,8},{10,11... | collective-permute-start | bytes 638984 | tf_op jit(solution)/shard_map/ppermute | solution.py:316
  31.2 1.0 %collective-permute-start.5 = (s16[208,512]{1,0:T(8,128)(2,1)S(1)}, s16[208,512]{1,0:T(8,128)(2,1)S(1)}, u32[]{:S(2)}, u32[]{:S(2)}) collective-permute-start(s16[208,512]{1,0:T(8,128)(2,1)S(1)} %get-tuple-element.52), channel_id=1, source_target_pairs={{0,1},{1,0},{2,3},{3,2},{4,5},{5,4},{6,7},{7,6},{8,9},{9,8},{10,11... | collective-permute-start | bytes 638984 | tf_op jit(solution)/shard_map/ppermute | solution.py:316
  32.5 1.8 %collective-permute-start.10 = (s16[400,512]{1,0:T(8,128)(2,1)S(1)}, s16[400,512]{1,0:T(8,128)(2,1)S(1)}, u32[]{:S(2)}, u32[]{:S(2)}) collective-permute-start(s16[400,512]{1,0:T(8,128)(2,1)S(1)} %hop3.2), channel_id=1, source_target_pairs={{0,4},{1,29},{2,6},{3,31},{4,8},{5,1},{6,10},{7,3},{8,12},{9,5},{1... | collective-permute-start | bytes 1228808 | tf_op jit(solution)/shard_map/ppermute | solution.py:316
  34.5 0.7 collective-permute-done.19.arrived
  35.4 2.0 %collective-permute-start.20 = (s16[400,512]{1,0:T(8,128)(2,1)S(1)}, s16[400,512]{1,0:T(8,128)(2,1)S(1)}, u32[]{:S(2)}, u32[]{:S(2)}) collective-permute-start(s16[400,512]{1,0:T(8,128)(2,1)S(1)} %hop3.3), channel_id=1, source_target_pairs={{0,4},{1,29},{2,6},{3,31},{4,8},{5,1},{6,10},{7,3},{8,12},{9,5},{1... | collective-permute-start | bytes 1228808 | tf_op jit(solution)/shard_map/ppermute | solution.py:316
  39.1 1.4 %collective-permute-start.3 = (s16[208,512]{1,0:T(8,128)(2,1)S(1)}, s16[208,512]{1,0:T(8,128)(2,1)S(1)}, u32[]{:S(2)}, u32[]{:S(2)}) collective-permute-start(s16[208,512]{1,0:T(8,128)(2,1)S(1)} %own.1._), channel_id=1, source_target_pairs={{0,2},{1,3},{2,0},{3,1},{4,6},{5,7},{6,4},{7,5},{8,10},{9,11},{10,... | collective-permute-start | bytes 638984 | tf_op jit(solution)/shard_map/ppermute | solution.py:316
  41.2 2.8 %collective-permute-start.11 = (s16[208,512]{1,0:T(8,128)(2,1)S(1)}, s16[208,512]{1,0:T(8,128)(2,1)S(1)}, u32[]{:S(2)}, u32[]{:S(2)}) collective-permute-start(s16[208,512]{1,0:T(8,128)(2,1)S(1)} %get-tuple-element.57), channel_id=1, source_target_pairs={{0,6},{1,31},{2,4},{3,29},{4,10},{5,3},{6,8},{7,1},{8,14},{9,7},{1... | collective-permute-start | bytes 638984 | tf_op jit(solution)/shard_map/ppermute | solution.py:316
  44.0 1.9 %collective-permute-start.12 = (s16[208,512]{1,0:T(8,128)(2,1)S(1)}, s16[208,512]{1,0:T(8,128)(2,1)S(1)}, u32[]{:S(2)}, u32[]{:S(2)}) collective-permute-start(s16[208,512]{1,0:T(8,128)(2,1)S(1)} %get-tuple-element.58), channel_id=1, source_target_pairs={{0,7},{1,30},{2,5},{3,28},{4,11},{5,2},{6,9},{7,0},{8,15},{9,6},{1... | collective-permute-start | bytes 638984 | tf_op jit(solution)/shard_map/ppermute | solution.py:316
  46.3 1.1 %collective-permute-start.21 = (s16[208,512]{1,0:T(8,128)(2,1)S(1)}, s16[208,512]{1,0:T(8,128)(2,1)S(1)}, u32[]{:S(2)}, u32[]{:S(2)}) collective-permute-start(s16[208,512]{1,0:T(8,128)(2,1)S(1)} %get-tuple-element.69), channel_id=1, source_target_pairs={{0,4},{1,29},{2,6},{3,31},{4,8},{5,1},{6,10},{7,3},{8,12},{9,5},{1... | collective-permute-start | bytes 638984 | tf_op jit(solution)/shard_map/ppermute | solution.py:316
  47.4 2.7 %collective-permute-start.22 = (s16[208,512]{1,0:T(8,128)(2,1)S(1)}, s16[208,512]{1,0:T(8,128)(2,1)S(1)}, u32[]{:S(2)}, u32[]{:S(2)}) collective-permute-start(s16[208,512]{1,0:T(8,128)(2,1)S(1)} %get-tuple-element.70), channel_id=1, source_target_pairs={{0,5},{1,28},{2,7},{3,30},{4,9},{5,0},{6,11},{7,2},{8,13},{9,4},{1... | collective-permute-start | bytes 638984 | tf_op jit(solution)/shard_map/ppermute | solution.py:316
  50.1 0.6 hot.1
  50.7 4.3 %collective-permute-done.3.refs_1_ = s16[208,512]{1,0:T(8,128)(2,1)S(1)} collective-permute-done((s16[208,512]{1,0:T(8,128)(2,1)S(1)}, s16[208,512]{1,0:T(8,128)(2,1)S(1)}, u32[]{:S(2)}, u32[]{:S(2)}) %collective-permute-start.3) | collective-permute-done | bytes 213024 | tf_op jit(solution)/shard_map/ppermute | solution.py:316
  55.0 2.5 %collective-permute-done.22.refs_5_ = s16[208,512]{1,0:T(8,128)(2,1)S(1)} collective-permute-done((s16[208,512]{1,0:T(8,128)(2,1)S(1)}, s16[208,512]{1,0:T(8,128)(2,1)S(1)}, u32[]{:S(2)}, u32[]{:S(2)}) %collective-permute-start.22) | collective-permute-done | bytes 213024 | tf_op jit(solution)/shard_map/ppermute | solution.py:316
  57.6 2.4 %pick.1 = (f32[192,512]{1,0:T(8,128)}, f32[8,48,128]{2,1,0:T(8,128)S(1)}) custom-call(f32[192,512]{1,0:T(8,128)S(1)} %get-tuple-element.46.kept, s16[208,512]{1,0:T(8,128)(2,1)S(1)} %collective-permute-done.1._.refs_0_, s16[208,512]{1,0:T(8,128)(2,1)S(1)} %collective-permute-done.3.refs_1_, s16[208,512]{1,0:T(8,128)(2,1)S(1)} %collective-permute-done.11.refs_2_, ...), custom_call_target="tpu_custom_call" | custom-call | tf_op jit(solution)/shard_map/pick/pallas_call | solution.py:462
  60.0 14.5 %all_to_all.5.gathered = f32[8,48,128]{2,1,0:T(8,128)S(1)} all-to-all(f32[8,48,128]{2,1,0:T(8,128)S(1)} %get-tuple-element.75), channel_id=1, replica_groups=mesh['rep'=8,'fsdp'=32] {'rep'}, dimensions={0} | all-to-all | bytes 393216 | tf_op jit(solution)/shard_map/all_to_all | solution.py:472
  74.5 3.1 %decode.1 = f32[192,512]{1,0:T(8,128)} custom-call(f32[8,48,128]{2,1,0:T(8,128)S(1)} %all_to_all.5.gathered, bf16[2,192,192]{2,1,0:T(8,128)(2,1)S(1)} %copy-done.1, bf16[2,256,256]{2,1,0:T(8,128)(2,1)S(1)} %copy-done), custom_call_target="tpu_custom_call" | custom-call | tf_op jit(solution)/shard_map/decode/pallas_call | solution.py:473
  (55 shorter events, 3.7 us)
Async XLA Ops:
  0.6 1.1 %copy-start.2 = (bf16[1,768,512]{2,1,0:T(8,128)(2,1)S(1)}, bf16[1,768,512]{2,1,0:T(8,128)(2,1)}, u32[]{:S(2)}) copy-start(bf16[1,768,512]{2,1,0:T(8,128)(2,1)} %param.10) | copy-start | bytes 2359300
  4.2 7.2 %collective-permute-start = (s16[3,208,512]{2,1,0:T(8,128)(2,1)S(1)}, s16[3,208,512]{2,1,0:T(8,128)(2,1)S(1)}, u32[]{:S(2)}, u32[]{:S(2)}) collective-permute-start(s16[3,208,512]{2,1,0:T(8,128)(2,1)S(1)} %get-tuple-element.41._), channel_id=1, source_target_pairs={{0,1},{1,0},{2,3},{3,2},{4,5},{5,4},{6,7},{7,6},{8,9},{9,8},{10,11... | collective-permute-start | bytes 1916936 | tf_op jit(solution)/shard_map/ppermute | solution.py:316
  10.0 1.4 %copy-start.6 = (bf16[4,768,384]{2,1,0:T(8,128)(2,1)}, bf16[4,768,384]{2,1,0:T(8,128)(2,1)S(1)}, u32[]{:S(2)}) copy-start(bf16[4,768,384]{2,1,0:T(8,128)(2,1)S(1)} %get-tuple-element.42.refs_2_) | copy-start | bytes 7077892
  11.4 8.2 %collective-permute-start.13 = (s16[3,208,512]{2,1,0:T(8,128)(2,1)S(1)}, s16[3,208,512]{2,1,0:T(8,128)(2,1)S(1)}, u32[]{:S(2)}, u32[]{:S(2)}) collective-permute-start(s16[3,208,512]{2,1,0:T(8,128)(2,1)S(1)} %get-tuple-element.62), channel_id=1, source_target_pairs={{0,1},{1,0},{2,3},{3,2},{4,5},{5,4},{6,7},{7,6},{8,9},{9,8},{10,11... | collective-permute-start | bytes 1916936 | tf_op jit(solution)/shard_map/ppermute | solution.py:316
  11.6 11.1 %collective-permute-start.4 = (s16[400,256]{1,0:T(8,128)(2,1)S(1)}, s16[400,256]{1,0:T(8,128)(2,1)S(1)}, u32[]{:S(2)}, u32[]{:S(2)}) collective-permute-start(s16[400,256]{1,0:T(8,128)(2,1)S(1)} %hop1.2.refs_3_), channel_id=1, source_target_pairs={{0,4},{1,29},{2,6},{3,31},{4,8},{5,1},{6,10},{7,3},{8,12},{9,5},{1... | collective-permute-start | bytes 614408 | tf_op jit(solution)/shard_map/ppermute | solution.py:316
  19.5 7.7 %collective-permute-start.2 = (s16[208,512]{1,0:T(8,128)(2,1)S(1)}, s16[208,512]{1,0:T(8,128)(2,1)S(1)}, u32[]{:S(2)}, u32[]{:S(2)}) collective-permute-start(s16[208,512]{1,0:T(8,128)(2,1)S(1)} %get-tuple-element.49), channel_id=1, source_target_pairs={{0,1},{1,0},{2,3},{3,2},{4,5},{5,4},{6,7},{7,6},{8,9},{9,8},{10,11... | collective-permute-start | bytes 638984 | tf_op jit(solution)/shard_map/ppermute | solution.py:316
  19.8 7.6 %collective-permute-start.14 = (s16[400,256]{1,0:T(8,128)(2,1)S(1)}, s16[400,256]{1,0:T(8,128)(2,1)S(1)}, u32[]{:S(2)}, u32[]{:S(2)}) collective-permute-start(s16[400,256]{1,0:T(8,128)(2,1)S(1)} %hop1.3), channel_id=1, source_target_pairs={{0,4},{1,29},{2,6},{3,31},{4,8},{5,1},{6,10},{7,3},{8,12},{9,5},{1... | collective-permute-start | bytes 614408 | tf_op jit(solution)/shard_map/ppermute | solution.py:316
  23.2 8.0 %collective-permute-start.9 = (s16[400,512]{1,0:T(8,128)(2,1)S(1)}, s16[400,512]{1,0:T(8,128)(2,1)S(1)}, u32[]{:S(2)}, u32[]{:S(2)}) collective-permute-start(s16[400,512]{1,0:T(8,128)(2,1)S(1)} %hop2.2.refs_3_), channel_id=1, source_target_pairs={{0,4},{1,29},{2,6},{3,31},{4,8},{5,1},{6,10},{7,3},{8,12},{9,5},{1... | collective-permute-start | bytes 1228808 | tf_op jit(solution)/shard_map/ppermute | solution.py:316
  26.6 4.0 %collective-permute-start.7 = (s16[208,512]{1,0:T(8,128)(2,1)S(1)}, s16[208,512]{1,0:T(8,128)(2,1)S(1)}, u32[]{:S(2)}, u32[]{:S(2)}) collective-permute-start(s16[208,512]{1,0:T(8,128)(2,1)S(1)} %get-tuple-element.55), channel_id=1, source_target_pairs={{0,1},{1,0},{2,3},{3,2},{4,5},{5,4},{6,7},{7,6},{8,9},{9,8},{10,11... | collective-permute-start | bytes 638984 | tf_op jit(solution)/shard_map/ppermute | solution.py:316
  26.7 4.1 %collective-permute-start.8 = (s16[208,512]{1,0:T(8,128)(2,1)S(1)}, s16[208,512]{1,0:T(8,128)(2,1)S(1)}, u32[]{:S(2)}, u32[]{:S(2)}) collective-permute-start(s16[208,512]{1,0:T(8,128)(2,1)S(1)} %get-tuple-element.56), channel_id=1, source_target_pairs={{0,1},{1,0},{2,3},{3,2},{4,5},{5,4},{6,7},{7,6},{8,9},{9,8},{10,11... | collective-permute-start | bytes 638984 | tf_op jit(solution)/shard_map/ppermute | solution.py:316
  27.9 7.4 %collective-permute-start.19 = (s16[400,512]{1,0:T(8,128)(2,1)S(1)}, s16[400,512]{1,0:T(8,128)(2,1)S(1)}, u32[]{:S(2)}, u32[]{:S(2)}) collective-permute-start(s16[400,512]{1,0:T(8,128)(2,1)S(1)} %hop2.3.refs_3_), channel_id=1, source_target_pairs={{0,4},{1,29},{2,6},{3,31},{4,8},{5,1},{6,10},{7,3},{8,12},{9,5},{1... | collective-permute-start | bytes 1228808 | tf_op jit(solution)/shard_map/ppermute | solution.py:316
  29.9 2.7 %collective-permute-start.17 = (s16[208,512]{1,0:T(8,128)(2,1)S(1)}, s16[208,512]{1,0:T(8,128)(2,1)S(1)}, u32[]{:S(2)}, u32[]{:S(2)}) collective-permute-start(s16[208,512]{1,0:T(8,128)(2,1)S(1)} %get-tuple-element.67), channel_id=1, source_target_pairs={{0,1},{1,0},{2,3},{3,2},{4,5},{5,4},{6,7},{7,6},{8,9},{9,8},{10,11... | collective-permute-start | bytes 638984 | tf_op jit(solution)/shard_map/ppermute | solution.py:316
  30.7 3.7 %collective-permute-start.18 = (s16[208,512]{1,0:T(8,128)(2,1)S(1)}, s16[208,512]{1,0:T(8,128)(2,1)S(1)}, u32[]{:S(2)}, u32[]{:S(2)}) collective-permute-start(s16[208,512]{1,0:T(8,128)(2,1)S(1)} %get-tuple-element.68), channel_id=1, source_target_pairs={{0,1},{1,0},{2,3},{3,2},{4,5},{5,4},{6,7},{7,6},{8,9},{9,8},{10,11... | collective-permute-start | bytes 638984 | tf_op jit(solution)/shard_map/ppermute | solution.py:316
  30.8 3.7 %collective-permute-start.1 = (s16[208,512]{1,0:T(8,128)(2,1)S(1)}, s16[208,512]{1,0:T(8,128)(2,1)S(1)}, u32[]{:S(2)}, u32[]{:S(2)}) collective-permute-start(s16[208,512]{1,0:T(8,128)(2,1)S(1)} %get-tuple-element.47), channel_id=1, source_target_pairs={{0,1},{1,0},{2,3},{3,2},{4,5},{5,4},{6,7},{7,6},{8,9},{9,8},{10,11... | collective-permute-start | bytes 638984 | tf_op jit(solution)/shard_map/ppermute | solution.py:316
  31.2 6.8 %collective-permute-start.5 = (s16[208,512]{1,0:T(8,128)(2,1)S(1)}, s16[208,512]{1,0:T(8,128)(2,1)S(1)}, u32[]{:S(2)}, u32[]{:S(2)}) collective-permute-start(s16[208,512]{1,0:T(8,128)(2,1)S(1)} %get-tuple-element.52), channel_id=1, source_target_pairs={{0,1},{1,0},{2,3},{3,2},{4,5},{5,4},{6,7},{7,6},{8,9},{9,8},{10,11... | collective-permute-start | bytes 638984 | tf_op jit(solution)/shard_map/ppermute | solution.py:316
  32.5 8.3 %collective-permute-start.10 = (s16[400,512]{1,0:T(8,128)(2,1)S(1)}, s16[400,512]{1,0:T(8,128)(2,1)S(1)}, u32[]{:S(2)}, u32[]{:S(2)}) collective-permute-start(s16[400,512]{1,0:T(8,128)(2,1)S(1)} %hop3.2), channel_id=1, source_target_pairs={{0,4},{1,29},{2,6},{3,31},{4,8},{5,1},{6,10},{7,3},{8,12},{9,5},{1... | collective-permute-start | bytes 1228808 | tf_op jit(solution)/shard_map/ppermute | solution.py:316
  35.4 10.5 %collective-permute-start.20 = (s16[400,512]{1,0:T(8,128)(2,1)S(1)}, s16[400,512]{1,0:T(8,128)(2,1)S(1)}, u32[]{:S(2)}, u32[]{:S(2)}) collective-permute-start(s16[400,512]{1,0:T(8,128)(2,1)S(1)} %hop3.3), channel_id=1, source_target_pairs={{0,4},{1,29},{2,6},{3,31},{4,8},{5,1},{6,10},{7,3},{8,12},{9,5},{1... | collective-permute-start | bytes 1228808 | tf_op jit(solution)/shard_map/ppermute | solution.py:316
  37.5 1.6 %collective-permute-start.6 = (s16[208,512]{1,0:T(8,128)(2,1)S(1)}, s16[208,512]{1,0:T(8,128)(2,1)S(1)}, u32[]{:S(2)}, u32[]{:S(2)}) collective-permute-start(s16[208,512]{1,0:T(8,128)(2,1)S(1)} %get-tuple-element.53), channel_id=1, source_target_pairs={{0,1},{1,0},{2,3},{3,2},{4,5},{5,4},{6,7},{7,6},{8,9},{9,8},{10,11... | collective-permute-start | bytes 638984 | tf_op jit(solution)/shard_map/ppermute | solution.py:316
  37.9 2.7 %collective-permute-start.15 = (s16[208,512]{1,0:T(8,128)(2,1)S(1)}, s16[208,512]{1,0:T(8,128)(2,1)S(1)}, u32[]{:S(2)}, u32[]{:S(2)}) collective-permute-start(s16[208,512]{1,0:T(8,128)(2,1)S(1)} %get-tuple-element.64), channel_id=1, source_target_pairs={{0,1},{1,0},{2,3},{3,2},{4,5},{5,4},{6,7},{7,6},{8,9},{9,8},{10,11... | collective-permute-start | bytes 638984 | tf_op jit(solution)/shard_map/ppermute | solution.py:316
  38.0 2.6 %collective-permute-start.16 = (s16[208,512]{1,0:T(8,128)(2,1)S(1)}, s16[208,512]{1,0:T(8,128)(2,1)S(1)}, u32[]{:S(2)}, u32[]{:S(2)}) collective-permute-start(s16[208,512]{1,0:T(8,128)(2,1)S(1)} %get-tuple-element.65), channel_id=1, source_target_pairs={{0,1},{1,0},{2,3},{3,2},{4,5},{5,4},{6,7},{7,6},{8,9},{9,8},{10,11... | collective-permute-start | bytes 638984 | tf_op jit(solution)/shard_map/ppermute | solution.py:316
  39.1 15.9 %collective-permute-start.3 = (s16[208,512]{1,0:T(8,128)(2,1)S(1)}, s16[208,512]{1,0:T(8,128)(2,1)S(1)}, u32[]{:S(2)}, u32[]{:S(2)}) collective-permute-start(s16[208,512]{1,0:T(8,128)(2,1)S(1)} %own.1._), channel_id=1, source_target_pairs={{0,2},{1,3},{2,0},{3,1},{4,6},{5,7},{6,4},{7,5},{8,10},{9,11},{10,... | collective-permute-start | bytes 638984 | tf_op jit(solution)/shard_map/ppermute | solution.py:316
  40.8 9.4 %copy-start.7 = (s32[1,3,8,128]{3,2,1,0:T(8,128)S(1)}, s32[1,3,8,128]{3,2,1,0:T(8,128)}, u32[]{:S(2)}) copy-start(s32[1,3,8,128]{3,2,1,0:T(8,128)} %param.12) | copy-start | bytes 36868
  40.8 16.8 %copy-start = (bf16[2,256,256]{2,1,0:T(8,128)(2,1)S(1)}, bf16[2,256,256]{2,1,0:T(8,128)(2,1)}, u32[]{:S(2)}) copy-start(bf16[2,256,256]{2,1,0:T(8,128)(2,1)} %constant.12.clone.refs_13_.cols) | copy-start | bytes 786436
  40.8 16.8 %copy-start.1 = (bf16[2,192,192]{2,1,0:T(8,128)(2,1)S(1)}, bf16[2,192,192]{2,1,0:T(8,128)(2,1)}, u32[]{:S(2)}) copy-start(bf16[2,192,192]{2,1,0:T(8,128)(2,1)} %constant.11.clone.refs_12_.rows_t) | copy-start | bytes 442372
  40.8 16.8 %copy-start.3 = (f32[1,192,512]{2,1,0:T(8,128)S(1)}, f32[1,192,512]{2,1,0:T(8,128)}, u32[]{:S(2)}) copy-start(f32[1,192,512]{2,1,0:T(8,128)} %param.11) | copy-start | bytes 1179652
  40.8 16.8 %copy-start.4 = (bf16[2,256,256]{2,1,0:T(8,128)(2,1)S(1)}, bf16[2,256,256]{2,1,0:T(8,128)(2,1)}, u32[]{:S(2)}) copy-start(bf16[2,256,256]{2,1,0:T(8,128)(2,1)} %constant.13.clone.refs_14_) | copy-start | bytes 786436
  40.8 16.8 %copy-start.5 = (bf16[2,192,192]{2,1,0:T(8,128)(2,1)S(1)}, bf16[2,192,192]{2,1,0:T(8,128)(2,1)}, u32[]{:S(2)}) copy-start(bf16[2,192,192]{2,1,0:T(8,128)(2,1)} %constant.10.clone.refs_11_) | copy-start | bytes 442372
  41.2 13.8 %collective-permute-start.11 = (s16[208,512]{1,0:T(8,128)(2,1)S(1)}, s16[208,512]{1,0:T(8,128)(2,1)S(1)}, u32[]{:S(2)}, u32[]{:S(2)}) collective-permute-start(s16[208,512]{1,0:T(8,128)(2,1)S(1)} %get-tuple-element.57), channel_id=1, source_target_pairs={{0,6},{1,31},{2,4},{3,29},{4,10},{5,3},{6,8},{7,1},{8,14},{9,7},{1... | collective-permute-start | bytes 638984 | tf_op jit(solution)/shard_map/ppermute | solution.py:316
  44.0 11.0 %collective-permute-start.12 = (s16[208,512]{1,0:T(8,128)(2,1)S(1)}, s16[208,512]{1,0:T(8,128)(2,1)S(1)}, u32[]{:S(2)}, u32[]{:S(2)}) collective-permute-start(s16[208,512]{1,0:T(8,128)(2,1)S(1)} %get-tuple-element.58), channel_id=1, source_target_pairs={{0,7},{1,30},{2,5},{3,28},{4,11},{5,2},{6,9},{7,0},{8,15},{9,6},{1... | collective-permute-start | bytes 638984 | tf_op jit(solution)/shard_map/ppermute | solution.py:316
  46.3 8.7 %collective-permute-start.21 = (s16[208,512]{1,0:T(8,128)(2,1)S(1)}, s16[208,512]{1,0:T(8,128)(2,1)S(1)}, u32[]{:S(2)}, u32[]{:S(2)}) collective-permute-start(s16[208,512]{1,0:T(8,128)(2,1)S(1)} %get-tuple-element.69), channel_id=1, source_target_pairs={{0,4},{1,29},{2,6},{3,31},{4,8},{5,1},{6,10},{7,3},{8,12},{9,5},{1... | collective-permute-start | bytes 638984 | tf_op jit(solution)/shard_map/ppermute | solution.py:316
  47.4 10.2 %collective-permute-start.22 = (s16[208,512]{1,0:T(8,128)(2,1)S(1)}, s16[208,512]{1,0:T(8,128)(2,1)S(1)}, u32[]{:S(2)}, u32[]{:S(2)}) collective-permute-start(s16[208,512]{1,0:T(8,128)(2,1)S(1)} %get-tuple-element.70), channel_id=1, source_target_pairs={{0,5},{1,28},{2,7},{3,30},{4,9},{5,0},{6,11},{7,2},{8,13},{9,4},{1... | collective-permute-start | bytes 638984 | tf_op jit(solution)/shard_map/ppermute | solution.py:316

commit v8 on v7

--- a/solution.py
+++ b/solution.py
@@ -106,7 +106,8 @@
 
 EARLY = (4, -3)
 LATE = (-2, -1)
-KEPT = (3, 2, 1, 0)
+KEPT = (3, 2, 1)
+OWN = (0,)
 
 
 def loads(steps, swap, inputs, blocks, sems):
@@ -159,20 +160,23 @@
         copy.wait()
 
 
-def kept_kernel(then, inputs, grads, blocks, _, *refs):
-    keeps, (keep0, away0, ahead, sums, out_sems, both, sems) = refs[:3], refs[3:]
+def kept_kernel(swap, then, inputs, grads, blocks, _, *refs):
+    keeps, (keep0, away0, ahead, sums, out_sems, both, own, own_sem, sems) = refs[:3], refs[3:]
+    mine, = loads(OWN, swap, inputs, own, own_sem)
+    mine.start()
     more = loads(*then, inputs, ahead, sems)
     for copy in more:
         copy.start()
-    core = place()[2]
-    both[...] = product(blocks[3], grads[...])
-    keep0[...] = both[pl.ds(pl.multiple_of(core * ROWS, ROWS), ROWS), :]
-    encode(both[pl.ds(pl.multiple_of((1 - core) * ROWS, ROWS), ROWS), :], away0)
     copies = []
     for n, keep in enumerate(keeps):
         sums[n] = product(blocks[n], grads[...])
         copies.append(pltpu.make_async_copy(sums.at[n], keep, out_sems.at[n]))
         copies[n].start()
+    core = place()[2]
+    mine.wait()
+    both[...] = product(own[0], grads[...])
+    keep0[...] = both[pl.ds(pl.multiple_of(core * ROWS, ROWS), ROWS), :]
+    encode(both[pl.ds(pl.multiple_of((1 - core) * ROWS, ROWS), ROWS), :], away0)
     for copy in copies + more:
         copy.wait()
 
@@ -234,12 +238,12 @@
     keep4, away, ahead = partial_sums(
         early_kernel, args(ahead, behind), early + [fetched(KEPT)], [both, sems(KEPT)], 2, "early")
     behind = yield keep4, away
-    sums = [vmem((3, *tall), F32), pltpu.SemaphoreType.DMA((3,)), both]
+    sums = [vmem((3, *tall), F32), sems(KEPT), both, vmem((1, tokens, BOTH), BF), sems(OWN)]
     *keeps, ahead = partial_sums(
-        lambda *refs: kept_kernel((KEPT, False), *refs), args(ahead, behind), kept + [fetched(KEPT)], sums + [sems(KEPT)], 4, "kept")
+        lambda *refs: kept_kernel(True, (KEPT, False), *refs), args(ahead, behind), kept + [fetched(KEPT)], sums + [sems(KEPT)], 4, "kept")
     behind = yield keeps
     *keeps, ahead = partial_sums(
-        lambda *refs: kept_kernel((LATE, True), *refs), args(ahead, behind), kept + [fetched(LATE)], sums + [sems(LATE)], 4, "kept")
+        lambda *refs: kept_kernel(False, (LATE, True), *refs), args(ahead, behind), kept + [fetched(LATE)], sums + [sems(LATE)], 4, "kept")
     behind = yield keeps
     *away, ahead = partial_sums(
         lambda *refs: late_kernel((LATE, False), *refs), args(ahead, behind), late + [fetched(LATE)], [sems(LATE)], 2, "late")
@@ -276,7 +280,7 @@
     return jnp.concatenate([decode(low), decode(high)], axis=0)
 
 
-def first_hop_kernel(keep, other, out):
+def first_hop_kernel(keep, other, _, out):
     half = keep.shape[1]
     encode(keep[...] + decode_pair(other.at[:, :half], other.at[:, half:]), out)
 
@@ -318,8 +322,8 @@
     def unit(n):
         return (None, short, breadth), (n, 0, 0)
 
-    def first_hop(keep, other):
-        return call_local(first_hop_kernel, (keep, other), (None, unit(0)), [((tall, breadth // 2), I16)], "hop1")[0]
+    def first_hop(keep, other, after):
+        return call_local(first_hop_kernel, (keep, other, after), (None, unit(0), ANYWHERE), [((tall, breadth // 2), I16)], "hop1")[0]
 
     def second_hop(keep, other, arrived, after):
         return call_local(
@@ -343,9 +347,9 @@
     early_a = send(away, WITHIN)
     keep4_b, away = sums.send(away)
     early_b = send(away, WITHIN)
-    ring_a = first_hop(keep4_a, early_a)
-    ring_b = first_hop(keep4_b, early_b)
-    *kept_a, keep0_a, away0 = sums.send(ring_a)
+    ring_a = first_hop(keep4_a, early_a, keep4_a)
+    ring_b = first_hop(keep4_b, early_b, ring_a)
+    *kept_a, keep0_a, away0 = sums.send(ring_b)
     away0_a = send(away0, WITHIN)
     *kept_b, keep0_b, away0 = sums.send(kept_a[0])
     away0_b = send(away0, WITHIN)

time: 78 us -> 76 us (0.974)
  Pallas kernels: 22.9 us -> 21.3 us
  waiting for transfers between devices: 7.6 us -> 9.06 us
  local copies, waits for them, and re-layouts: 2.59 us -> 1.17 us
  blocking collectives: 14.5 us -> 13.7 us
    pallas_call x6, Pallas kernels: 13.8 us -> 12.2 us  [partial_sums(): pl.pallas_call(kernel, in_specs=[pl.BlockSpec(memory_space=space) for _,...]
    ppermute x23, waiting for transfers between devices: 7.6 us -> 9.06 us  [send(): return lax.ppermute(array, 'fsdp', pairs)]
    unnamed x16 -> x14, local copies, waits for them, and re-layouts: 2.59 us -> 1.17 us
    all_to_all x1, blocking collectives: 14.5 us -> 13.7 us  [body(): gathered = lax.all_to_all(payload, 'rep', 0, 0)]
  transfers between devices with their start and end apart: 23 -> 23, of which waited for: 3 -> 4; matrix products, arithmetic and copies ran while one was open for 0% -> 0% of each run, Pallas kernels for 19% -> 17%
where the time goes in v8:
time: 76 us; the launch traced here: 75.7 us
  starting transfers between devices  28.9 us (38%)
  Pallas kernels  21.3 us (28%)
  blocking collectives  13.7 us (18%)
  waiting for transfers between devices  9.06 us (12%)
  between operations  1.63 us (2%)
  local copies, waits for them, and re-layouts  1.17 us (2%)
    ppermute x23, starting transfers between devices, send(): return lax.ppermute(array, 'fsdp', pairs)  28.9 us
    all_to_all x1, blocking collectives, body(): gathered = lax.all_to_all(payload, 'rep', 0, 0)  13.7 us
    pallas_call x6, Pallas kernels, partial_sums(): pl.pallas_call(kernel, in_specs=[pl.BlockSpec(memory_space=space) for _,...  12.2 us
    ppermute x23, waiting for transfers between devices, send(): return lax.ppermute(array, 'fsdp', pairs)  9.06 us
    pallas_call x14, Pallas kernels, call_local(): pl.pallas_call(kernel, grid=(1,), in_specs=[spec(arg, cut) for arg, cut i...  3.5 us
    pallas_call x1, Pallas kernels, body(): pl.pallas_call(decode_kernel, out_shape=jax.ShapeDtypeStruct((height, bre...  3.12 us
    pallas_call x1, Pallas kernels, body(): pl.pallas_call(pick_kernel, out_shape=[jax.ShapeDtypeStruct((height, brea...  2.44 us
  transfers between devices with their start and end apart: 23, of which 4 were waited for; matrix products, arithmetic and copies ran while one was open for 0% of the time, Pallas kernels for 17%

profile of v8, /device:TPU:1, one launch (start us, length us, event | category | flops | bytes accessed | tf_op | source)
XLA Modules:
  0.0 75.7 jit_solution(14201931757015435280)
XLA Ops:
  0.6 1.1 %copy-done.2 = bf16[1,768,512]{2,1,0:T(8,128)(2,1)S(1)} copy-done((bf16[1,768,512]{2,1,0:T(8,128)(2,1)S(1)}, bf16[1,768,512]{2,1,0:T(8,128)(2,1)}, u32[]{:S(2)}) %copy-start.2) | copy-done | bytes 786456
  1.8 2.5 %early.2 = (f32[384,256]{1,0:T(8,128)S(1)}, s16[3,208,512]{2,1,0:T(8,128)(2,1)S(1)}, bf16[768,512]{1,0:T(8,128)(2,1)S(1)}, bf16[2,768,384]{2,1,0:T(8,128)(2,1)S(1)}) custom-call(bf16[768,6144]{1,0:T(8,128)(2,1)} %bitcast.10, bf16[768,512]{1,0:T(8,128)(2,1)S(1)} %bitcast.8), custom_call_target="tpu_custom_call" | custom-call | flops 2717908992 | bytes 2949120 | tf_op jit(solution)/shard_map/early/pallas_call | solution.py:199
  4.2 3.3 %collective-permute-start.1 = (s16[3,208,512]{2,1,0:T(8,128)(2,1)S(1)}, s16[3,208,512]{2,1,0:T(8,128)(2,1)S(1)}, u32[]{:S(2)}, u32[]{:S(2)}) collective-permute-start(s16[3,208,512]{2,1,0:T(8,128)(2,1)S(1)} %get-tuple-element.41._), channel_id=1, source_target_pairs={{0,1},{1,0},{2,3},{3,2},{4,5},{5,4},{6,7},{7,6},{8,9},{9,8},{10,11... | collective-permute-start | bytes 1916936 | tf_op jit(solution)/shard_map/ppermute | solution.py:320
  7.6 2.2 %early.3 = (f32[384,256]{1,0:T(8,128)S(1)}, s16[3,208,512]{2,1,0:T(8,128)(2,1)S(1)}, bf16[3,768,384]{2,1,0:T(8,128)(2,1)S(1)}) custom-call(bf16[768,6144]{1,0:T(8,128)(2,1)} %bitcast.11, bf16[768,512]{1,0:T(8,128)(2,1)S(1)} %get-tuple-element.39.grads.refs_1_, bf16[2,768,384]{2,1,0:T(8,128)(2,1)S(1)} %get-tuple-element.40.blocks, ...), custom_call_target="tpu_custom_call" | custom-call | flops 1811939328 | bytes 1966080 | tf_op jit(solution)/shard_map/early/pallas_call | solution.py:199
  10.0 3.9 %collective-permute-start.5 = (s16[400,256]{1,0:T(8,128)(2,1)S(1)}, s16[400,256]{1,0:T(8,128)(2,1)S(1)}, u32[]{:S(2)}, u32[]{:S(2)}) collective-permute-start(s16[400,256]{1,0:T(8,128)(2,1)S(1)} %hop1.2._), channel_id=1, source_target_pairs={{0,4},{1,29},{2,6},{3,31},{4,8},{5,1},{6,10},{7,3},{8,12},{9,5},{1... | collective-permute-start | bytes 614408 | tf_op jit(solution)/shard_map/ppermute | solution.py:320
  14.1 1.9 %collective-permute-start.14 = (s16[400,256]{1,0:T(8,128)(2,1)S(1)}, s16[400,256]{1,0:T(8,128)(2,1)S(1)}, u32[]{:S(2)}, u32[]{:S(2)}) collective-permute-start(s16[400,256]{1,0:T(8,128)(2,1)S(1)} %hop1.3.refs_3_), channel_id=1, source_target_pairs={{0,4},{1,29},{2,6},{3,31},{4,8},{5,1},{6,10},{7,3},{8,12},{9,5},{1... | collective-permute-start | bytes 614408 | tf_op jit(solution)/shard_map/ppermute | solution.py:320
  16.0 2.4 %kept.2 = (f32[384,512]{1,0:T(8,128)S(1)}, f32[384,512]{1,0:T(8,128)S(1)}, f32[384,512]{1,0:T(8,128)S(1)}, f32[192,512]{1,0:T(8,128)S(1)}, s16[208,512]{1,0:T(8,...) custom-call(bf16[768,6144]{1,0:T(8,128)(2,1)} %bitcast.12, bf16[768,512]{1,0:T(8,128)(2,1)S(1)} %get-tuple-element.39.grads.refs_1_, ...), custom_call_target="tpu_custom_call" | custom-call | flops 3623878656 | bytes 3932160 | tf_op jit(solution)/shard_map/kept/pallas_call | solution.py:199
  18.5 2.4 %kept.3 = (f32[384,512]{1,0:T(8,128)S(1)}, f32[384,512]{1,0:T(8,128)S(1)}, f32[384,512]{1,0:T(8,128)S(1)}, f32[192,512]{1,0:T(8,128)S(1)}, s16[208,512]{1,0:T(8,...) custom-call(bf16[768,6144]{1,0:T(8,128)(2,1)} %bitcast.13, bf16[768,512]{1,0:T(8,128)(2,1)S(1)} %get-tuple-element.39.grads.refs_1_, ...), custom_call_target="tpu_custom_call" | custom-call | flops 3623878656 | bytes 3932160 | tf_op jit(solution)/shard_map/kept/pallas_call | solution.py:199
  20.8 0.5 hop2.2.refs_3_
  21.3 0.8 %collective-permute-start.10 = (s16[400,512]{1,0:T(8,128)(2,1)S(1)}, s16[400,512]{1,0:T(8,128)(2,1)S(1)}, u32[]{:S(2)}, u32[]{:S(2)}) collective-permute-start(s16[400,512]{1,0:T(8,128)(2,1)S(1)} %hop2.2.refs_3_), channel_id=1, source_target_pairs={{0,4},{1,29},{2,6},{3,31},{4,8},{5,1},{6,10},{7,3},{8,12},{9,5},{1... | collective-permute-start | bytes 1228808 | tf_op jit(solution)/shard_map/ppermute | solution.py:320
  22.1 1.9 %late.2 = (s16[208,512]{1,0:T(8,128)(2,1)S(1)}, s16[208,512]{1,0:T(8,128)(2,1)S(1)}, s16[208,512]{1,0:T(8,128)(2,1)S(1)}, s16[208,512]{1,0:T(8,128)(2,1)S(1)}, bf16[2,768,384]{2,1,0:T(8,128)(2,1)S(1)}) custom-call(bf16[768,6144]{1,0:T(8,128)(2,1)} %bitcast.14, bf16[768,512]{1,0:T(8,128)(2,1)S(1)} %get-tuple-element.39.grads.refs_1_, ...), custom_call_target="tpu_custom_call" | custom-call | flops 1811939328 | bytes 1966080 | tf_op jit(solution)/shard_map/late/pallas_call | solution.py:199
  24.1 0.5 collective-permute-start.9
  24.7 0.5 hop2.3.refs_3_
  25.2 2.6 %collective-permute-start.19 = (s16[400,512]{1,0:T(8,128)(2,1)S(1)}, s16[400,512]{1,0:T(8,128)(2,1)S(1)}, u32[]{:S(2)}, u32[]{:S(2)}) collective-permute-start(s16[400,512]{1,0:T(8,128)(2,1)S(1)} %hop2.3.refs_3_), channel_id=1, source_target_pairs={{0,4},{1,29},{2,6},{3,31},{4,8},{5,1},{6,10},{7,3},{8,12},{9,5},{1... | collective-permute-start | bytes 1228808 | tf_op jit(solution)/shard_map/ppermute | solution.py:320
  27.8 0.9 %late.3 = (s16[208,512]{1,0:T(8,128)(2,1)S(1)}, s16[208,512]{1,0:T(8,128)(2,1)S(1)}, s16[208,512]{1,0:T(8,128)(2,1)S(1)}, s16[208,512]{1,0:T(8,128)(2,1)S(1)}) custom-call(bf16[768,6144]{1,0:T(8,128)(2,1)} %bitcast.15, bf16[768,512]{1,0:T(8,128)(2,1)S(1)} %get-tuple-element.39.grads.refs_1_, bf16[2,768,384]{2,1,0:T(8,128)(2,1)S(1)} %get-tuple-element.62.refs_2_, ...), custom_call_target="tpu_custom_call" | custom-call | flops 1811939328 | bytes 1966080 | tf_op jit(solution)/shard_map/late/pallas_call | solution.py:199
  28.8 0.5 collective-permute-start.18
  29.4 1.6 %collective-permute-start.6 = (s16[208,512]{1,0:T(8,128)(2,1)S(1)}, s16[208,512]{1,0:T(8,128)(2,1)S(1)}, u32[]{:S(2)}, u32[]{:S(2)}) collective-permute-start(s16[208,512]{1,0:T(8,128)(2,1)S(1)} %get-tuple-element.54), channel_id=1, source_target_pairs={{0,1},{1,0},{2,3},{3,2},{4,5},{5,4},{6,7},{7,6},{8,9},{9,8},{10,11... | collective-permute-start | bytes 638984 | tf_op jit(solution)/shard_map/ppermute | solution.py:320
  31.6 1.3 %collective-permute-done.19.arrived = s16[400,512]{1,0:T(8,128)(2,1)S(1)} collective-permute-done((s16[400,512]{1,0:T(8,128)(2,1)S(1)}, s16[400,512]{1,0:T(8,128)(2,1)S(1)}, u32[]{:S(2)}, u32[]{:S(2)}) %collective-permute-start.19) | collective-permute-done | bytes 409632 | tf_op jit(solution)/shard_map/ppermute | solution.py:320
  33.1 3.0 %collective-permute-start.20 = (s16[400,512]{1,0:T(8,128)(2,1)S(1)}, s16[400,512]{1,0:T(8,128)(2,1)S(1)}, u32[]{:S(2)}, u32[]{:S(2)}) collective-permute-start(s16[400,512]{1,0:T(8,128)(2,1)S(1)} %hop3.3), channel_id=1, source_target_pairs={{0,4},{1,29},{2,6},{3,31},{4,8},{5,1},{6,10},{7,3},{8,12},{9,5},{1... | collective-permute-start | bytes 1228808 | tf_op jit(solution)/shard_map/ppermute | solution.py:320
  36.1 0.5 collective-permute-start.15
  37.6 1.3 %collective-permute-start.4 = (s16[208,512]{1,0:T(8,128)(2,1)S(1)}, s16[208,512]{1,0:T(8,128)(2,1)S(1)}, u32[]{:S(2)}, u32[]{:S(2)}) collective-permute-start(s16[208,512]{1,0:T(8,128)(2,1)S(1)} %own.1._), channel_id=1, source_target_pairs={{0,2},{1,3},{2,0},{3,1},{4,6},{5,7},{6,4},{7,5},{8,10},{9,11},{10,... | collective-permute-start | bytes 638984 | tf_op jit(solution)/shard_map/ppermute | solution.py:320
  39.2 0.4 hop4.2
  39.6 2.6 %collective-permute-start.12 = (s16[208,512]{1,0:T(8,128)(2,1)S(1)}, s16[208,512]{1,0:T(8,128)(2,1)S(1)}, u32[]{:S(2)}, u32[]{:S(2)}) collective-permute-start(s16[208,512]{1,0:T(8,128)(2,1)S(1)} %get-tuple-element.59), channel_id=1, source_target_pairs={{0,6},{1,31},{2,4},{3,29},{4,10},{5,3},{6,8},{7,1},{8,14},{9,7},{1... | collective-permute-start | bytes 638984 | tf_op jit(solution)/shard_map/ppermute | solution.py:320
  42.1 2.7 %collective-permute-start.13 = (s16[208,512]{1,0:T(8,128)(2,1)S(1)}, s16[208,512]{1,0:T(8,128)(2,1)S(1)}, u32[]{:S(2)}, u32[]{:S(2)}) collective-permute-start(s16[208,512]{1,0:T(8,128)(2,1)S(1)} %get-tuple-element.60), channel_id=1, source_target_pairs={{0,7},{1,30},{2,5},{3,28},{4,11},{5,2},{6,9},{7,0},{8,15},{9,6},{1... | collective-permute-start | bytes 638984 | tf_op jit(solution)/shard_map/ppermute | solution.py:320
  44.8 0.3 hop4.3
  45.5 2.8 %collective-permute-start.22 = (s16[208,512]{1,0:T(8,128)(2,1)S(1)}, s16[208,512]{1,0:T(8,128)(2,1)S(1)}, u32[]{:S(2)}, u32[]{:S(2)}) collective-permute-start(s16[208,512]{1,0:T(8,128)(2,1)S(1)} %get-tuple-element.70), channel_id=1, source_target_pairs={{0,5},{1,28},{2,7},{3,30},{4,9},{5,0},{6,11},{7,2},{8,13},{9,4},{1... | collective-permute-start | bytes 638984 | tf_op jit(solution)/shard_map/ppermute | solution.py:320
  48.3 0.6 hot.1
  48.9 4.3 %collective-permute-done.4.refs_1_ = s16[208,512]{1,0:T(8,128)(2,1)S(1)} collective-permute-done((s16[208,512]{1,0:T(8,128)(2,1)S(1)}, s16[208,512]{1,0:T(8,128)(2,1)S(1)}, u32[]{:S(2)}, u32[]{:S(2)}) %collective-permute-start.4) | collective-permute-done | bytes 213024 | tf_op jit(solution)/shard_map/ppermute | solution.py:320
  53.2 3.2 %collective-permute-done.22.refs_5_ = s16[208,512]{1,0:T(8,128)(2,1)S(1)} collective-permute-done((s16[208,512]{1,0:T(8,128)(2,1)S(1)}, s16[208,512]{1,0:T(8,128)(2,1)S(1)}, u32[]{:S(2)}, u32[]{:S(2)}) %collective-permute-start.22) | collective-permute-done | bytes 213024 | tf_op jit(solution)/shard_map/ppermute | solution.py:320
  56.4 2.4 %pick.1 = (f32[192,512]{1,0:T(8,128)}, f32[8,48,128]{2,1,0:T(8,128)S(1)}) custom-call(f32[192,512]{1,0:T(8,128)S(1)} %get-tuple-element.48.kept, s16[208,512]{1,0:T(8,128)(2,1)S(1)} %collective-permute-done.2._.refs_0_, s16[208,512]{1,0:T(8,128)(2,1)S(1)} %collective-permute-done.4.refs_1_, s16[208,512]{1,0:T(8,128)(2,1)S(1)} %collective-permute-done.12.refs_2_, ...), custom_call_target="tpu_custom_call" | custom-call | tf_op jit(solution)/shard_map/pick/pallas_call | solution.py:466
  58.9 13.7 %all_to_all.5.gathered = f32[8,48,128]{2,1,0:T(8,128)S(1)} all-to-all(f32[8,48,128]{2,1,0:T(8,128)S(1)} %get-tuple-element.75), channel_id=1, replica_groups=mesh['rep'=8,'fsdp'=32] {'rep'}, dimensions={0} | all-to-all | bytes 393216 | tf_op jit(solution)/shard_map/all_to_all | solution.py:476
  72.6 3.1 %decode.1 = f32[192,512]{1,0:T(8,128)} custom-call(f32[8,48,128]{2,1,0:T(8,128)S(1)} %all_to_all.5.gathered, bf16[2,192,192]{2,1,0:T(8,128)(2,1)S(1)} %copy-done.1, bf16[2,256,256]{2,1,0:T(8,128)(2,1)S(1)} %copy-done), custom_call_target="tpu_custom_call" | custom-call | tf_op jit(solution)/shard_map/decode/pallas_call | solution.py:477
  (53 shorter events, 2.5 us)
Async XLA Ops:
  0.6 1.1 %copy-start.2 = (bf16[1,768,512]{2,1,0:T(8,128)(2,1)S(1)}, bf16[1,768,512]{2,1,0:T(8,128)(2,1)}, u32[]{:S(2)}) copy-start(bf16[1,768,512]{2,1,0:T(8,128)(2,1)} %param.10) | copy-start | bytes 2359300
  4.2 5.7 %collective-permute-start.1 = (s16[3,208,512]{2,1,0:T(8,128)(2,1)S(1)}, s16[3,208,512]{2,1,0:T(8,128)(2,1)S(1)}, u32[]{:S(2)}, u32[]{:S(2)}) collective-permute-start(s16[3,208,512]{2,1,0:T(8,128)(2,1)S(1)} %get-tuple-element.41._), channel_id=1, source_target_pairs={{0,1},{1,0},{2,3},{3,2},{4,5},{5,4},{6,7},{7,6},{8,9},{9,8},{10,11... | collective-permute-start | bytes 1916936 | tf_op jit(solution)/shard_map/ppermute | solution.py:320
  9.8 4.2 %collective-permute-start = (s16[3,208,512]{2,1,0:T(8,128)(2,1)S(1)}, s16[3,208,512]{2,1,0:T(8,128)(2,1)S(1)}, u32[]{:S(2)}, u32[]{:S(2)}) collective-permute-start(s16[3,208,512]{2,1,0:T(8,128)(2,1)S(1)} %get-tuple-element.44), channel_id=1, source_target_pairs={{0,1},{1,0},{2,3},{3,2},{4,5},{5,4},{6,7},{7,6},{8,9},{9,8},{10,11... | collective-permute-start | bytes 1916936 | tf_op jit(solution)/shard_map/ppermute | solution.py:320
  10.0 10.8 %collective-permute-start.5 = (s16[400,256]{1,0:T(8,128)(2,1)S(1)}, s16[400,256]{1,0:T(8,128)(2,1)S(1)}, u32[]{:S(2)}, u32[]{:S(2)}) collective-permute-start(s16[400,256]{1,0:T(8,128)(2,1)S(1)} %hop1.2._), channel_id=1, source_target_pairs={{0,4},{1,29},{2,6},{3,31},{4,8},{5,1},{6,10},{7,3},{8,12},{9,5},{1... | collective-permute-start | bytes 614408 | tf_op jit(solution)/shard_map/ppermute | solution.py:320
  14.1 10.6 %collective-permute-start.14 = (s16[400,256]{1,0:T(8,128)(2,1)S(1)}, s16[400,256]{1,0:T(8,128)(2,1)S(1)}, u32[]{:S(2)}, u32[]{:S(2)}) collective-permute-start(s16[400,256]{1,0:T(8,128)(2,1)S(1)} %hop1.3.refs_3_), channel_id=1, source_target_pairs={{0,4},{1,29},{2,6},{3,31},{4,8},{5,1},{6,10},{7,3},{8,12},{9,5},{1... | collective-permute-start | bytes 614408 | tf_op jit(solution)/shard_map/ppermute | solution.py:320
  18.4 6.2 %collective-permute-start.3 = (s16[208,512]{1,0:T(8,128)(2,1)S(1)}, s16[208,512]{1,0:T(8,128)(2,1)S(1)}, u32[]{:S(2)}, u32[]{:S(2)}) collective-permute-start(s16[208,512]{1,0:T(8,128)(2,1)S(1)} %get-tuple-element.51), channel_id=1, source_target_pairs={{0,1},{1,0},{2,3},{3,2},{4,5},{5,4},{6,7},{7,6},{8,9},{9,8},{10,11... | collective-permute-start | bytes 638984 | tf_op jit(solution)/shard_map/ppermute | solution.py:320
  21.3 8.1 %collective-permute-start.10 = (s16[400,512]{1,0:T(8,128)(2,1)S(1)}, s16[400,512]{1,0:T(8,128)(2,1)S(1)}, u32[]{:S(2)}, u32[]{:S(2)}) collective-permute-start(s16[400,512]{1,0:T(8,128)(2,1)S(1)} %hop2.2.refs_3_), channel_id=1, source_target_pairs={{0,4},{1,29},{2,6},{3,31},{4,8},{5,1},{6,10},{7,3},{8,12},{9,5},{1... | collective-permute-start | bytes 1228808 | tf_op jit(solution)/shard_map/ppermute | solution.py:320
  24.0 4.8 %collective-permute-start.8 = (s16[208,512]{1,0:T(8,128)(2,1)S(1)}, s16[208,512]{1,0:T(8,128)(2,1)S(1)}, u32[]{:S(2)}, u32[]{:S(2)}) collective-permute-start(s16[208,512]{1,0:T(8,128)(2,1)S(1)} %get-tuple-element.57), channel_id=1, source_target_pairs={{0,1},{1,0},{2,3},{3,2},{4,5},{5,4},{6,7},{7,6},{8,9},{9,8},{10,11... | collective-permute-start | bytes 638984 | tf_op jit(solution)/shard_map/ppermute | solution.py:320
  24.1 5.2 %collective-permute-start.9 = (s16[208,512]{1,0:T(8,128)(2,1)S(1)}, s16[208,512]{1,0:T(8,128)(2,1)S(1)}, u32[]{:S(2)}, u32[]{:S(2)}) collective-permute-start(s16[208,512]{1,0:T(8,128)(2,1)S(1)} %get-tuple-element.58), channel_id=1, source_target_pairs={{0,1},{1,0},{2,3},{3,2},{4,5},{5,4},{6,7},{7,6},{8,9},{9,8},{10,11... | collective-permute-start | bytes 638984 | tf_op jit(solution)/shard_map/ppermute | solution.py:320
  25.2 7.7 %collective-permute-start.19 = (s16[400,512]{1,0:T(8,128)(2,1)S(1)}, s16[400,512]{1,0:T(8,128)(2,1)S(1)}, u32[]{:S(2)}, u32[]{:S(2)}) collective-permute-start(s16[400,512]{1,0:T(8,128)(2,1)S(1)} %hop2.3.refs_3_), channel_id=1, source_target_pairs={{0,4},{1,29},{2,6},{3,31},{4,8},{5,1},{6,10},{7,3},{8,12},{9,5},{1... | collective-permute-start | bytes 1228808 | tf_op jit(solution)/shard_map/ppermute | solution.py:320
  28.7 2.7 %collective-permute-start.17 = (s16[208,512]{1,0:T(8,128)(2,1)S(1)}, s16[208,512]{1,0:T(8,128)(2,1)S(1)}, u32[]{:S(2)}, u32[]{:S(2)}) collective-permute-start(s16[208,512]{1,0:T(8,128)(2,1)S(1)} %get-tuple-element.67), channel_id=1, source_target_pairs={{0,1},{1,0},{2,3},{3,2},{4,5},{5,4},{6,7},{7,6},{8,9},{9,8},{10,11... | collective-permute-start | bytes 638984 | tf_op jit(solution)/shard_map/ppermute | solution.py:320
  28.8 2.7 %collective-permute-start.18 = (s16[208,512]{1,0:T(8,128)(2,1)S(1)}, s16[208,512]{1,0:T(8,128)(2,1)S(1)}, u32[]{:S(2)}, u32[]{:S(2)}) collective-permute-start(s16[208,512]{1,0:T(8,128)(2,1)S(1)} %get-tuple-element.68), channel_id=1, source_target_pairs={{0,1},{1,0},{2,3},{3,2},{4,5},{5,4},{6,7},{7,6},{8,9},{9,8},{10,11... | collective-permute-start | bytes 638984 | tf_op jit(solution)/shard_map/ppermute | solution.py:320
  29.3 2.3 %collective-permute-start.2 = (s16[208,512]{1,0:T(8,128)(2,1)S(1)}, s16[208,512]{1,0:T(8,128)(2,1)S(1)}, u32[]{:S(2)}, u32[]{:S(2)}) collective-permute-start(s16[208,512]{1,0:T(8,128)(2,1)S(1)} %get-tuple-element.49), channel_id=1, source_target_pairs={{0,1},{1,0},{2,3},{3,2},{4,5},{5,4},{6,7},{7,6},{8,9},{9,8},{10,11... | collective-permute-start | bytes 638984 | tf_op jit(solution)/shard_map/ppermute | solution.py:320
  29.4 7.2 %collective-permute-start.6 = (s16[208,512]{1,0:T(8,128)(2,1)S(1)}, s16[208,512]{1,0:T(8,128)(2,1)S(1)}, u32[]{:S(2)}, u32[]{:S(2)}) collective-permute-start(s16[208,512]{1,0:T(8,128)(2,1)S(1)} %get-tuple-element.54), channel_id=1, source_target_pairs={{0,1},{1,0},{2,3},{3,2},{4,5},{5,4},{6,7},{7,6},{8,9},{9,8},{10,11... | collective-permute-start | bytes 638984 | tf_op jit(solution)/shard_map/ppermute | solution.py:320
  31.4 7.8 %collective-permute-start.11 = (s16[400,512]{1,0:T(8,128)(2,1)S(1)}, s16[400,512]{1,0:T(8,128)(2,1)S(1)}, u32[]{:S(2)}, u32[]{:S(2)}) collective-permute-start(s16[400,512]{1,0:T(8,128)(2,1)S(1)} %hop3.2), channel_id=1, source_target_pairs={{0,4},{1,29},{2,6},{3,31},{4,8},{5,1},{6,10},{7,3},{8,12},{9,5},{1... | collective-permute-start | bytes 1228808 | tf_op jit(solution)/shard_map/ppermute | solution.py:320
  33.1 11.7 %collective-permute-start.20 = (s16[400,512]{1,0:T(8,128)(2,1)S(1)}, s16[400,512]{1,0:T(8,128)(2,1)S(1)}, u32[]{:S(2)}, u32[]{:S(2)}) collective-permute-start(s16[400,512]{1,0:T(8,128)(2,1)S(1)} %hop3.3), channel_id=1, source_target_pairs={{0,4},{1,29},{2,6},{3,31},{4,8},{5,1},{6,10},{7,3},{8,12},{9,5},{1... | collective-permute-start | bytes 1228808 | tf_op jit(solution)/shard_map/ppermute | solution.py:320
  36.1 1.5 %collective-permute-start.7 = (s16[208,512]{1,0:T(8,128)(2,1)S(1)}, s16[208,512]{1,0:T(8,128)(2,1)S(1)}, u32[]{:S(2)}, u32[]{:S(2)}) collective-permute-start(s16[208,512]{1,0:T(8,128)(2,1)S(1)} %get-tuple-element.55), channel_id=1, source_target_pairs={{0,1},{1,0},{2,3},{3,2},{4,5},{5,4},{6,7},{7,6},{8,9},{9,8},{10,11... | collective-permute-start | bytes 638984 | tf_op jit(solution)/shard_map/ppermute | solution.py:320
  36.1 2.9 %collective-permute-start.15 = (s16[208,512]{1,0:T(8,128)(2,1)S(1)}, s16[208,512]{1,0:T(8,128)(2,1)S(1)}, u32[]{:S(2)}, u32[]{:S(2)}) collective-permute-start(s16[208,512]{1,0:T(8,128)(2,1)S(1)} %get-tuple-element.64), channel_id=1, source_target_pairs={{0,1},{1,0},{2,3},{3,2},{4,5},{5,4},{6,7},{7,6},{8,9},{9,8},{10,11... | collective-permute-start | bytes 638984 | tf_op jit(solution)/shard_map/ppermute | solution.py:320
  36.6 2.4 %collective-permute-start.16 = (s16[208,512]{1,0:T(8,128)(2,1)S(1)}, s16[208,512]{1,0:T(8,128)(2,1)S(1)}, u32[]{:S(2)}, u32[]{:S(2)}) collective-permute-start(s16[208,512]{1,0:T(8,128)(2,1)S(1)} %get-tuple-element.65), channel_id=1, source_target_pairs={{0,1},{1,0},{2,3},{3,2},{4,5},{5,4},{6,7},{7,6},{8,9},{9,8},{10,11... | collective-permute-start | bytes 638984 | tf_op jit(solution)/shard_map/ppermute | solution.py:320
  37.6 15.6 %collective-permute-start.4 = (s16[208,512]{1,0:T(8,128)(2,1)S(1)}, s16[208,512]{1,0:T(8,128)(2,1)S(1)}, u32[]{:S(2)}, u32[]{:S(2)}) collective-permute-start(s16[208,512]{1,0:T(8,128)(2,1)S(1)} %own.1._), channel_id=1, source_target_pairs={{0,2},{1,3},{2,0},{3,1},{4,6},{5,7},{6,4},{7,5},{8,10},{9,11},{10,... | collective-permute-start | bytes 638984 | tf_op jit(solution)/shard_map/ppermute | solution.py:320
  39.1 9.2 %copy-start.6 = (s32[1,3,8,128]{3,2,1,0:T(8,128)S(1)}, s32[1,3,8,128]{3,2,1,0:T(8,128)}, u32[]{:S(2)}) copy-start(s32[1,3,8,128]{3,2,1,0:T(8,128)} %param.12) | copy-start | bytes 36868
  39.1 17.3 %copy-start = (bf16[2,256,256]{2,1,0:T(8,128)(2,1)S(1)}, bf16[2,256,256]{2,1,0:T(8,128)(2,1)}, u32[]{:S(2)}) copy-start(bf16[2,256,256]{2,1,0:T(8,128)(2,1)} %constant.12.clone.refs_13_.cols) | copy-start | bytes 786436
  39.1 17.3 %copy-start.1 = (bf16[2,192,192]{2,1,0:T(8,128)(2,1)S(1)}, bf16[2,192,192]{2,1,0:T(8,128)(2,1)}, u32[]{:S(2)}) copy-start(bf16[2,192,192]{2,1,0:T(8,128)(2,1)} %constant.11.clone.refs_12_.rows_t) | copy-start | bytes 442372
  39.2 17.3 %copy-start.3 = (f32[1,192,512]{2,1,0:T(8,128)S(1)}, f32[1,192,512]{2,1,0:T(8,128)}, u32[]{:S(2)}) copy-start(f32[1,192,512]{2,1,0:T(8,128)} %param.11) | copy-start | bytes 1179652
  39.2 17.2 %copy-start.4 = (bf16[2,256,256]{2,1,0:T(8,128)(2,1)S(1)}, bf16[2,256,256]{2,1,0:T(8,128)(2,1)}, u32[]{:S(2)}) copy-start(bf16[2,256,256]{2,1,0:T(8,128)(2,1)} %constant.13.clone.refs_14_) | copy-start | bytes 786436
  39.2 17.2 %copy-start.5 = (bf16[2,192,192]{2,1,0:T(8,128)(2,1)S(1)}, bf16[2,192,192]{2,1,0:T(8,128)(2,1)}, u32[]{:S(2)}) copy-start(bf16[2,192,192]{2,1,0:T(8,128)(2,1)} %constant.10.clone.refs_11_) | copy-start | bytes 442372
  39.6 13.6 %collective-permute-start.12 = (s16[208,512]{1,0:T(8,128)(2,1)S(1)}, s16[208,512]{1,0:T(8,128)(2,1)S(1)}, u32[]{:S(2)}, u32[]{:S(2)}) collective-permute-start(s16[208,512]{1,0:T(8,128)(2,1)S(1)} %get-tuple-element.59), channel_id=1, source_target_pairs={{0,6},{1,31},{2,4},{3,29},{4,10},{5,3},{6,8},{7,1},{8,14},{9,7},{1... | collective-permute-start | bytes 638984 | tf_op jit(solution)/shard_map/ppermute | solution.py:320
  42.1 11.1 %collective-permute-start.13 = (s16[208,512]{1,0:T(8,128)(2,1)S(1)}, s16[208,512]{1,0:T(8,128)(2,1)S(1)}, u32[]{:S(2)}, u32[]{:S(2)}) collective-permute-start(s16[208,512]{1,0:T(8,128)(2,1)S(1)} %get-tuple-element.60), channel_id=1, source_target_pairs={{0,7},{1,30},{2,5},{3,28},{4,11},{5,2},{6,9},{7,0},{8,15},{9,6},{1... | collective-permute-start | bytes 638984 | tf_op jit(solution)/shard_map/ppermute | solution.py:320
  45.2 8.0 %collective-permute-start.21 = (s16[208,512]{1,0:T(8,128)(2,1)S(1)}, s16[208,512]{1,0:T(8,128)(2,1)S(1)}, u32[]{:S(2)}, u32[]{:S(2)}) collective-permute-start(s16[208,512]{1,0:T(8,128)(2,1)S(1)} %get-tuple-element.69), channel_id=1, source_target_pairs={{0,4},{1,29},{2,6},{3,31},{4,8},{5,1},{6,10},{7,3},{8,12},{9,5},{1... | collective-permute-start | bytes 638984 | tf_op jit(solution)/shard_map/ppermute | solution.py:320
  45.5 10.9 %collective-permute-start.22 = (s16[208,512]{1,0:T(8,128)(2,1)S(1)}, s16[208,512]{1,0:T(8,128)(2,1)S(1)}, u32[]{:S(2)}, u32[]{:S(2)}) collective-permute-start(s16[208,512]{1,0:T(8,128)(2,1)S(1)} %get-tuple-element.70), channel_id=1, source_target_pairs={{0,5},{1,28},{2,7},{3,30},{4,9},{5,0},{6,11},{7,2},{8,13},{9,4},{1... | collective-permute-start | bytes 638984 | tf_op jit(solution)/shard_map/ppermute | solution.py:320

commit v9 on v6

--- a/solution.py
+++ b/solution.py
@@ -354,7 +354,7 @@
     parts = (
         late_b[4], beside, send(mine_a, ASLANT), send(other_a, ASLANT_ACROSS), send(mine_b, ALONG), send(other_b, ACROSS),
     )
-    return keep0_b, parts
+    return keep0_b, parts, mine_b
 
 
 def spread(row, height):
@@ -365,39 +365,45 @@
     return lax.broadcasted_iota(jnp.int32, (height, width), 0).astype(F32).astype(BF)
 
 
+GROUP = 4
+
+
+def hot_kernel(places, _, col_hots, row_hots, mask):
+    tile_cols = mask.shape[1] // CH
+    numbers = row_numbers(GROUP * CH, GROUP * SLOTS)
+    one, none = jnp.ones((), BF), jnp.zeros((), BF)
+    for g in range(col_hots.shape[0]):
+        part = [places[GROUP * g + n:GROUP * g + n + 1, :] for n in range(GROUP)]
+        row_code = (jnp.concatenate(part, axis=1) >> 6).astype(F32)
+        col_code = jnp.concatenate([(p & 63) + CH * n for n, p in enumerate(part)], axis=1).astype(F32)
+        col_hots[g] = jnp.where(numbers == spread(col_code, GROUP * CH), one, none)
+        row_hots[g] = jnp.where(numbers[:CH] == spread(row_code, CH), one, none)
+        i, j = (GROUP * g) // tile_cols, (GROUP * g) % tile_cols
+        mask[i * CH:(i + 1) * CH, j * CH:(j + GROUP) * CH] = dot_nt(row_hots[g], col_hots[g])
+
+
 def pick_kernel(kept, *refs):
-    parts, (momentum, places, rows, rows_t, cols, cols_t, new_moment, payload, coef, sparse) = refs[:6], refs[6:]
+    parts, refs = refs[:6], refs[6:]
+    momentum, places, col_hots, row_hots, mask, rows, rows_t, cols, cols_t, new_moment, payload, coef = refs
     grad = kept[...]
     for part in parts:
         grad = grad + decode(part)
     moment = 0.9 * momentum[...] + grad
     coef[...] = right_product(left_product(rows, moment), cols_t)
-    tile_rows, tile_cols = momentum.shape[0] // CH, momentum.shape[1] // CH
-    group = 4
-    tiles = tile_rows * tile_cols
-    width = group * SLOTS
-    numbers = row_numbers(group * CH, width)
-    one, none = jnp.ones((), BF), jnp.zeros((), BF)
-    for i in range(tile_rows):
-        for h in range(tile_cols // group):
-            first = i * tile_cols + h * group
-            part = [places[first + n:first + n + 1, :] for n in range(group)]
-            row_code = (jnp.concatenate(part, axis=1) >> 6).astype(F32)
-            col_code = jnp.concatenate([(p & 63) + CH * n for n, p in enumerate(part)], axis=1).astype(F32)
-            col_hot = jnp.where(numbers == spread(col_code, group * CH), one, none)
-            row_hot = jnp.where(numbers[:CH] == spread(row_code, CH), one, none)
-            block = coef[i * CH:(i + 1) * CH, h * group * CH:(h + 1) * group * CH]
-            high, low = split(block)
-            chosen = dot(jnp.concatenate([high, low], axis=0), col_hot)
-            chosen = chosen[:CH] + chosen[CH:]
-            value = jnp.sum(chosen * row_hot.astype(F32), axis=0, keepdims=True)
-            for n in range(group):
-                for r in range(payload.shape[0]):
-                    payload[r, first + n:first + n + 1, :] = value[:, n * SLOTS:(n + 1) * SLOTS]
-            sparse[i * CH:(i + 1) * CH, h * group * CH:(h + 1) * group * CH] = block * dot_nt(row_hot, col_hot)
+    tile_cols = momentum.shape[1] // CH
+    for g in range(col_hots.shape[0]):
+        i, j = (GROUP * g) // tile_cols, (GROUP * g) % tile_cols
+        high, low = split(coef[i * CH:(i + 1) * CH, j * CH:(j + GROUP) * CH])
+        chosen = dot(jnp.concatenate([high, low], axis=0), col_hots[g])
+        chosen = chosen[:CH] + chosen[CH:]
+        value = jnp.sum(chosen * row_hots[g].astype(F32), axis=0, keepdims=True)
+        for n in range(GROUP):
+            for r in range(payload.shape[0]):
+                payload[r, GROUP * g + n:GROUP * g + n + 1, :] = value[:, n * SLOTS:(n + 1) * SLOTS]
+    tiles = places.shape[0]
     for r in range(payload.shape[0]):
         payload[r, tiles:, :] = places[...].astype(F32)
-    new_moment[...] = moment - right_product(left_product(rows_t, sparse[...]), cols)
+    new_moment[...] = moment - right_product(left_product(rows_t, coef[...] * mask[...]), cols)
 
 
 def decode_kernel(gathered, rows_t, cols, step_dir, total):
@@ -440,17 +446,21 @@
     tiles = (height // CH) * (breadth // CH)
     live = lax.broadcasted_iota(jnp.int32, indices.shape[1:], 2) < counts[0]
     places = jnp.where(live, indices[0], -1).reshape(tiles, SLOTS)
-    kept, parts = replica_sum(activations[0], out_grads[0])
+    kept, parts, after = replica_sum(activations[0], out_grads[0])
+    groups = tiles // GROUP
+    hots = call_local(hot_kernel, (places, after), (None, ANYWHERE), [
+        ((groups, GROUP * CH, GROUP * SLOTS), BF), ((groups, CH, GROUP * SLOTS), BF), ((height, breadth), F32),
+    ], "hot")
     new_moment, payload = pl.pallas_call(
         pick_kernel,
         out_shape=[
             jax.ShapeDtypeStruct((height, breadth), F32),
             jax.ShapeDtypeStruct((reps, 2 * tiles, SLOTS), F32),
         ],
-        scratch_shapes=[pltpu.VMEM((height, breadth), F32), pltpu.VMEM((height, breadth), F32)],
+        scratch_shapes=[pltpu.VMEM((height, breadth), F32)],
         compiler_params=pltpu.CompilerParams(vmem_limit_bytes=32 << 20),
         name="pick",
-    )(kept, *parts, momentum[0], places, rows, rows_t, cols, cols_t)
+    )(kept, *parts, momentum[0], places, *hots, rows, rows_t, cols, cols_t)
     gathered = lax.all_to_all(payload, "rep", 0, 0)
     step_dir = pl.pallas_call(
         decode_kernel,

time: 75.1 us -> 74.5 us (level)
  the two profiles are of different devices: /device:TPU:1 before, /device:TPU:96 now
where the time goes in v9:
time: 74.5 us; the launch traced here: 74.2 us
  starting transfers between devices  23.7 us (32%)
  Pallas kernels  21.1 us (28%)
  blocking collectives  15.1 us (20%)
  waiting for transfers between devices  11.6 us (16%)
  between operations  1.53 us (2%)
  local copies, waits for them, and re-layouts  1.15 us (2%)
    ppermute x23, starting transfers between devices, send(): return lax.ppermute(array, 'fsdp', pairs)  23.7 us
    all_to_all x1, blocking collectives, body(): gathered = lax.all_to_all(payload, 'rep', 0, 0)  15.1 us
    pallas_call x6, Pallas kernels, partial_sums(): pl.pallas_call(kernel, in_specs=[pl.BlockSpec(memory_space=space) for _,...  12.1 us
    ppermute x23, waiting for transfers between devices, send(): return lax.ppermute(array, 'fsdp', pairs)  11.6 us
    pallas_call x10, Pallas kernels, call_local(): pl.pallas_call(kernel, grid=(1,), in_specs=[spec(arg, cut) for arg, cut i...  3.42 us
    pallas_call x1, Pallas kernels, body(): pl.pallas_call(decode_kernel, out_shape=jax.ShapeDtypeStruct((height, bre...  3.12 us
    pallas_call x1, Pallas kernels, body(): pl.pallas_call(pick_kernel, out_shape=[jax.ShapeDtypeStruct((height, brea...  2.43 us
  transfers between devices with their start and end apart: 23, of which 4 were waited for; matrix products, arithmetic and copies ran while one was open for 0% of the time, Pallas kernels for 18%

profile of v9, /device:TPU:96, one launch (start us, length us, event | category | flops | bytes accessed | tf_op | source)
XLA Modules:
  0.0 74.2 jit_solution(8223614441754726096)
XLA Ops:
  0.6 1.1 %copy-done.2 = bf16[1,768,512]{2,1,0:T(8,128)(2,1)S(1)} copy-done((bf16[1,768,512]{2,1,0:T(8,128)(2,1)S(1)}, bf16[1,768,512]{2,1,0:T(8,128)(2,1)}, u32[]{:S(2)}) %copy-start.2) | copy-done | bytes 786456
  1.8 2.5 %early.2 = (f32[384,256]{1,0:T(8,128)S(1)}, s16[3,208,512]{2,1,0:T(8,128)(2,1)S(1)}, bf16[768,512]{1,0:T(8,128)(2,1)S(1)}, bf16[2,768,384]{2,1,0:T(8,128)(2,1)S(1)}) custom-call(bf16[768,6144]{1,0:T(8,128)(2,1)} %bitcast.10, bf16[768,512]{1,0:T(8,128)(2,1)S(1)} %bitcast.8), custom_call_target="tpu_custom_call" | custom-call | flops 2717908992 | bytes 2949120 | tf_op jit(solution)/shard_map/early/pallas_call | solution.py:196
  4.3 2.2 %early.3 = (f32[384,256]{1,0:T(8,128)S(1)}, s16[3,208,512]{2,1,0:T(8,128)(2,1)S(1)}, bf16[3,768,384]{2,1,0:T(8,128)(2,1)S(1)}) custom-call(bf16[768,6144]{1,0:T(8,128)(2,1)} %bitcast.11, bf16[768,512]{1,0:T(8,128)(2,1)S(1)} %get-tuple-element.39.grads.refs_1_, bf16[2,768,384]{2,1,0:T(8,128)(2,1)S(1)} %get-tuple-element.40.blocks, ...), custom_call_target="tpu_custom_call" | custom-call | flops 1811939328 | bytes 1966080 | tf_op jit(solution)/shard_map/early/pallas_call | solution.py:196
  6.6 0.6 collective-permute-start.2
  7.3 3.2 %collective-permute-start.1 = (s16[400,256]{1,0:T(8,128)(2,1)S(1)}, s16[400,256]{1,0:T(8,128)(2,1)S(1)}, u32[]{:S(2)}, u32[]{:S(2)}) collective-permute-start(s16[400,256]{1,0:T(8,128)(2,1)S(1)} %hop1.2.refs_3_), channel_id=1, source_target_pairs={{0,4},{1,29},{2,6},{3,31},{4,8},{5,1},{6,10},{7,3},{8,12},{9,5},{1... | collective-permute-start | bytes 614408 | tf_op jit(solution)/shard_map/ppermute | solution.py:315
  10.6 1.6 %collective-permute-start.3 = (s16[400,256]{1,0:T(8,128)(2,1)S(1)}, s16[400,256]{1,0:T(8,128)(2,1)S(1)}, u32[]{:S(2)}, u32[]{:S(2)}) collective-permute-start(s16[400,256]{1,0:T(8,128)(2,1)S(1)} %hop1.3), channel_id=1, source_target_pairs={{0,4},{1,29},{2,6},{3,31},{4,8},{5,1},{6,10},{7,3},{8,12},{9,5},{1... | collective-permute-start | bytes 614408 | tf_op jit(solution)/shard_map/ppermute | solution.py:315
  12.2 1.7 %kept.2 = (f32[384,512]{1,0:T(8,128)S(1)}, f32[384,512]{1,0:T(8,128)S(1)}, f32[384,512]{1,0:T(8,128)S(1)}, bf16[3,768,384]{2,1,0:T(8,128)(2,1)S(1)}) custom-call(bf16[768,6144]{1,0:T(8,128)(2,1)} %bitcast.12, bf16[768,512]{1,0:T(8,128)(2,1)S(1)} %get-tuple-element.39.grads.refs_1_, bf16[3,768,384]{2,1,0:T(8,128)(2,1)S(1)} %get-tuple-element.42.refs_2_, ...), custom_call_target="tpu_custom_call" | custom-call | flops 2717908992 | bytes 2949120 | tf_op jit(solution)/shard_map/kept/pallas_call | solution.py:196
  13.9 1.7 %kept.3 = (f32[384,512]{1,0:T(8,128)S(1)}, f32[384,512]{1,0:T(8,128)S(1)}, f32[384,512]{1,0:T(8,128)S(1)}, bf16[3,768,384]{2,1,0:T(8,128)(2,1)S(1)}) custom-call(bf16[768,6144]{1,0:T(8,128)(2,1)} %bitcast.13, bf16[768,512]{1,0:T(8,128)(2,1)S(1)} %get-tuple-element.39.grads.refs_1_, bf16[3,768,384]{2,1,0:T(8,128)(2,1)S(1)} %get-tuple-element.44.refs_2_, ...), custom_call_target="tpu_custom_call" | custom-call | flops 2717908992 | bytes 2949120 | tf_op jit(solution)/shard_map/kept/pallas_call | solution.py:196
  15.7 0.5 hop2.2.refs_3_
  16.1 1.9 %collective-permute-start.11 = (s16[400,512]{1,0:T(8,128)(2,1)S(1)}, s16[400,512]{1,0:T(8,128)(2,1)S(1)}, u32[]{:S(2)}, u32[]{:S(2)}) collective-permute-start(s16[400,512]{1,0:T(8,128)(2,1)S(1)} %hop2.2.refs_3_), channel_id=1, source_target_pairs={{0,4},{1,29},{2,6},{3,31},{4,8},{5,1},{6,10},{7,3},{8,12},{9,5},{1... | collective-permute-start | bytes 1228808 | tf_op jit(solution)/shard_map/ppermute | solution.py:315
  18.0 0.5 hop2.3.refs_3_
  18.5 1.7 %collective-permute-start.19 = (s16[400,512]{1,0:T(8,128)(2,1)S(1)}, s16[400,512]{1,0:T(8,128)(2,1)S(1)}, u32[]{:S(2)}, u32[]{:S(2)}) collective-permute-start(s16[400,512]{1,0:T(8,128)(2,1)S(1)} %hop2.3.refs_3_), channel_id=1, source_target_pairs={{0,4},{1,29},{2,6},{3,31},{4,8},{5,1},{6,10},{7,3},{8,12},{9,5},{1... | collective-permute-start | bytes 1228808 | tf_op jit(solution)/shard_map/ppermute | solution.py:315
  20.2 2.7 %late.2 = (f32[192,512]{1,0:T(8,128)S(1)}, s16[208,512]{1,0:T(8,128)(2,1)S(1)}, s16[208,512]{1,0:T(8,128)(2,1)S(1)}, s16[208,512]{1,0:T(8,128)(2,1)S(1)}, s16[20...) custom-call(bf16[768,6144]{1,0:T(8,128)(2,1)} %bitcast.14, ...), custom_call_target="tpu_custom_call" | custom-call | flops 2717908992 | bytes 2949120 | tf_op jit(solution)/shard_map/late/pallas_call | solution.py:196
  23.0 0.5 collective-permute-start.9
  23.6 1.3 %late.3 = (f32[192,512]{1,0:T(8,128)S(1)}, s16[208,512]{1,0:T(8,128)(2,1)S(1)}, s16[208,512]{1,0:T(8,128)(2,1)S(1)}, s16[208,512]{1,0:T(8,128)(2,1)S(1)}, s16[20...) custom-call(bf16[768,6144]{1,0:T(8,128)(2,1)} %bitcast.15, bf16[768,512]{1,0:T(8,128)(2,1)S(1)} %get-tuple-element.39.grads.refs_1_, ...), custom_call_target="tpu_custom_call" | custom-call | flops 2717908992 | bytes 2949120 | tf_op jit(solution)/shard_map/late/pallas_call | solution.py:196
  24.9 0.5 collective-permute-start.17
  26.5 1.2 %collective-permute-start.12 = (s16[400,512]{1,0:T(8,128)(2,1)S(1)}, s16[400,512]{1,0:T(8,128)(2,1)S(1)}, u32[]{:S(2)}, u32[]{:S(2)}) collective-permute-start(s16[400,512]{1,0:T(8,128)(2,1)S(1)} %hop3.2), channel_id=1, source_target_pairs={{0,4},{1,29},{2,6},{3,31},{4,8},{5,1},{6,10},{7,3},{8,12},{9,5},{1... | collective-permute-start | bytes 1228808 | tf_op jit(solution)/shard_map/ppermute | solution.py:315
  27.7 0.8 %collective-permute-done.19.arrived = s16[400,512]{1,0:T(8,128)(2,1)S(1)} collective-permute-done((s16[400,512]{1,0:T(8,128)(2,1)S(1)}, s16[400,512]{1,0:T(8,128)(2,1)S(1)}, u32[]{:S(2)}, u32[]{:S(2)}) %collective-permute-start.19) | collective-permute-done | bytes 409632 | tf_op jit(solution)/shard_map/ppermute | solution.py:315
  28.9 3.1 %collective-permute-start.20 = (s16[400,512]{1,0:T(8,128)(2,1)S(1)}, s16[400,512]{1,0:T(8,128)(2,1)S(1)}, u32[]{:S(2)}, u32[]{:S(2)}) collective-permute-start(s16[400,512]{1,0:T(8,128)(2,1)S(1)} %hop3.3), channel_id=1, source_target_pairs={{0,4},{1,29},{2,6},{3,31},{4,8},{5,1},{6,10},{7,3},{8,12},{9,5},{1... | collective-permute-start | bytes 1228808 | tf_op jit(solution)/shard_map/ppermute | solution.py:315
  32.0 0.5 collective-permute-start.16
  33.2 1.3 %collective-permute-done.12.arrived = s16[400,512]{1,0:T(8,128)(2,1)S(1)} collective-permute-done((s16[400,512]{1,0:T(8,128)(2,1)S(1)}, s16[400,512]{1,0:T(8,128)(2,1)S(1)}, u32[]{:S(2)}, u32[]{:S(2)}) %collective-permute-start.12) | collective-permute-done | bytes 409632 | tf_op jit(solution)/shard_map/ppermute | solution.py:315
  34.5 1.6 %collective-permute-start.6 = (s16[208,512]{1,0:T(8,128)(2,1)S(1)}, s16[208,512]{1,0:T(8,128)(2,1)S(1)}, u32[]{:S(2)}, u32[]{:S(2)}) collective-permute-start(s16[208,512]{1,0:T(8,128)(2,1)S(1)} %own.1.rest_0_._), channel_id=1, source_target_pairs={{0,2},{1,3},{2,0},{3,1},{4,6},{5,7},{6,4},{7,5},{8,10},{9,11},{10,... | collective-permute-start | bytes 638984 | tf_op jit(solution)/shard_map/ppermute | solution.py:315
  36.2 0.4 hop4.2
  36.6 2.3 %collective-permute-start.13 = (s16[208,512]{1,0:T(8,128)(2,1)S(1)}, s16[208,512]{1,0:T(8,128)(2,1)S(1)}, u32[]{:S(2)}, u32[]{:S(2)}) collective-permute-start(s16[208,512]{1,0:T(8,128)(2,1)S(1)} %get-tuple-element.61), channel_id=1, source_target_pairs={{0,6},{1,31},{2,4},{3,29},{4,10},{5,3},{6,8},{7,1},{8,14},{9,7},{1... | collective-permute-start | bytes 638984 | tf_op jit(solution)/shard_map/ppermute | solution.py:315
  38.9 1.5 %collective-permute-start.14 = (s16[208,512]{1,0:T(8,128)(2,1)S(1)}, s16[208,512]{1,0:T(8,128)(2,1)S(1)}, u32[]{:S(2)}, u32[]{:S(2)}) collective-permute-start(s16[208,512]{1,0:T(8,128)(2,1)S(1)} %get-tuple-element.62), channel_id=1, source_target_pairs={{0,7},{1,30},{2,5},{3,28},{4,11},{5,2},{6,9},{7,0},{8,15},{9,6},{1... | collective-permute-start | bytes 638984 | tf_op jit(solution)/shard_map/ppermute | solution.py:315
  40.8 2.6 %collective-permute-start.22 = (s16[208,512]{1,0:T(8,128)(2,1)S(1)}, s16[208,512]{1,0:T(8,128)(2,1)S(1)}, u32[]{:S(2)}, u32[]{:S(2)}) collective-permute-start(s16[208,512]{1,0:T(8,128)(2,1)S(1)} %get-tuple-element.70), channel_id=1, source_target_pairs={{0,5},{1,28},{2,7},{3,30},{4,9},{5,0},{6,11},{7,2},{8,13},{9,4},{1... | collective-permute-start | bytes 638984 | tf_op jit(solution)/shard_map/ppermute | solution.py:315
  43.5 0.6 hot.1
  44.1 7.2 %collective-permute-done.6.refs_1_ = s16[208,512]{1,0:T(8,128)(2,1)S(1)} collective-permute-done((s16[208,512]{1,0:T(8,128)(2,1)S(1)}, s16[208,512]{1,0:T(8,128)(2,1)S(1)}, u32[]{:S(2)}, u32[]{:S(2)}) %collective-permute-start.6) | collective-permute-done | bytes 213024 | tf_op jit(solution)/shard_map/ppermute | solution.py:315
  51.3 2.2 %collective-permute-done.21.refs_4_ = s16[208,512]{1,0:T(8,128)(2,1)S(1)} collective-permute-done((s16[208,512]{1,0:T(8,128)(2,1)S(1)}, s16[208,512]{1,0:T(8,128)(2,1)S(1)}, u32[]{:S(2)}, u32[]{:S(2)}) %collective-permute-start.21) | collective-permute-done | bytes 213024 | tf_op jit(solution)/shard_map/ppermute | solution.py:315
  53.6 2.4 %pick.1 = (f32[192,512]{1,0:T(8,128)}, f32[8,48,128]{2,1,0:T(8,128)S(1)}) custom-call(f32[192,512]{1,0:T(8,128)S(1)} %get-tuple-element.51.kept, s16[208,512]{1,0:T(8,128)(2,1)S(1)} %collective-permute-done.4.refs_0_, s16[208,512]{1,0:T(8,128)(2,1)S(1)} %collective-permute-done.6.refs_1_, s16[208,512]{1,0:T(8,128)(2,1)S(1)} %collective-permute-done.13.refs_2_, ...), custom_call_target="tpu_custom_call" | custom-call | tf_op jit(solution)/shard_map/pick/pallas_call | solution.py:454
  56.0 15.1 %all_to_all.5.gathered = f32[8,48,128]{2,1,0:T(8,128)S(1)} all-to-all(f32[8,48,128]{2,1,0:T(8,128)S(1)} %get-tuple-element.75), channel_id=1, replica_groups=mesh['rep'=8,'fsdp'=32] {'rep'}, dimensions={0} | all-to-all | bytes 393216 | tf_op jit(solution)/shard_map/all_to_all | solution.py:464
  71.1 3.1 %decode.1 = f32[192,512]{1,0:T(8,128)} custom-call(f32[8,48,128]{2,1,0:T(8,128)S(1)} %all_to_all.5.gathered, bf16[2,192,192]{2,1,0:T(8,128)(2,1)S(1)} %copy-done.1, bf16[2,256,256]{2,1,0:T(8,128)(2,1)S(1)} %copy-done), custom_call_target="tpu_custom_call" | custom-call | tf_op jit(solution)/shard_map/decode/pallas_call | solution.py:465
  (49 shorter events, 2.6 us)
Async XLA Ops:
  0.6 1.1 %copy-start.2 = (bf16[1,768,512]{2,1,0:T(8,128)(2,1)S(1)}, bf16[1,768,512]{2,1,0:T(8,128)(2,1)}, u32[]{:S(2)}) copy-start(bf16[1,768,512]{2,1,0:T(8,128)(2,1)} %param.10) | copy-start | bytes 2359300
  4.2 2.9 %collective-permute-start = (s16[3,208,512]{2,1,0:T(8,128)(2,1)S(1)}, s16[3,208,512]{2,1,0:T(8,128)(2,1)S(1)}, u32[]{:S(2)}, u32[]{:S(2)}) collective-permute-start(s16[3,208,512]{2,1,0:T(8,128)(2,1)S(1)} %get-tuple-element.41._), channel_id=1, source_target_pairs={{0,1},{1,0},{2,3},{3,2},{4,5},{5,4},{6,7},{7,6},{8,9},{9,8},{10,11... | collective-permute-start | bytes 1916936 | tf_op jit(solution)/shard_map/ppermute | solution.py:315
  6.6 3.9 %collective-permute-start.2 = (s16[3,208,512]{2,1,0:T(8,128)(2,1)S(1)}, s16[3,208,512]{2,1,0:T(8,128)(2,1)S(1)}, u32[]{:S(2)}, u32[]{:S(2)}) collective-permute-start(s16[3,208,512]{2,1,0:T(8,128)(2,1)S(1)} %get-tuple-element.49), channel_id=1, source_target_pairs={{0,1},{1,0},{2,3},{3,2},{4,5},{5,4},{6,7},{7,6},{8,9},{9,8},{10,11... | collective-permute-start | bytes 1916936 | tf_op jit(solution)/shard_map/ppermute | solution.py:315
  7.3 8.4 %collective-permute-start.1 = (s16[400,256]{1,0:T(8,128)(2,1)S(1)}, s16[400,256]{1,0:T(8,128)(2,1)S(1)}, u32[]{:S(2)}, u32[]{:S(2)}) collective-permute-start(s16[400,256]{1,0:T(8,128)(2,1)S(1)} %hop1.2.refs_3_), channel_id=1, source_target_pairs={{0,4},{1,29},{2,6},{3,31},{4,8},{5,1},{6,10},{7,3},{8,12},{9,5},{1... | collective-permute-start | bytes 614408 | tf_op jit(solution)/shard_map/ppermute | solution.py:315
  10.6 7.4 %collective-permute-start.3 = (s16[400,256]{1,0:T(8,128)(2,1)S(1)}, s16[400,256]{1,0:T(8,128)(2,1)S(1)}, u32[]{:S(2)}, u32[]{:S(2)}) collective-permute-start(s16[400,256]{1,0:T(8,128)(2,1)S(1)} %hop1.3), channel_id=1, source_target_pairs={{0,4},{1,29},{2,6},{3,31},{4,8},{5,1},{6,10},{7,3},{8,12},{9,5},{1... | collective-permute-start | bytes 614408 | tf_op jit(solution)/shard_map/ppermute | solution.py:315
  16.1 9.8 %collective-permute-start.11 = (s16[400,512]{1,0:T(8,128)(2,1)S(1)}, s16[400,512]{1,0:T(8,128)(2,1)S(1)}, u32[]{:S(2)}, u32[]{:S(2)}) collective-permute-start(s16[400,512]{1,0:T(8,128)(2,1)S(1)} %hop2.2.refs_3_), channel_id=1, source_target_pairs={{0,4},{1,29},{2,6},{3,31},{4,8},{5,1},{6,10},{7,3},{8,12},{9,5},{1... | collective-permute-start | bytes 1228808 | tf_op jit(solution)/shard_map/ppermute | solution.py:315
  18.5 10.1 %collective-permute-start.19 = (s16[400,512]{1,0:T(8,128)(2,1)S(1)}, s16[400,512]{1,0:T(8,128)(2,1)S(1)}, u32[]{:S(2)}, u32[]{:S(2)}) collective-permute-start(s16[400,512]{1,0:T(8,128)(2,1)S(1)} %hop2.3.refs_3_), channel_id=1, source_target_pairs={{0,4},{1,29},{2,6},{3,31},{4,8},{5,1},{6,10},{7,3},{8,12},{9,5},{1... | collective-permute-start | bytes 1228808 | tf_op jit(solution)/shard_map/ppermute | solution.py:315
  22.9 2.0 %collective-permute-start.5 = (s16[208,512]{1,0:T(8,128)(2,1)S(1)}, s16[208,512]{1,0:T(8,128)(2,1)S(1)}, u32[]{:S(2)}, u32[]{:S(2)}) collective-permute-start(s16[208,512]{1,0:T(8,128)(2,1)S(1)} %get-tuple-element.54), channel_id=1, source_target_pairs={{0,1},{1,0},{2,3},{3,2},{4,5},{5,4},{6,7},{7,6},{8,9},{9,8},{10,11... | collective-permute-start | bytes 638984 | tf_op jit(solution)/shard_map/ppermute | solution.py:315
  23.0 2.4 %collective-permute-start.9 = (s16[208,512]{1,0:T(8,128)(2,1)S(1)}, s16[208,512]{1,0:T(8,128)(2,1)S(1)}, u32[]{:S(2)}, u32[]{:S(2)}) collective-permute-start(s16[208,512]{1,0:T(8,128)(2,1)S(1)} %get-tuple-element.59), channel_id=1, source_target_pairs={{0,1},{1,0},{2,3},{3,2},{4,5},{5,4},{6,7},{7,6},{8,9},{9,8},{10,11... | collective-permute-start | bytes 638984 | tf_op jit(solution)/shard_map/ppermute | solution.py:315
  23.5 2.0 %collective-permute-start.10 = (s16[208,512]{1,0:T(8,128)(2,1)S(1)}, s16[208,512]{1,0:T(8,128)(2,1)S(1)}, u32[]{:S(2)}, u32[]{:S(2)}) collective-permute-start(s16[208,512]{1,0:T(8,128)(2,1)S(1)} %get-tuple-element.60), channel_id=1, source_target_pairs={{0,1},{1,0},{2,3},{3,2},{4,5},{5,4},{6,7},{7,6},{8,9},{9,8},{10,11... | collective-permute-start | bytes 638984 | tf_op jit(solution)/shard_map/ppermute | solution.py:315
  24.9 1.6 %collective-permute-start.17 = (s16[208,512]{1,0:T(8,128)(2,1)S(1)}, s16[208,512]{1,0:T(8,128)(2,1)S(1)}, u32[]{:S(2)}, u32[]{:S(2)}) collective-permute-start(s16[208,512]{1,0:T(8,128)(2,1)S(1)} %get-tuple-element.67), channel_id=1, source_target_pairs={{0,1},{1,0},{2,3},{3,2},{4,5},{5,4},{6,7},{7,6},{8,9},{9,8},{10,11... | collective-permute-start | bytes 638984 | tf_op jit(solution)/shard_map/ppermute | solution.py:315
  25.4 2.3 %collective-permute-start.18 = (s16[208,512]{1,0:T(8,128)(2,1)S(1)}, s16[208,512]{1,0:T(8,128)(2,1)S(1)}, u32[]{:S(2)}, u32[]{:S(2)}) collective-permute-start(s16[208,512]{1,0:T(8,128)(2,1)S(1)} %get-tuple-element.68), channel_id=1, source_target_pairs={{0,1},{1,0},{2,3},{3,2},{4,5},{5,4},{6,7},{7,6},{8,9},{9,8},{10,11... | collective-permute-start | bytes 638984 | tf_op jit(solution)/shard_map/ppermute | solution.py:315
  25.5 6.4 %collective-permute-start.7 = (s16[208,512]{1,0:T(8,128)(2,1)S(1)}, s16[208,512]{1,0:T(8,128)(2,1)S(1)}, u32[]{:S(2)}, u32[]{:S(2)}) collective-permute-start(s16[208,512]{1,0:T(8,128)(2,1)S(1)} %get-tuple-element.56), channel_id=1, source_target_pairs={{0,1},{1,0},{2,3},{3,2},{4,5},{5,4},{6,7},{7,6},{8,9},{9,8},{10,11... | collective-permute-start | bytes 638984 | tf_op jit(solution)/shard_map/ppermute | solution.py:315
  25.9 6.5 %collective-permute-start.8 = (s16[208,512]{1,0:T(8,128)(2,1)S(1)}, s16[208,512]{1,0:T(8,128)(2,1)S(1)}, u32[]{:S(2)}, u32[]{:S(2)}) collective-permute-start(s16[208,512]{1,0:T(8,128)(2,1)S(1)} %get-tuple-element.57), channel_id=1, source_target_pairs={{0,1},{1,0},{2,3},{3,2},{4,5},{5,4},{6,7},{7,6},{8,9},{9,8},{10,11... | collective-permute-start | bytes 638984 | tf_op jit(solution)/shard_map/ppermute | solution.py:315
  26.5 8.0 %collective-permute-start.12 = (s16[400,512]{1,0:T(8,128)(2,1)S(1)}, s16[400,512]{1,0:T(8,128)(2,1)S(1)}, u32[]{:S(2)}, u32[]{:S(2)}) collective-permute-start(s16[400,512]{1,0:T(8,128)(2,1)S(1)} %hop3.2), channel_id=1, source_target_pairs={{0,4},{1,29},{2,6},{3,31},{4,8},{5,1},{6,10},{7,3},{8,12},{9,5},{1... | collective-permute-start | bytes 1228808 | tf_op jit(solution)/shard_map/ppermute | solution.py:315
  28.9 11.5 %collective-permute-start.20 = (s16[400,512]{1,0:T(8,128)(2,1)S(1)}, s16[400,512]{1,0:T(8,128)(2,1)S(1)}, u32[]{:S(2)}, u32[]{:S(2)}) collective-permute-start(s16[400,512]{1,0:T(8,128)(2,1)S(1)} %hop3.3), channel_id=1, source_target_pairs={{0,4},{1,29},{2,6},{3,31},{4,8},{5,1},{6,10},{7,3},{8,12},{9,5},{1... | collective-permute-start | bytes 1228808 | tf_op jit(solution)/shard_map/ppermute | solution.py:315
  32.0 4.7 %collective-permute-start.15 = (s16[208,512]{1,0:T(8,128)(2,1)S(1)}, s16[208,512]{1,0:T(8,128)(2,1)S(1)}, u32[]{:S(2)}, u32[]{:S(2)}) collective-permute-start(s16[208,512]{1,0:T(8,128)(2,1)S(1)} %get-tuple-element.64), channel_id=1, source_target_pairs={{0,1},{1,0},{2,3},{3,2},{4,5},{5,4},{6,7},{7,6},{8,9},{9,8},{10,11... | collective-permute-start | bytes 638984 | tf_op jit(solution)/shard_map/ppermute | solution.py:315
  32.0 6.9 %collective-permute-start.16 = (s16[208,512]{1,0:T(8,128)(2,1)S(1)}, s16[208,512]{1,0:T(8,128)(2,1)S(1)}, u32[]{:S(2)}, u32[]{:S(2)}) collective-permute-start(s16[208,512]{1,0:T(8,128)(2,1)S(1)} %get-tuple-element.65), channel_id=1, source_target_pairs={{0,1},{1,0},{2,3},{3,2},{4,5},{5,4},{6,7},{7,6},{8,9},{9,8},{10,11... | collective-permute-start | bytes 638984 | tf_op jit(solution)/shard_map/ppermute | solution.py:315
  32.5 11.0 %collective-permute-start.4 = (s16[208,512]{1,0:T(8,128)(2,1)S(1)}, s16[208,512]{1,0:T(8,128)(2,1)S(1)}, u32[]{:S(2)}, u32[]{:S(2)}) collective-permute-start(s16[208,512]{1,0:T(8,128)(2,1)S(1)} %get-tuple-element.52), channel_id=1, source_target_pairs={{0,1},{1,0},{2,3},{3,2},{4,5},{5,4},{6,7},{7,6},{8,9},{9,8},{10,11... | collective-permute-start | bytes 638984 | tf_op jit(solution)/shard_map/ppermute | solution.py:315
  34.5 16.8 %collective-permute-start.6 = (s16[208,512]{1,0:T(8,128)(2,1)S(1)}, s16[208,512]{1,0:T(8,128)(2,1)S(1)}, u32[]{:S(2)}, u32[]{:S(2)}) collective-permute-start(s16[208,512]{1,0:T(8,128)(2,1)S(1)} %own.1.rest_0_._), channel_id=1, source_target_pairs={{0,2},{1,3},{2,0},{3,1},{4,6},{5,7},{6,4},{7,5},{8,10},{9,11},{10,... | collective-permute-start | bytes 638984 | tf_op jit(solution)/shard_map/ppermute | solution.py:315
  36.1 7.4 %copy-start.6 = (s32[1,3,8,128]{3,2,1,0:T(8,128)S(1)}, s32[1,3,8,128]{3,2,1,0:T(8,128)}, u32[]{:S(2)}) copy-start(s32[1,3,8,128]{3,2,1,0:T(8,128)} %param.12) | copy-start | bytes 36868
  36.1 17.4 %copy-start = (bf16[2,256,256]{2,1,0:T(8,128)(2,1)S(1)}, bf16[2,256,256]{2,1,0:T(8,128)(2,1)}, u32[]{:S(2)}) copy-start(bf16[2,256,256]{2,1,0:T(8,128)(2,1)} %constant.12.clone.refs_13_.cols) | copy-start | bytes 786436
  36.1 17.4 %copy-start.1 = (bf16[2,192,192]{2,1,0:T(8,128)(2,1)S(1)}, bf16[2,192,192]{2,1,0:T(8,128)(2,1)}, u32[]{:S(2)}) copy-start(bf16[2,192,192]{2,1,0:T(8,128)(2,1)} %constant.11.clone.refs_12_.rows_t) | copy-start | bytes 442372
  36.1 17.4 %copy-start.3 = (f32[1,192,512]{2,1,0:T(8,128)S(1)}, f32[1,192,512]{2,1,0:T(8,128)}, u32[]{:S(2)}) copy-start(f32[1,192,512]{2,1,0:T(8,128)} %param.11) | copy-start | bytes 1179652
  36.1 17.4 %copy-start.4 = (bf16[2,256,256]{2,1,0:T(8,128)(2,1)S(1)}, bf16[2,256,256]{2,1,0:T(8,128)(2,1)}, u32[]{:S(2)}) copy-start(bf16[2,256,256]{2,1,0:T(8,128)(2,1)} %constant.13.clone.refs_14_) | copy-start | bytes 786436
  36.2 17.4 %copy-start.5 = (bf16[2,192,192]{2,1,0:T(8,128)(2,1)S(1)}, bf16[2,192,192]{2,1,0:T(8,128)(2,1)}, u32[]{:S(2)}) copy-start(bf16[2,192,192]{2,1,0:T(8,128)(2,1)} %constant.10.clone.refs_11_) | copy-start | bytes 442372
  36.6 14.7 %collective-permute-start.13 = (s16[208,512]{1,0:T(8,128)(2,1)S(1)}, s16[208,512]{1,0:T(8,128)(2,1)S(1)}, u32[]{:S(2)}, u32[]{:S(2)}) collective-permute-start(s16[208,512]{1,0:T(8,128)(2,1)S(1)} %get-tuple-element.61), channel_id=1, source_target_pairs={{0,6},{1,31},{2,4},{3,29},{4,10},{5,3},{6,8},{7,1},{8,14},{9,7},{1... | collective-permute-start | bytes 638984 | tf_op jit(solution)/shard_map/ppermute | solution.py:315
  38.9 12.4 %collective-permute-start.14 = (s16[208,512]{1,0:T(8,128)(2,1)S(1)}, s16[208,512]{1,0:T(8,128)(2,1)S(1)}, u32[]{:S(2)}, u32[]{:S(2)}) collective-permute-start(s16[208,512]{1,0:T(8,128)(2,1)S(1)} %get-tuple-element.62), channel_id=1, source_target_pairs={{0,7},{1,30},{2,5},{3,28},{4,11},{5,2},{6,9},{7,0},{8,15},{9,6},{1... | collective-permute-start | bytes 638984 | tf_op jit(solution)/shard_map/ppermute | solution.py:315
  40.8 10.5 %collective-permute-start.22 = (s16[208,512]{1,0:T(8,128)(2,1)S(1)}, s16[208,512]{1,0:T(8,128)(2,1)S(1)}, u32[]{:S(2)}, u32[]{:S(2)}) collective-permute-start(s16[208,512]{1,0:T(8,128)(2,1)S(1)} %get-tuple-element.70), channel_id=1, source_target_pairs={{0,5},{1,28},{2,7},{3,30},{4,9},{5,0},{6,11},{7,2},{8,13},{9,4},{1... | collective-permute-start | bytes 638984 | tf_op jit(solution)/shard_map/ppermute | solution.py:315
  43.5 10.1 %collective-permute-start.21 = (s16[208,512]{1,0:T(8,128)(2,1)S(1)}, s16[208,512]{1,0:T(8,128)(2,1)S(1)}, u32[]{:S(2)}, u32[]{:S(2)}) collective-permute-start(s16[208,512]{1,0:T(8,128)(2,1)S(1)} %get-tuple-element.69._), channel_id=1, source_target_pairs={{0,4},{1,29},{2,6},{3,31},{4,8},{5,1},{6,10},{7,3},{8,12},{9,5},{1... | collective-permute-start | bytes 638984 | tf_op jit(solution)/shard_map/ppermute | solution.py:315
